TPU v7x, 32 devices: a whole 2x2x4 slice. The times are simulated.
32 devices in a mesh: groups: 2 (over x), blk: 16 (over z, y, core).
Axes of the slice: x: 2, y: 2, z: 4, core: 2. Of those that a mesh axis runs over, the one named last changes fastest.
Arguments:
- points_in: bfloat16 [16384, 768], P(('groups', 'blk')), parts along dimension 0, may hold values from -6 to 6
- hidden_weight: bfloat16 [768, 2560], replicated, may hold values from -0.21875 to 0.21875
- output_weight: bfloat16 [2560, 768], replicated, may hold values from -0.125 to 0.125
- point_owner: int32 [16384, 1], P(('groups', 'blk')), parts along dimension 0, may hold values from 0 to 15; in each aligned block of 512 rows (0 to 511, 512 to 1023, ...) at most 64 rows name the same one
- point_node: int32 [16384], P(('groups', 'blk')), parts along dimension 0, may hold values from 0 to 31
- point_weight: int32 [16384], P(('groups', 'blk')), parts along dimension 0, may hold values from 1 to 4
- proj_weight: bfloat16 [768, 2304], replicated, may hold values from -8 to 8
- final_gain: bfloat16 [768], replicated, may hold values from 0.5 to 1.5
Outputs:
- supernodes: bfloat16 [1024, 768], P(('groups', 'blk')), parts along dimension 0
There are 2 independent parts, one for each index of `groups`. A program takes and returns all parts, laid end to end along the dimension named above; an argument that names none is the same for every part. Nothing has to cross between parts.
Inputs may be any that keep to these rules, and one draw needn't show every extreme that they name: `point_owner`: among the 512 points of one blk index, at most 64 name the same owner, a bound that some block reaches of them.
All inputs are finite; a program needn't handle non-finite values.
Results may differ from a plain program's by a relative error of at most 0.0067.
Values may be sent and summed in bfloat16 or wider, within the bound.
No kernel may reach another device: no remote copies, remote signals or barrier semaphores. Data moves between devices by JAX's collectives and lax.ppermute only.
A program may use at most 128 MiB of HBM per device.

v0:
```python
import jax
import jax.numpy as jnp
from jax import lax
from jax.sharding import PartitionSpec as P

D = 768
HEADS = 12
S_DEV = 32
DH = 64


def rms_rows(values):
    return values * lax.rsqrt(jnp.mean(values * values, axis=-1, keepdims=True) + 1e-06)


def body(
    points_in,
    hidden_weight,
    output_weight,
    point_owner,
    point_node,
    point_weight,
    proj_weight,
    final_gain,
):
    point_rows = points_in.shape[0]
    devices = lax.axis_size("blk")
    normed = rms_rows(points_in.astype(jnp.float32)).astype(jnp.bfloat16)
    hidden = jax.nn.gelu(
        jnp.dot(normed, hidden_weight, preferred_element_type=jnp.float32), approximate=False
    ).astype(jnp.bfloat16)
    features = (
        points_in.astype(jnp.float32)
        + jnp.dot(hidden, output_weight, preferred_element_type=jnp.float32)
    ).astype(jnp.bfloat16)
    target_owner = point_owner[:, 0]
    slots = 2 * point_rows // devices
    matches = (target_owner[:, None] == jnp.arange(devices, dtype=jnp.int32)[None, :]).astype(
        jnp.int32
    )
    places = jnp.sum(jnp.cumsum(matches, axis=0) * matches, axis=1) - 1
    target = target_owner * slots + places
    send_rows = (
        jnp.zeros((devices * slots, D), jnp.bfloat16)
        .at[target]
        .set(features)
        .reshape(devices, slots, D)
    )
    send_nodes = (
        jnp.zeros((devices * slots,), jnp.int32).at[target].set(point_node).reshape(devices, slots)
    )
    send_weights = (
        jnp.zeros((devices * slots,), jnp.int32)
        .at[target]
        .set(point_weight)
        .reshape(devices, slots)
    )
    got_rows, got_nodes, got_weights = (
        lax.all_to_all(send_rows, "blk", split_axis=0, concat_axis=0, tiled=True),
        lax.all_to_all(send_nodes, "blk", split_axis=0, concat_axis=0, tiled=True),
        lax.all_to_all(send_weights, "blk", split_axis=0, concat_axis=0, tiled=True),
    )
    node_flat = got_nodes.reshape(-1)
    weight_flat = got_weights.reshape(-1)
    selected = node_flat[None, :] == jnp.arange(S_DEV, dtype=jnp.int32)[:, None]
    coeffs = jnp.where(selected, weight_flat[None, :], 0)
    pooled_sums = jnp.dot(
        coeffs.astype(jnp.bfloat16), got_rows.reshape(-1, D), preferred_element_type=jnp.float32
    )
    totals = jnp.sum(coeffs, axis=1).astype(jnp.float32)
    pooled = pooled_sums / (1.0 + totals[:, None])
    normed_nodes = rms_rows(pooled).astype(jnp.bfloat16)
    projected = jnp.dot(normed_nodes, proj_weight, preferred_element_type=jnp.float32).astype(
        jnp.bfloat16
    )
    queries = projected[:, :D].reshape(S_DEV, HEADS, DH)
    score_scale = DH ** (-0.5)
    key_value = jnp.dot(
        lax.all_gather(normed_nodes, "blk", axis=0, tiled=True),
        proj_weight[:, D:],
        preferred_element_type=jnp.float32,
    ).astype(jnp.bfloat16)
    key_piece = key_value[:, :D]
    running_max = jnp.full((HEADS, S_DEV), -1e30, jnp.float32)
    piece_rows = key_piece.shape[0]
    key_heads = key_piece.reshape(piece_rows, HEADS, DH)
    value_heads = key_value[:, D:].reshape(piece_rows, HEADS, DH)
    scores = (
        jnp.einsum("qhd,khd->hqk", queries, key_heads, preferred_element_type=jnp.float32)
        * score_scale
    )
    newest = jnp.maximum(running_max, jnp.max(scores, axis=-1))
    exps = jnp.exp(scores - newest[:, :, None])
    running_sum = jnp.sum(exps, axis=-1)
    update = jnp.einsum(
        "hqk,khd->qhd", exps.astype(jnp.bfloat16), value_heads, preferred_element_type=jnp.float32
    )
    attended = (update / jnp.transpose(running_sum)[:, :, None]).reshape(S_DEV, D)
    return (rms_rows(attended) * final_gain.astype(jnp.float32)).astype(jnp.bfloat16)


def solution(mesh):
    placed = (
        P(("groups", "blk"), None),
        P(),
        P(),
        P(("groups", "blk"), None),
        P(("groups", "blk")),
        P(("groups", "blk")),
        P(),
        P(),
    )
    return jax.shard_map(
        body, mesh=mesh, in_specs=placed, out_specs=P(("groups", "blk"), None), check_vma=False
    )
```

profile of v0, /device:TPU:0, one launch (start us, length us, event | category | flops | bytes accessed | tf_op | source)
XLA Modules:
  0.0 119.5 jit_solution(7085627692140071162)
XLA Ops:
  0.0 0.7 fusion.39
  0.7 1.1 reduce-window.6
  1.8 0.2 slice_reduce_fusion
  2.1 0.8 fusion.38
  2.9 0.7 compare_select_fusion
  3.6 2.6 %scatter_custom_fusion.1 = s32[1024]{0:T(1024)S(1)} fusion(s32[512]{0:T(512)S(1)} %bitcast.43, s32[512]{0:T(512)} %param.13, s32[]{:T(128)} %constant.40.clone.1), kind=kCustom, calls=%fused_computation.66 | custom fusion | bytes 4608 | tf_op jit(solution)/shard_map/scatter | solution.py:55
  6.2 0.7 all_to_all.17
  6.8 7.4 %all-to-all-start.1 = ((s32[16,1,64]{2,1,0:T(1,128)}), s32[16,1,64]{2,1,0:T(1,128)S(1)}, u32[]{:S(2)}, u32[]{:S(2)}) async-start(s32[16,1,64]{2,1,0:T(1,128)} %all_to_all.17), calls=%async_computation.1 | async-start | bytes 16384 | tf_op jit(solution)/shard_map/all_to_all | solution.py:61
  14.2 1.4 %fusion.13 = f32[512]{0:T(512)S(1)} fusion(bf16[512,768]{1,0:T(8,128)(2,1)} %param.8), kind=kLoop, calls=%fused_computation.28 | loop fusion | flops 1179136 | bytes 788480 | tf_op jit(solution)/shard_map/reduce_sum | solution.py:13
  15.6 2.6 %scatter_custom_fusion = s32[1024]{0:T(1024)S(1)} fusion(s32[512]{0:T(512)S(1)} %bitcast.44, s32[512]{0:T(512)} %param.12, s32[]{:T(128)} %constant.40.clone.1), kind=kCustom, calls=%fused_computation.68 | custom fusion | bytes 4608 | tf_op jit(solution)/shard_map/scatter | solution.py:50
  18.2 0.7 all_to_all.15
  18.9 1.7 %all-to-all-done.1 = s32[16,1,64]{2,1,0:T(1,128)S(1)} async-done(((s32[16,1,64]{2,1,0:T(1,128)}), s32[16,1,64]{2,1,0:T(1,128)S(1)}, u32[]{:S(2)}, u32[]{:S(2)}) %all-to-all-start.1) | async-done | bytes 4128 | tf_op jit(solution)/shard_map/all_to_all | solution.py:61
  20.6 4.5 %all-to-all-start = ((s32[16,1,64]{2,1,0:T(1,128)}), s32[16,1,64]{2,1,0:T(1,128)S(1)}, u32[]{:S(2)}, u32[]{:S(2)}) async-start(s32[16,1,64]{2,1,0:T(1,128)} %all_to_all.15), calls=%async_computation | async-start | bytes 16384 | tf_op jit(solution)/shard_map/all_to_all | solution.py:60
  25.1 17.9 %fusion.15 = bf16[512,768]{1,0:T(8,128)(2,1)S(1)} fusion(bf16[512,768]{1,0:T(8,128)(2,1)} %param.8, bf16[2560,768]{1,0:T(8,128)(2,1)} %param.10, bf16[768,2560]{1,0:T(8,128)(2,1)} %param.9, f32[512]{0:T(512)S(1)} %add_rsqrt_fusion), kind=kOutput, calls=%fused_computation.30 | convolution fusion | flops 4114087936 | bytes 9439232 | tf_op jit(solution)/shard_map/dot_general | solution.py:34
  43.0 0.0 copy-start.1
  43.0 3.8 %scatter_custom_fusion.2 = bf16[1024,768]{1,0:T(8,128)(2,1)} fusion(s32[512]{0:T(512)S(1)} %bitcast.45, bf16[512,768]{1,0:T(8,128)(2,1)S(1)} %fusion.15, bf16[]{:T(256)} %constant.44.clone.1), kind=kCustom, calls=%fused_computation.38 | custom fusion | bytes 1572866 | tf_op jit(solution)/shard_map/scatter | solution.py:46
  46.8 0.0 all-to-all-done
  46.8 5.8 %all-to-all-start.2 = ((bf16[16,64,768]{2,1,0:T(8,128)(2,1)}), bf16[16,64,768]{2,1,0:T(8,128)(2,1)S(1)}, u32[]{:S(2)}, u32[]{:S(2)}) async-start(bf16[16,64,768]{2,1,0:T(8,128)(2,1)} %bitcast.5), calls=%async_computation.2 | async-start | bytes 3145728 | tf_op jit(solution)/shard_map/all_to_all | solution.py:59
  52.7 0.0 copy-done.1
  52.7 0.5 broadcast.124
  53.2 0.7 reduce.9
  53.9 0.1 broadcast_in_dim.18
  54.0 0.7 reduce.10
  54.6 0.1 eq.48
  54.7 0.1 select_reduce_fusion
  54.8 29.8 %all-to-all-done.2 = bf16[16,64,768]{2,1,0:T(8,128)(2,1)S(1)} async-done(((bf16[16,64,768]{2,1,0:T(8,128)(2,1)}), bf16[16,64,768]{2,1,0:T(8,128)(2,1)S(1)}, u32[]{:S(2)}, u32[]{:S(2)}) %all-to-all-start.2) | async-done | bytes 1572896 | tf_op jit(solution)/shard_map/all_to_all | solution.py:59
  84.7 0.0 copy-start
  84.7 0.5 multiply_reduce_fusion.1
  85.2 0.1 multiply_convert_fusion.1
  85.2 27.2 %all_gather.3 = bf16[512,768]{1,0:T(8,128)(2,1)S(1)} all-gather(bf16[32,768]{1,0:T(8,128)(2,1)S(1)} %multiply_convert_fusion.1), channel_id=1, replica_groups=mesh['groups'=2,'blk'=16] {'blk'}, dimensions={0}, use_global_device_ids=true | all-gather | bytes 835584 | tf_op jit(solution)/shard_map/all_gather | solution.py:79
  112.5 2.7 %fusion.77 = bf16[32,2304]{1,0:T(8,128)(2,1)S(1)} fusion(bf16[32,768]{1,0:T(8,128)(2,1)S(1)} %multiply_convert_fusion.1, bf16[768,2304]{1,0:T(8,128)(2,1)} %param.14), kind=kOutput, calls=%fused_computation.107 | convolution fusion | flops 113246208 | bytes 3735552 | tf_op jit(solution)/shard_map/dot_general | solution.py:73
  115.2 0.0 copy-done
  115.2 1.4 %convolution_convert_fusion = bf16[512,1536]{1,0:T(8,128)(2,1)S(1)} fusion(bf16[512,768]{1,0:T(8,128)(2,1)S(1)} %all_gather.3, bf16[768,2304]{1,0:T(8,128)(2,1)S(1)} %copy-done), kind=kOutput, calls=%fused_computation.22 | convolution fusion | flops 1208745984 | bytes 4718592 | tf_op jit(solution)/shard_map/dot_general | solution.py:78
  116.6 0.1 fusion.75
  116.7 0.3 copy.19
  117.0 0.1 reshape.93
  117.2 0.3 fusion.76
  117.5 0.3 copy.18
  117.8 0.3 fusion.29
  118.1 0.5 multiply_reduce_fusion
  118.6 0.1 copy.21
  118.7 0.1 reshape.95
  118.8 0.7 multiply_convert_fusion
  (10 shorter events, 0.1 us)
Async XLA Ops:
  6.8 13.7 %all-to-all-start.1 = ((s32[16,1,64]{2,1,0:T(1,128)}), s32[16,1,64]{2,1,0:T(1,128)S(1)}, u32[]{:S(2)}, u32[]{:S(2)}) async-start(s32[16,1,64]{2,1,0:T(1,128)} %all_to_all.17), calls=%async_computation.1 | async-start | bytes 16384 | tf_op jit(solution)/shard_map/all_to_all | solution.py:61
  20.6 26.3 %all-to-all-start = ((s32[16,1,64]{2,1,0:T(1,128)}), s32[16,1,64]{2,1,0:T(1,128)S(1)}, u32[]{:S(2)}, u32[]{:S(2)}) async-start(s32[16,1,64]{2,1,0:T(1,128)} %all_to_all.15), calls=%async_computation | async-start | bytes 16384 | tf_op jit(solution)/shard_map/all_to_all | solution.py:60
  43.0 9.7 %copy-start.1 = (bf16[768]{0:T(1024)(128)(2,1)S(1)}, bf16[768]{0:T(1024)(128)(2,1)}, u32[]{:S(2)}) copy-start(bf16[768]{0:T(1024)(128)(2,1)} %param.15) | copy-start | bytes 4612
  46.8 37.8 %all-to-all-start.2 = ((bf16[16,64,768]{2,1,0:T(8,128)(2,1)}), bf16[16,64,768]{2,1,0:T(8,128)(2,1)S(1)}, u32[]{:S(2)}, u32[]{:S(2)}) async-start(bf16[16,64,768]{2,1,0:T(8,128)(2,1)} %bitcast.5), calls=%async_computation.2 | async-start | bytes 3145728 | tf_op jit(solution)/shard_map/all_to_all | solution.py:59
  84.7 30.5 %copy-start = (bf16[768,2304]{1,0:T(8,128)(2,1)S(1)}, bf16[768,2304]{1,0:T(8,128)(2,1)}, u32[]{:S(2)}) copy-start(bf16[768,2304]{1,0:T(8,128)(2,1)} %param.14) | copy-start | bytes 10616836
where the time goes:
time: 120 us
  waiting for transfers between devices  31.5 us (26%)
  blocking collectives  27.2 us (23%)
  matrix products  23.4 us (20%)
  starting transfers between devices  17.7 us (15%)
  local copies, waits for them, and re-layouts  12.3 us (10%)
  other arithmetic  7.26 us (6%)
    all_to_all x1, waiting for transfers between devices, body(): lax.all_to_all(send_rows, 'blk', split_axis=0, concat_axis=0, tiled=True)  29.8 us
    all_gather x1, blocking collectives, body(): lax.all_gather(normed_nodes, 'blk', axis=0, tiled=True)  27.2 us
    dot_general x1, matrix products, body(): jnp.dot(hidden, output_weight, preferred_element_type=jnp.float32)  17.9 us
    all_to_all x1, starting transfers between devices, body(): lax.all_to_all(send_weights, 'blk', split_axis=0, concat_axis=0, tiled=True)  7.39 us
    all_to_all x1, starting transfers between devices, body(): lax.all_to_all(send_rows, 'blk', split_axis=0, concat_axis=0, tiled=True)  5.83 us
    all_to_all x1, starting transfers between devices, body(): lax.all_to_all(send_nodes, 'blk', split_axis=0, concat_axis=0, tiled=True)  4.52 us
    scatter x1, local copies, waits for them, and re-layouts, body(): send_rows = jnp.zeros((devices * slots, D), jnp.bfloat16).at[target].set(...  3.81 us
    dot_general x1, matrix products, body(): jnp.dot(normed_nodes, proj_weight, preferred_element_type=jnp.float32)  2.73 us
  transfers between devices with their start and end apart: 3, of which 2 were waited for; matrix products, arithmetic and copies ran while one was open for 23% of the time, Pallas kernels for 0%

commit v1 on v0

v1 whole, which is shorter than its diff:
```python
import functools

import jax
import jax.numpy as jnp
from jax import lax
from jax.experimental import pallas as pl
from jax.experimental.pallas import tpu as pltpu
from jax.sharding import PartitionSpec as P

D = 768
HEADS = 12
S_DEV = 32
DH = 64
LANES = 128
GROUP_ROWS = 2 * S_DEV
COLS = D // LANES
TOTAL_ROWS = 16
CHUNK = COLS * GROUP_ROWS + TOTAL_ROWS
LANES_PER_GROUP = LANES // (GROUP_ROWS // TOTAL_ROWS)
MAX_TOTAL_BITS = 12
VMEM_LIMIT = 56 * 1024 * 1024


def digit_bits(devices):
    return max(1, (256 // devices).bit_length() - 1)


def gelu(values):
    return 0.5 * values * (1.0 + lax.erf(values * 0.7071067811865476))


def points_kernel(
    devices, steps, me_ref, x_ref, hidden_ref, output_ref, owner_ref, node_ref, weight_ref,
    send_ref, keep_ref, normed_ref, total_ref,
):
    step = pl.program_id(0)
    rows = x_ref.shape[0]
    part = min(rows, 256)

    @pl.when(step == 0)
    def _():
        x = x_ref[...].astype(jnp.float32)
        scale = lax.rsqrt(jnp.mean(x * x, axis=-1, keepdims=True) + 1e-06)
        normed_ref[...] = (x * scale).astype(jnp.bfloat16)
        total_ref[...] = x

    for first in range(0, rows, part):
        at = pl.ds(first, part)
        hidden = gelu(
            jnp.dot(normed_ref[at, :], hidden_ref[...], preferred_element_type=jnp.float32)
        ).astype(jnp.bfloat16)
        total_ref[at, :] += jnp.dot(hidden, output_ref[...], preferred_element_type=jnp.float32)

    @pl.when(step == steps - 1)
    def _():
        features = total_ref[...].astype(jnp.bfloat16)
        me = me_ref[0]
        owner = owner_ref[...]
        near = (owner ^ me) & (devices // 2 - 1)
        chunk_of = near // 2
        row_of = chunk_of * GROUP_ROWS + (owner // (devices // 2)) * S_DEV + node_ref[...]
        chunks = devices // 4
        half = chunks * GROUP_ROWS
        shift = digit_bits(devices)
        digits = -(-MAX_TOTAL_BITS // shift)
        lane = lax.broadcasted_iota(jnp.int32, (TOTAL_ROWS, LANES), 1)
        digit = lane % LANES_PER_GROUP
        held = jnp.where(digit < digits, digit * shift, 31)
        for core, out_ref in ((0, keep_ref), (1, send_ref)):
            place = jnp.where((near & 1) == core, row_of, -1)
            coeffs = jnp.where(
                place == lax.broadcasted_iota(jnp.int32, (half, rows), 0), weight_ref[...], 0
            ).astype(jnp.float32)
            sums = jnp.dot(
                coeffs.astype(jnp.bfloat16), features, preferred_element_type=jnp.float32
            ).astype(jnp.bfloat16)
            totals = jnp.sum(coeffs, axis=1, keepdims=True).astype(jnp.int32)
            for chunk in range(chunks):
                base = chunk * CHUNK
                first = chunk * GROUP_ROWS
                for col in range(COLS):
                    out_ref[base + col * GROUP_ROWS : base + (col + 1) * GROUP_ROWS, :] = sums[
                        first : first + GROUP_ROWS, col * LANES : (col + 1) * LANES
                    ]
                tile = jnp.zeros((TOTAL_ROWS, LANES), jnp.int32)
                for group in range(GROUP_ROWS // TOTAL_ROWS):
                    start = first + group * TOTAL_ROWS
                    value = jnp.broadcast_to(
                        totals[start : start + TOTAL_ROWS], (TOTAL_ROWS, LANES)
                    )
                    tile = jnp.where(lane // LANES_PER_GROUP == group, value, tile)
                tile = (tile >> held) & ((1 << shift) - 1)
                out_ref[base + COLS * GROUP_ROWS : base + CHUNK, :] = tile.astype(
                    jnp.float32
                ).astype(jnp.bfloat16)


def run_points(devices, me, x, hidden_weight, output_weight, owner, node, weight):
    rows, ff = x.shape[0], hidden_weight.shape[1]
    step_cols = 512
    steps = ff // step_cols
    out = jax.ShapeDtypeStruct((devices // 4 * CHUNK, LANES), jnp.bfloat16)
    whole = lambda shape: pl.BlockSpec(shape, lambda s: (0, 0))
    return pl.pallas_call(
        functools.partial(points_kernel, devices, steps),
        grid=(steps,),
        in_specs=[
            pl.BlockSpec(memory_space=pltpu.SMEM),
            whole((rows, D)),
            pl.BlockSpec((D, step_cols), lambda s: (0, s)),
            pl.BlockSpec((step_cols, D), lambda s: (s, 0)),
            whole((1, rows)),
            whole((1, rows)),
            whole((1, rows)),
        ],
        out_specs=[whole(out.shape)] * 2,
        out_shape=[out, out],
        scratch_shapes=[pltpu.VMEM((rows, D), jnp.bfloat16), pltpu.VMEM((rows, D), jnp.float32)],
        compiler_params=pltpu.CompilerParams(vmem_limit_bytes=VMEM_LIMIT),
        name="points",
    )(me, x, hidden_weight, output_weight, owner, node, weight)


def nodes_kernel(devices, mine_ref, other_ref, out_ref):
    def part(start, size):
        at = slice(start, start + size)
        return mine_ref[at, :].astype(jnp.float32) + other_ref[at, :].astype(jnp.float32)

    shift = digit_bits(devices)
    digits = -(-MAX_TOTAL_BITS // shift)
    lane = lax.broadcasted_iota(jnp.int32, (TOTAL_ROWS, LANES), 1)
    digit = lane % LANES_PER_GROUP
    worth = jnp.where(digit < digits, 1 << jnp.minimum(digit * shift, 30), 0).astype(jnp.float32)
    tile = part(COLS * GROUP_ROWS, TOTAL_ROWS) * worth
    totals = jnp.concatenate(
        [
            jnp.sum(jnp.where(lane // LANES_PER_GROUP == g, tile, 0.0), axis=1, keepdims=True)
            for g in range(GROUP_ROWS // TOTAL_ROWS)
        ],
        axis=0,
    )
    pooled = jnp.concatenate(
        [part(col * GROUP_ROWS, GROUP_ROWS) for col in range(COLS)], axis=1
    ) / (1.0 + totals)
    scale = lax.rsqrt(jnp.mean(pooled * pooled, axis=-1, keepdims=True) + 1e-06)
    out_ref[...] = (pooled * scale).astype(jnp.bfloat16)


def run_nodes(devices, mine, other):
    return pl.pallas_call(
        functools.partial(nodes_kernel, devices),
        out_shape=jax.ShapeDtypeStruct((GROUP_ROWS, D), jnp.bfloat16),
        compiler_params=pltpu.CompilerParams(vmem_limit_bytes=VMEM_LIMIT),
        name="nodes",
    )(mine, other)


def attention_kernel(first_ref, nodes_ref, proj_ref, gain_ref, out_ref):
    first = pl.multiple_of(first_ref[0], S_DEV)
    own = nodes_ref[pl.ds(first, S_DEV), :]
    queries = jnp.dot(own, proj_ref[:, :D], preferred_element_type=jnp.float32).astype(
        jnp.bfloat16
    )
    nodes = nodes_ref[...]
    keys = jnp.dot(nodes, proj_ref[:, D : 2 * D], preferred_element_type=jnp.float32).astype(
        jnp.bfloat16
    )
    values = jnp.dot(nodes, proj_ref[:, 2 * D :], preferred_element_type=jnp.float32).astype(
        jnp.bfloat16
    )
    lane = lax.broadcasted_iota(jnp.int32, (S_DEV, LANES), 1)
    low = lane < DH
    pieces = []
    for pair in range(COLS):
        at = slice(pair * LANES, (pair + 1) * LANES)
        both = queries[:, at]
        zero = jnp.zeros_like(both)
        stacked = jnp.concatenate(
            [jnp.where(low, both, zero), jnp.where(low, zero, both)], axis=0
        )
        scores = lax.dot_general(
            stacked, keys[:, at], (((1,), (1,)), ((), ())), preferred_element_type=jnp.float32
        ) * (DH**-0.5)
        exps = jnp.exp(scores - jnp.max(scores, axis=-1, keepdims=True))
        total = jnp.sum(exps, axis=-1, keepdims=True)
        summed = (
            jnp.dot(exps.astype(jnp.bfloat16), values[:, at], preferred_element_type=jnp.float32)
            / total
        )
        pieces.append(jnp.where(low, summed[:S_DEV], summed[S_DEV:]))
    attended = jnp.concatenate(pieces, axis=1)
    scale = lax.rsqrt(jnp.mean(attended * attended, axis=-1, keepdims=True) + 1e-06)
    out_ref[...] = (attended * scale * gain_ref[...].astype(jnp.float32)).astype(jnp.bfloat16)


def run_attention(first, nodes, proj_weight, gain):
    vmem = pl.BlockSpec(memory_space=pltpu.VMEM)
    return pl.pallas_call(
        attention_kernel,
        in_specs=[pl.BlockSpec(memory_space=pltpu.SMEM), vmem, vmem, vmem],
        out_specs=vmem,
        out_shape=jax.ShapeDtypeStruct((S_DEV, D), jnp.bfloat16),
        compiler_params=pltpu.CompilerParams(vmem_limit_bytes=VMEM_LIMIT),
        name="attention",
    )(first, nodes, proj_weight, gain)


def add_up(first, *rest):
    total = first.astype(jnp.float32)
    for term in rest:
        total = total + term.astype(jnp.float32)
    return total.astype(jnp.bfloat16)


def body(
    points_in,
    hidden_weight,
    output_weight,
    point_owner,
    point_node,
    point_weight,
    proj_weight,
    final_gain,
):
    rows = points_in.shape[0]
    devices = lax.axis_size("blk")
    me = lax.axis_index("blk").astype(jnp.int32)

    def swap(array, flip):
        return lax.ppermute(array, "blk", [(i, i ^ flip) for i in range(devices)])

    send, keep = run_points(
        devices,
        me.reshape(1),
        points_in,
        hidden_weight,
        output_weight,
        point_owner.reshape(1, rows),
        point_node.reshape(1, rows),
        point_weight.reshape(1, rows),
    )
    table = add_up(keep, swap(send, 1))
    groups = []
    width = (devices // 4).bit_length() - 1
    while width > 0:
        take = min(2, width)
        width -= take
        groups.append((take, width))
    for take, width in groups:
        size = (1 << width) * CHUNK
        parts = [table[j * size : (j + 1) * size] for j in range(1 << take)]
        order = list(range(1, 1 << take))[::-1]
        table = add_up(parts[0], *[swap(parts[j], j << (width + 1)) for j in order])
    nodes = run_nodes(devices, table, swap(table, devices // 2))
    for take, width in groups[::-1]:
        order = list(range(1, 1 << take))
        nodes = jnp.concatenate([nodes] + [swap(nodes, j << (width + 1)) for j in order], axis=0)
    nodes = jnp.concatenate([nodes, swap(nodes, 1)], axis=0)
    first = (me // (devices // 2) * S_DEV).reshape(1)
    return run_attention(first, nodes, proj_weight, final_gain.reshape(1, D))


def solution(mesh):
    placed = (
        P(("groups", "blk"), None),
        P(),
        P(),
        P(("groups", "blk"), None),
        P(("groups", "blk")),
        P(("groups", "blk")),
        P(),
        P(),
    )
    return jax.shard_map(
        body, mesh=mesh, in_specs=placed, out_specs=P(("groups", "blk"), None), check_vma=False
    )
```

time: 120 us -> 50 us (0.42)
  blocking collectives: 27.2 us -> 0 us
  matrix products: 23.4 us -> 0 us
  Pallas kernels: 0 us -> 17.7 us
  waiting for transfers between devices: 31.5 us -> 15.5 us
  local copies, waits for them, and re-layouts: 12.3 us -> 3.12 us
  starting transfers between devices: 17.7 us -> 11.2 us
  other arithmetic: 7.26 us -> 2.09 us
    all_to_all x3 -> x0, waiting for transfers between devices: 31.5 us -> none  [the longest x1 29.8 us: body(): lax.all_to_all(send_rows, 'blk', split_axis=0, concat_axis=0, tiled=True)]
    all_gather x1 -> x0, blocking collectives: 27.2 us -> none  [body(): lax.all_gather(normed_nodes, 'blk', axis=0, tiled=True)]
    dot_general x6 -> x0, matrix products: 23.4 us -> none  [the longest x1 17.9 us: body(): jnp.dot(hidden, output_weight, preferred_element_type=jnp.float32)]
    all_to_all x3 -> x0, starting transfers between devices: 17.7 us -> none  [the longest x1 7.39 us: body(): lax.all_to_all(send_weights, 'blk', split_axis=0, concat_axis=0, tiled=True)]
    pallas_call x0 -> x3, Pallas kernels: none -> 17.7 us  [the longest x1 9.87 us: run_points(): pl.pallas_call(functools.partial(points_kernel, devices, steps), grid=(st...]
    ppermute x0 -> x9, waiting for transfers between devices: none -> 15.5 us  [swap(): return lax.ppermute(array, 'blk', [(i, i ^ flip) for i in range(devices)])]
    ppermute x0 -> x9, starting transfers between devices: none -> 11.2 us  [swap(): return lax.ppermute(array, 'blk', [(i, i ^ flip) for i in range(devices)])]
    scatter x3 -> x0, local copies, waits for them, and re-layouts: 9.01 us -> none  [the longest x1 3.81 us: body(): send_rows = jnp.zeros((devices * slots, D), jnp.bfloat16).at[target].set(...]
  transfers between devices with their start and end apart: 3 -> 9, of which waited for: 2 -> 9; matrix products, arithmetic and copies ran while one was open for 23% -> 3% of each run, Pallas kernels for 0% -> 0%
where the time goes in v1:
time: 50 us; the launch traced here: 49.7 us
  Pallas kernels  17.7 us (35%)
  waiting for transfers between devices  15.5 us (31%)
  starting transfers between devices  11.2 us (22%)
  local copies, waits for them, and re-layouts  3.12 us (6%)
  other arithmetic  2.09 us (4%)
    ppermute x9, waiting for transfers between devices, swap(): return lax.ppermute(array, 'blk', [(i, i ^ flip) for i in range(devices)])  15.5 us
    ppermute x9, starting transfers between devices, swap(): return lax.ppermute(array, 'blk', [(i, i ^ flip) for i in range(devices)])  11.2 us
    pallas_call x1, Pallas kernels, run_points(): pl.pallas_call(functools.partial(points_kernel, devices, steps), grid=(st...  9.87 us
    pallas_call x1, Pallas kernels, run_attention(): pl.pallas_call(attention_kernel, in_specs=[pl.BlockSpec(memory_space=pltp...  5.97 us
    unnamed x12, local copies, waits for them, and re-layouts  2.48 us
    pallas_call x1, Pallas kernels, run_nodes(): pl.pallas_call(functools.partial(nodes_kernel, devices), out_shape=jax.Sh...  1.87 us
    convert_element_type x2, other arithmetic, add_up(): return total.astype(jnp.bfloat16)  1.17 us
  transfers between devices with their start and end apart: 9, of which 9 were waited for; matrix products, arithmetic and copies ran while one was open for 3% of the time, Pallas kernels for 0%

profile of v1, /device:TPU:0, one launch (start us, length us, event | category | flops | bytes accessed | tf_op | source)
XLA Modules:
  0.0 49.7 jit_solution(16647009373381461042)
XLA Ops:
  0.0 0.0 copy-start.3
  0.0 9.9 %points.1 = (bf16[1600,128]{1,0:T(8,128)(2,1)}, bf16[1600,128]{1,0:T(8,128)(2,1)}) custom-call(s32[1]{0:T(128)} %bitcast.1.me_ref, bf16[512,768]{1,0:T(8,128)(2,1)} %x_ref.1, bf16[768,2560]{1,0:T(8,128)(2,1)} %hidden_ref.1, bf16[2560,768]{1,0:T(8,128)(2,1)} %output_ref.1, s32[1,512]{1,0:T(1,128)} %bitcast.5, s32[1,512]{1,0:T(1,128)} %bitcast.6, s32[1,512]{1,0:T(1,128)} %bitcast.7), custom_call_target="tpu_custom_call" | custom-call | tf_op jit(solution)/shard_map/points/pallas_call | solution.py:104
  9.9 0.5 collective-permute-start
  10.4 1.6 %collective-permute-done = bf16[1600,128]{1,0:T(8,128)(2,1)S(1)} collective-permute-done((bf16[1600,128]{1,0:T(8,128)(2,1)}, bf16[1600,128]{1,0:T(8,128)(2,1)S(1)}, u32[]{:S(2)}, u32[]{:S(2)}) %collective-permute-start) | collective-permute-done | bytes 409632 | tf_op jit(solution)/shard_map/ppermute | solution.py:230
  11.9 1.1 %add_convert_fusion = bf16[1600,128]{1,0:T(8,128)(2,1)S(1)} fusion(bf16[1600,128]{1,0:T(8,128)(2,1)S(1)} %collective-permute-done, bf16[1600,128]{1,0:T(8,128)(2,1)} %get-tuple-element.7), kind=kLoop, calls=%fused_computation | loop fusion | flops 819200 | bytes 1228800 | tf_op jit(solution)/shard_map/convert_element_type | solution.py:212
  13.1 2.9 %collective-permute-start.3 = (bf16[400,128]{1,0:T(8,128)(2,1)S(1)}, bf16[400,128]{1,0:T(8,128)(2,1)S(1)}, u32[]{:S(2)}, u32[]{:S(2)}) collective-permute-start(bf16[400,128]{1,0:T(8,128)(2,1)S(1)} %get-tuple-element.10), channel_id=1, source_target_pairs={{0,2},{1,3},{2,0},{3,1},{4,6},{5,7},{6,4},{7,5},{8,10},{9,11},{10,... | collective-permute-start | bytes 307208 | tf_op jit(solution)/shard_map/ppermute | solution.py:230
  16.0 1.6 %collective-permute-start.2 = (bf16[400,128]{1,0:T(8,128)(2,1)S(1)}, bf16[400,128]{1,0:T(8,128)(2,1)S(1)}, u32[]{:S(2)}, u32[]{:S(2)}) collective-permute-start(bf16[400,128]{1,0:T(8,128)(2,1)S(1)} %get-tuple-element.11), channel_id=1, source_target_pairs={{0,4},{1,5},{2,6},{3,7},{4,0},{5,1},{6,2},{7,3},{8,12},{9,13},{10,... | collective-permute-start | bytes 307208 | tf_op jit(solution)/shard_map/ppermute | solution.py:230
  17.6 0.0 collective-permute-start.1
  17.6 1.6 %collective-permute-done.3 = bf16[400,128]{1,0:T(8,128)(2,1)S(1)} collective-permute-done((bf16[400,128]{1,0:T(8,128)(2,1)S(1)}, bf16[400,128]{1,0:T(8,128)(2,1)S(1)}, u32[]{:S(2)}, u32[]{:S(2)}) %collective-permute-start.3) | collective-permute-done | bytes 102432 | tf_op jit(solution)/shard_map/ppermute | solution.py:230
  19.2 2.4 %collective-permute-done.2 = bf16[400,128]{1,0:T(8,128)(2,1)S(1)} collective-permute-done((bf16[400,128]{1,0:T(8,128)(2,1)S(1)}, bf16[400,128]{1,0:T(8,128)(2,1)S(1)}, u32[]{:S(2)}, u32[]{:S(2)}) %collective-permute-start.2) | collective-permute-done | bytes 102432 | tf_op jit(solution)/shard_map/ppermute | solution.py:230
  21.7 1.5 %collective-permute-done.1 = bf16[400,128]{1,0:T(8,128)(2,1)S(1)} collective-permute-done((bf16[400,128]{1,0:T(8,128)(2,1)S(1)}, bf16[400,128]{1,0:T(8,128)(2,1)S(1)}, u32[]{:S(2)}, u32[]{:S(2)}) %collective-permute-start.1) | collective-permute-done | bytes 102432 | tf_op jit(solution)/shard_map/ppermute | solution.py:230
  23.2 0.1 add_convert_fusion.1.mine_ref
  23.2 0.0 copy-start.1
  23.2 2.6 %collective-permute-start.4 = (bf16[400,128]{1,0:T(8,128)(2,1)S(1)}, bf16[400,128]{1,0:T(8,128)(2,1)S(1)}, u32[]{:S(2)}, u32[]{:S(2)}) collective-permute-start(bf16[400,128]{1,0:T(8,128)(2,1)S(1)} %add_convert_fusion.1.mine_ref), channel_id=1, source_target_pairs={{0,8},{1,9},{2,10},{3,11},{4,12},{5,13},{6,14},{7,15},{8,0},{9,1},... | collective-permute-start | bytes 307208 | tf_op jit(solution)/shard_map/ppermute | solution.py:230
  25.9 4.1 %collective-permute-done.4.other_ref = bf16[400,128]{1,0:T(8,128)(2,1)S(1)} collective-permute-done((bf16[400,128]{1,0:T(8,128)(2,1)S(1)}, bf16[400,128]{1,0:T(8,128)(2,1)S(1)}, u32[]{:S(2)}, u32[]{:S(2)}) %collective-permute-start.4) | collective-permute-done | bytes 102432 | tf_op jit(solution)/shard_map/ppermute | solution.py:230
  30.0 0.0 copy-done.1
  30.0 0.0 copy-start.2
  30.0 0.6 %copy-done.2 = bf16[400,128]{1,0:T(8,128)(2,1)} copy-done((bf16[400,128]{1,0:T(8,128)(2,1)}, bf16[400,128]{1,0:T(8,128)(2,1)S(1)}, u32[]{:S(2)}) %copy-start.2) | copy-done | bytes 102424
  30.6 1.9 %nodes.1 = bf16[64,768]{1,0:T(8,128)(2,1)} custom-call(bf16[400,128]{1,0:T(8,128)(2,1)} %copy-done.1, bf16[400,128]{1,0:T(8,128)(2,1)} %copy-done.2), custom_call_target="tpu_custom_call" | custom-call | tf_op jit(solution)/shard_map/nodes/pallas_call | solution.py:150
  32.5 1.5 %collective-permute-start.5 = (bf16[64,768]{1,0:T(8,128)(2,1)}, bf16[64,768]{1,0:T(8,128)(2,1)S(1)}, u32[]{:S(2)}, u32[]{:S(2)}) collective-permute-start(bf16[64,768]{1,0:T(8,128)(2,1)} %nodes.1), channel_id=1, source_target_pairs={{0,2},{1,3},{2,0},{3,1},{4,6},{5,7},{6,4},{7,5},{8,10},{9,11},{10,... | collective-permute-start | bytes 294920 | tf_op jit(solution)/shard_map/ppermute | solution.py:230
  34.0 0.3 collective-permute-start.6
  34.3 1.6 %collective-permute-start.7 = (bf16[64,768]{1,0:T(8,128)(2,1)}, bf16[64,768]{1,0:T(8,128)(2,1)S(1)}, u32[]{:S(2)}, u32[]{:S(2)}) collective-permute-start(bf16[64,768]{1,0:T(8,128)(2,1)} %nodes.1), channel_id=1, source_target_pairs={{0,6},{1,7},{2,4},{3,5},{4,2},{5,3},{6,0},{7,1},{8,14},{9,15},{10,... | collective-permute-start | bytes 294920 | tf_op jit(solution)/shard_map/ppermute | solution.py:230
  36.0 0.0 copy-done.3
  36.0 0.6 %reshape.23.gain_ref = bf16[1,768]{1,0:T(2,128)(2,1)} reshape(bf16[768]{0:T(1024)(128)(2,1)S(1)} %copy-done.3) | data formatting | bytes 3072 | tf_op jit(solution)/shard_map/reshape | solution.py:260
  36.6 1.2 %collective-permute-done.5 = bf16[64,768]{1,0:T(8,128)(2,1)S(1)} collective-permute-done((bf16[64,768]{1,0:T(8,128)(2,1)}, bf16[64,768]{1,0:T(8,128)(2,1)S(1)}, u32[]{:S(2)}, u32[]{:S(2)}) %collective-permute-start.5) | collective-permute-done | bytes 98336 | tf_op jit(solution)/shard_map/ppermute | solution.py:230
  37.8 1.1 %collective-permute-done.6 = bf16[64,768]{1,0:T(8,128)(2,1)S(1)} collective-permute-done((bf16[64,768]{1,0:T(8,128)(2,1)}, bf16[64,768]{1,0:T(8,128)(2,1)S(1)}, u32[]{:S(2)}, u32[]{:S(2)}) %collective-permute-start.6) | collective-permute-done | bytes 98336 | tf_op jit(solution)/shard_map/ppermute | solution.py:230
  38.8 1.2 %collective-permute-done.7 = bf16[64,768]{1,0:T(8,128)(2,1)S(1)} collective-permute-done((bf16[64,768]{1,0:T(8,128)(2,1)}, bf16[64,768]{1,0:T(8,128)(2,1)S(1)}, u32[]{:S(2)}, u32[]{:S(2)}) %collective-permute-start.7) | collective-permute-done | bytes 98336 | tf_op jit(solution)/shard_map/ppermute | solution.py:230
  40.1 0.9 %pad_maximum_fusion = bf16[256,768]{1,0:T(8,128)(2,1)S(1)} fusion(bf16[64,768]{1,0:T(8,128)(2,1)S(1)} %collective-permute-done.7, bf16[64,768]{1,0:T(8,128)(2,1)S(1)} %collective-permute-done.6, bf16[64,768]{1,0:T(8,128)(2,1)S(1)} %collective-permute-done.5, bf16[64,768]{1,0:T(8,128)(2,1)} %nodes.1), kind=kLoop, calls=%fused_computation.1 | loop fusion | flops 1572864 | bytes 786432 | tf_op jit(solution)/shard_map/concatenate | solution.py:257
  41.0 0.1 collective-permute-start.8
  41.1 0.9 %constant_dynamic-update-slice_fusion.4 = bf16[512,768]{1,0:T(8,128)(2,1)S(1)} fusion(bf16[64,768]{1,0:T(8,128)(2,1)} %nodes.1), kind=kLoop, calls=%fused_computation.7 | loop fusion | bytes 196608
  42.0 0.8 %collective-permute-done.8 = bf16[256,768]{1,0:T(8,128)(2,1)S(1)} collective-permute-done((bf16[256,768]{1,0:T(8,128)(2,1)S(1)}, bf16[256,768]{1,0:T(8,128)(2,1)S(1)}, u32[]{:S(2)}, u32[]{:S(2)}) %collective-permute-start.8) | collective-permute-done | bytes 393248 | tf_op jit(solution)/shard_map/ppermute | solution.py:230
  42.8 0.0 copy-start
  42.8 0.9 %copy-done = bf16[512,768]{1,0:T(8,128)(2,1)} copy-done((bf16[512,768]{1,0:T(8,128)(2,1)}, bf16[512,768]{1,0:T(8,128)(2,1)S(1)}, u32[]{:S(2)}) %copy-start) | copy-done | bytes 786456
  43.7 6.0 %attention.1 = bf16[32,768]{1,0:T(8,128)(2,1)} custom-call(s32[1]{0:T(128)} %bitcast.first_ref, bf16[512,768]{1,0:T(8,128)(2,1)} %copy-done, bf16[768,2304]{1,0:T(8,128)(2,1)} %proj_ref.1, bf16[1,768]{1,0:T(2,128)(2,1)} %reshape.23.gain_ref), custom_call_target="tpu_custom_call" | custom-call | tf_op jit(solution)/shard_map/attention/pallas_call | solution.py:198
  (5 shorter events, 0.1 us)
Async XLA Ops:
  0.0 36.0 %copy-start.3 = (bf16[768]{0:T(1024)(128)(2,1)S(1)}, bf16[768]{0:T(1024)(128)(2,1)}, u32[]{:S(2)}) copy-start(bf16[768]{0:T(1024)(128)(2,1)} %param.15) | copy-start | bytes 4612
  9.9 2.1 %collective-permute-start = (bf16[1600,128]{1,0:T(8,128)(2,1)}, bf16[1600,128]{1,0:T(8,128)(2,1)S(1)}, u32[]{:S(2)}, u32[]{:S(2)}) collective-permute-start(bf16[1600,128]{1,0:T(8,128)(2,1)} %get-tuple-element.8), channel_id=1, source_target_pairs={{0,1},{1,0},{2,3},{3,2},{4,5},{5,4},{6,7},{7,6},{8,9},{9,8},{10,11... | collective-permute-start | bytes 1228808 | tf_op jit(solution)/shard_map/ppermute | solution.py:230
  13.1 6.1 %collective-permute-start.3 = (bf16[400,128]{1,0:T(8,128)(2,1)S(1)}, bf16[400,128]{1,0:T(8,128)(2,1)S(1)}, u32[]{:S(2)}, u32[]{:S(2)}) collective-permute-start(bf16[400,128]{1,0:T(8,128)(2,1)S(1)} %get-tuple-element.10), channel_id=1, source_target_pairs={{0,2},{1,3},{2,0},{3,1},{4,6},{5,7},{6,4},{7,5},{8,10},{9,11},{10,... | collective-permute-start | bytes 307208 | tf_op jit(solution)/shard_map/ppermute | solution.py:230
  16.0 5.6 %collective-permute-start.2 = (bf16[400,128]{1,0:T(8,128)(2,1)S(1)}, bf16[400,128]{1,0:T(8,128)(2,1)S(1)}, u32[]{:S(2)}, u32[]{:S(2)}) collective-permute-start(bf16[400,128]{1,0:T(8,128)(2,1)S(1)} %get-tuple-element.11), channel_id=1, source_target_pairs={{0,4},{1,5},{2,6},{3,7},{4,0},{5,1},{6,2},{7,3},{8,12},{9,13},{10,... | collective-permute-start | bytes 307208 | tf_op jit(solution)/shard_map/ppermute | solution.py:230
  17.6 5.6 %collective-permute-start.1 = (bf16[400,128]{1,0:T(8,128)(2,1)S(1)}, bf16[400,128]{1,0:T(8,128)(2,1)S(1)}, u32[]{:S(2)}, u32[]{:S(2)}) collective-permute-start(bf16[400,128]{1,0:T(8,128)(2,1)S(1)} %get-tuple-element.9), channel_id=1, source_target_pairs={{0,6},{1,7},{2,4},{3,5},{4,2},{5,3},{6,0},{7,1},{8,14},{9,15},{10,... | collective-permute-start | bytes 307208 | tf_op jit(solution)/shard_map/ppermute | solution.py:230
  23.2 6.7 %copy-start.1 = (bf16[400,128]{1,0:T(8,128)(2,1)}, bf16[400,128]{1,0:T(8,128)(2,1)S(1)}, u32[]{:S(2)}) copy-start(bf16[400,128]{1,0:T(8,128)(2,1)S(1)} %add_convert_fusion.1.mine_ref) | copy-start | bytes 307204
  23.2 6.7 %collective-permute-start.4 = (bf16[400,128]{1,0:T(8,128)(2,1)S(1)}, bf16[400,128]{1,0:T(8,128)(2,1)S(1)}, u32[]{:S(2)}, u32[]{:S(2)}) collective-permute-start(bf16[400,128]{1,0:T(8,128)(2,1)S(1)} %add_convert_fusion.1.mine_ref), channel_id=1, source_target_pairs={{0,8},{1,9},{2,10},{3,11},{4,12},{5,13},{6,14},{7,15},{8,0},{9,1},... | collective-permute-start | bytes 307208 | tf_op jit(solution)/shard_map/ppermute | solution.py:230
  30.0 0.6 %copy-start.2 = (bf16[400,128]{1,0:T(8,128)(2,1)}, bf16[400,128]{1,0:T(8,128)(2,1)S(1)}, u32[]{:S(2)}) copy-start(bf16[400,128]{1,0:T(8,128)(2,1)S(1)} %collective-permute-done.4.other_ref) | copy-start | bytes 307204
  32.5 5.3 %collective-permute-start.5 = (bf16[64,768]{1,0:T(8,128)(2,1)}, bf16[64,768]{1,0:T(8,128)(2,1)S(1)}, u32[]{:S(2)}, u32[]{:S(2)}) collective-permute-start(bf16[64,768]{1,0:T(8,128)(2,1)} %nodes.1), channel_id=1, source_target_pairs={{0,2},{1,3},{2,0},{3,1},{4,6},{5,7},{6,4},{7,5},{8,10},{9,11},{10,... | collective-permute-start | bytes 294920 | tf_op jit(solution)/shard_map/ppermute | solution.py:230
  34.0 4.8 %collective-permute-start.6 = (bf16[64,768]{1,0:T(8,128)(2,1)}, bf16[64,768]{1,0:T(8,128)(2,1)S(1)}, u32[]{:S(2)}, u32[]{:S(2)}) collective-permute-start(bf16[64,768]{1,0:T(8,128)(2,1)} %nodes.1), channel_id=1, source_target_pairs={{0,4},{1,5},{2,6},{3,7},{4,0},{5,1},{6,2},{7,3},{8,12},{9,13},{10,... | collective-permute-start | bytes 294920 | tf_op jit(solution)/shard_map/ppermute | solution.py:230
  34.3 5.7 %collective-permute-start.7 = (bf16[64,768]{1,0:T(8,128)(2,1)}, bf16[64,768]{1,0:T(8,128)(2,1)S(1)}, u32[]{:S(2)}, u32[]{:S(2)}) collective-permute-start(bf16[64,768]{1,0:T(8,128)(2,1)} %nodes.1), channel_id=1, source_target_pairs={{0,6},{1,7},{2,4},{3,5},{4,2},{5,3},{6,0},{7,1},{8,14},{9,15},{10,... | collective-permute-start | bytes 294920 | tf_op jit(solution)/shard_map/ppermute | solution.py:230
  41.0 1.8 %collective-permute-start.8 = (bf16[256,768]{1,0:T(8,128)(2,1)S(1)}, bf16[256,768]{1,0:T(8,128)(2,1)S(1)}, u32[]{:S(2)}, u32[]{:S(2)}) collective-permute-start(bf16[256,768]{1,0:T(8,128)(2,1)S(1)} %pad_maximum_fusion), channel_id=1, source_target_pairs={{0,1},{1,0},{2,3},{3,2},{4,5},{5,4},{6,7},{7,6},{8,9},{9,8},{10,11... | collective-permute-start | bytes 1179656 | tf_op jit(solution)/shard_map/ppermute | solution.py:230
  42.8 0.9 %copy-start = (bf16[512,768]{1,0:T(8,128)(2,1)}, bf16[512,768]{1,0:T(8,128)(2,1)S(1)}, u32[]{:S(2)}) copy-start(bf16[512,768]{1,0:T(8,128)(2,1)S(1)} %constant_dynamic-update-slice_fusion.nodes_ref) | copy-start | bytes 2359300

commit v2 on v1

v2 whole, which is shorter than its diff:
```python
import functools

import jax
import jax.numpy as jnp
from jax import lax
from jax.experimental import pallas as pl
from jax.experimental.pallas import tpu as pltpu
from jax.sharding import PartitionSpec as P

D = 768
HEADS = 12
S_DEV = 32
DH = 64
LANES = 128
GROUP_ROWS = 2 * S_DEV
COLS = D // LANES
TOTAL_ROWS = 16
CHUNK = COLS * GROUP_ROWS + TOTAL_ROWS
LANES_PER_GROUP = LANES // (GROUP_ROWS // TOTAL_ROWS)
MIB = 1024 * 1024


def digit_bits(devices):
    return max(1, (256 // devices).bit_length() - 1)


def total_bits(rows):
    return (4 * rows).bit_length()


def gelu(values):
    return 0.5 * values * (1.0 + lax.erf(values * 0.7071067811865476))


def hidden_cols(ff):
    return 512 if ff % 512 == 0 else ff


def points_kernel(
    devices, me_ref, x_hbm, hidden_hbm, output_hbm, owner_hbm, node_hbm, weight_hbm,
    send_ref, keep_ref, owner_ref, node_ref, weight_ref, x_ref, normed_ref, hidden_ref, output_ref, coeffs_ref, middle_ref, sems,
):
    rows = x_ref.shape[0]
    ff = hidden_ref.shape[1]
    cols = hidden_cols(ff)

    def hidden_copy(part):
        at = pl.ds(pl.multiple_of(part * cols, cols), cols)
        return pltpu.make_async_copy(hidden_hbm.at[:, at], hidden_ref.at[:, at], sems.at[2 + part])

    x_copy = pltpu.make_async_copy(x_hbm, x_ref, sems.at[0])
    output_copy = pltpu.make_async_copy(output_hbm, output_ref, sems.at[1])
    index_copies = [
        pltpu.make_async_copy(source, target, sems.at[2 + ff // cols + i])
        for i, (source, target) in enumerate(
            ((owner_hbm, owner_ref), (node_hbm, node_ref), (weight_hbm, weight_ref))
        )
    ]
    for copy in index_copies:
        copy.start()
    x_copy.start()
    for part in range(ff // cols):
        hidden_copy(part).start()
    output_copy.start()

    chunks = devices // 4
    half = chunks * GROUP_ROWS
    places = [
        (out_ref, chunk * CHUNK, core * half + chunk * GROUP_ROWS)
        for core, out_ref in ((0, keep_ref), (1, send_ref))
        for chunk in range(chunks)
    ]
    me = me_ref[0]

    @pl.when(me >= 0)
    def _():
        for copy in index_copies:
            copy.wait()
        owner = owner_ref[...]
        near = (owner ^ me) & (devices // 2 - 1)
        row_of = (near // 2) * GROUP_ROWS + (owner // (devices // 2)) * S_DEV + node_ref[...]
        row_of = row_of + (near & 1) * half
        coeffs = jnp.where(
            row_of == lax.broadcasted_iota(jnp.int32, (2 * half, rows), 0), weight_ref[...], 0
        ).astype(jnp.float32)
        coeffs_ref[...] = coeffs.astype(jnp.bfloat16)
        totals = jnp.sum(coeffs, axis=1, keepdims=True).astype(jnp.int32)
        shift = digit_bits(devices)
        digits = -(-total_bits(rows) // shift)
        lane = lax.broadcasted_iota(jnp.int32, (TOTAL_ROWS, LANES), 1)
        digit = lane % LANES_PER_GROUP
        held = jnp.where(digit < digits, digit * shift, 31)
        for out_ref, base, first in places:
            tile = jnp.zeros((TOTAL_ROWS, LANES), jnp.int32)
            for group in range(GROUP_ROWS // TOTAL_ROWS):
                start = first + group * TOTAL_ROWS
                value = jnp.broadcast_to(totals[start : start + TOTAL_ROWS], (TOTAL_ROWS, LANES))
                tile = jnp.where(lane // LANES_PER_GROUP == group, value, tile)
            tile = (tile >> held) & ((1 << shift) - 1)
            out_ref[base + COLS * GROUP_ROWS : base + CHUNK, :] = tile.astype(
                jnp.float32
            ).astype(jnp.bfloat16)

    x_copy.wait()
    x = x_ref[...].astype(jnp.float32)
    scale = lax.rsqrt(jnp.mean(x * x, axis=-1, keepdims=True) + 1e-06)
    normed_ref[...] = (x * scale).astype(jnp.bfloat16)

    def one_part(part, carry):
        at = pl.ds(pl.multiple_of(part * cols, cols), cols)
        hidden_copy(part).wait()
        middle_ref[:, at] = gelu(
            jnp.dot(normed_ref[...], hidden_ref[:, at], preferred_element_type=jnp.float32)
        ).astype(jnp.bfloat16)
        return carry

    lax.fori_loop(0, ff // cols, one_part, 0)
    output_copy.wait()
    features = (
        x_ref[...].astype(jnp.float32)
        + jnp.dot(middle_ref[...], output_ref[...], preferred_element_type=jnp.float32)
    ).astype(jnp.bfloat16)
    sums = jnp.dot(coeffs_ref[...], features, preferred_element_type=jnp.float32).astype(
        jnp.bfloat16
    )
    for out_ref, base, first in places:
        for col in range(COLS):
            out_ref[base + col * GROUP_ROWS : base + (col + 1) * GROUP_ROWS, :] = sums[
                first : first + GROUP_ROWS, col * LANES : (col + 1) * LANES
            ]


def run_points(devices, me, x, hidden_weight, output_weight, owner, node, weight):
    rows, ff = x.shape[0], hidden_weight.shape[1]
    nodes = devices * S_DEV
    out = pltpu.VMEM((devices // 4 * CHUNK, LANES), jnp.bfloat16)
    hbm = pl.BlockSpec(memory_space=pl.ANY)
    vmem = pl.BlockSpec(memory_space=pltpu.VMEM)
    in_hbm = [
        pltpu.with_memory_space_constraint(array, pltpu.HBM)
        for array in (x, hidden_weight, output_weight, owner, node, weight)
    ]
    return pl.pallas_call(
        functools.partial(points_kernel, devices),
        in_specs=[pl.BlockSpec(memory_space=pltpu.SMEM)] + [hbm] * 6,
        out_specs=[vmem, vmem],
        out_shape=[out, out],
        scratch_shapes=[
            pltpu.VMEM((1, rows), jnp.int32),
            pltpu.VMEM((1, rows), jnp.int32),
            pltpu.VMEM((1, rows), jnp.int32),
            pltpu.VMEM((rows, D), jnp.bfloat16),
            pltpu.VMEM((rows, D), jnp.bfloat16),
            pltpu.VMEM((D, ff), jnp.bfloat16),
            pltpu.VMEM((ff, D), jnp.bfloat16),
            pltpu.VMEM((nodes, rows), jnp.bfloat16),
            pltpu.VMEM((rows, ff), jnp.bfloat16),
            pltpu.SemaphoreType.DMA((5 + ff // hidden_cols(ff),)),
        ],
        compiler_params=pltpu.CompilerParams(vmem_limit_bytes=28 * MIB + 8 * nodes * D),
        name="points",
    )(me, *in_hbm)


def nodes_kernel(devices, rows, mine_ref, other_ref, out_ref):
    def part(start, size):
        at = slice(start, start + size)
        return mine_ref[at, :].astype(jnp.float32) + other_ref[at, :].astype(jnp.float32)

    shift = digit_bits(devices)
    digits = -(-total_bits(rows) // shift)
    lane = lax.broadcasted_iota(jnp.int32, (TOTAL_ROWS, LANES), 1)
    digit = lane % LANES_PER_GROUP
    worth = jnp.where(digit < digits, 1 << jnp.minimum(digit * shift, 30), 0).astype(jnp.float32)
    tile = part(COLS * GROUP_ROWS, TOTAL_ROWS) * worth
    totals = jnp.concatenate(
        [
            jnp.sum(jnp.where(lane // LANES_PER_GROUP == g, tile, 0.0), axis=1, keepdims=True)
            for g in range(GROUP_ROWS // TOTAL_ROWS)
        ],
        axis=0,
    )
    pooled = jnp.concatenate(
        [part(col * GROUP_ROWS, GROUP_ROWS) for col in range(COLS)], axis=1
    ) / (1.0 + totals)
    scale = lax.rsqrt(jnp.mean(pooled * pooled, axis=-1, keepdims=True) + 1e-06)
    out_ref[...] = (pooled * scale).astype(jnp.bfloat16)


def run_nodes(devices, rows, mine, other):
    return pl.pallas_call(
        functools.partial(nodes_kernel, devices, rows),
        out_shape=pltpu.VMEM((GROUP_ROWS, D), jnp.bfloat16),
        compiler_params=pltpu.CompilerParams(vmem_limit_bytes=8 * MIB),
        name="nodes",
    )(mine, other)


def attention_kernel(first_ref, proj_ref, gain_ref, *refs):
    *pieces, out_ref, nodes_ref = refs
    first = pl.multiple_of(first_ref[0], S_DEV)
    queries = jnp.dot(
        pieces[0][pl.ds(first, S_DEV), :], proj_ref[:, :D], preferred_element_type=jnp.float32
    ).astype(jnp.bfloat16)
    start = 0
    for piece in pieces:
        nodes_ref[start : start + piece.shape[0], :] = piece[...]
        start += piece.shape[0]
    nodes = nodes_ref[...]
    keys = jnp.dot(nodes, proj_ref[:, D : 2 * D], preferred_element_type=jnp.float32).astype(
        jnp.bfloat16
    )
    values = jnp.dot(nodes, proj_ref[:, 2 * D :], preferred_element_type=jnp.float32).astype(
        jnp.bfloat16
    )
    lane = lax.broadcasted_iota(jnp.int32, (S_DEV, LANES), 1)
    low = lane < DH
    heads = []
    for pair in range(COLS):
        at = slice(pair * LANES, (pair + 1) * LANES)
        both = queries[:, at]
        zero = jnp.zeros_like(both)
        stacked = jnp.concatenate(
            [jnp.where(low, both, zero), jnp.where(low, zero, both)], axis=0
        )
        scores = lax.dot_general(
            stacked, keys[:, at], (((1,), (1,)), ((), ())), preferred_element_type=jnp.float32
        ) * (DH**-0.5)
        exps = jnp.exp(scores - jnp.max(scores, axis=-1, keepdims=True))
        total = jnp.sum(exps, axis=-1, keepdims=True)
        summed = (
            jnp.dot(exps.astype(jnp.bfloat16), values[:, at], preferred_element_type=jnp.float32)
            / total
        )
        heads.append(jnp.where(low, summed[:S_DEV], summed[S_DEV:]))
    attended = jnp.concatenate(heads, axis=1)
    scale = lax.rsqrt(jnp.mean(attended * attended, axis=-1, keepdims=True) + 1e-06)
    out_ref[...] = (attended * scale * gain_ref[...].astype(jnp.float32)).astype(jnp.bfloat16)


def run_attention(first, proj_weight, gain, pieces):
    vmem = pl.BlockSpec(memory_space=pltpu.VMEM)
    nodes = sum(piece.shape[0] for piece in pieces)
    return pl.pallas_call(
        attention_kernel,
        in_specs=[pl.BlockSpec(memory_space=pltpu.SMEM)] + [vmem] * (2 + len(pieces)),
        out_specs=vmem,
        out_shape=jax.ShapeDtypeStruct((S_DEV, D), jnp.bfloat16),
        scratch_shapes=[pltpu.VMEM((nodes, D), jnp.bfloat16)],
        compiler_params=pltpu.CompilerParams(vmem_limit_bytes=16 * MIB + 6 * nodes * D),
        name="attention",
    )(first, proj_weight, gain, *pieces)


def add_up(first, *rest):
    total = first.astype(jnp.float32)
    for term in rest:
        total = total + term.astype(jnp.float32)
    return total.astype(jnp.bfloat16)


def body(
    points_in,
    hidden_weight,
    output_weight,
    point_owner,
    point_node,
    point_weight,
    proj_weight,
    final_gain,
):
    rows = points_in.shape[0]
    devices = lax.axis_size("blk")
    me = lax.axis_index("blk").astype(jnp.int32)

    def swap(array, flip):
        return lax.ppermute(array, "blk", [(i, i ^ flip) for i in range(devices)])

    send, keep = run_points(
        devices,
        me.reshape(1),
        points_in,
        hidden_weight,
        output_weight,
        point_owner.reshape(1, rows),
        point_node.reshape(1, rows),
        point_weight.reshape(1, rows),
    )
    table = add_up(keep, swap(send, 1))
    groups = []
    width = (devices // 4).bit_length() - 1
    while width > 0:
        take = min(2, width)
        width -= take
        groups.append((take, width))
    for take, width in groups:
        size = (1 << width) * CHUNK
        parts = [table[j * size : (j + 1) * size] for j in range(1 << take)]
        order = list(range(1, 1 << take))[::-1]
        table = add_up(parts[0], *[swap(parts[j], j << (width + 1)) for j in order])
    nodes = run_nodes(devices, rows, table, swap(table, devices // 2))
    pieces = [nodes]
    for take, width in groups[::-1]:
        nodes = jnp.concatenate(pieces, axis=0)
        pieces = [nodes] + [swap(nodes, j << (width + 1)) for j in range(1, 1 << take)]
    pieces.append(swap(jnp.concatenate(pieces, axis=0), 1))
    first = (me // (devices // 2) * S_DEV).reshape(1)
    return run_attention(first, proj_weight, final_gain.reshape(1, D), pieces)


def solution(mesh):
    placed = (
        P(("groups", "blk"), None),
        P(),
        P(),
        P(("groups", "blk"), None),
        P(("groups", "blk")),
        P(("groups", "blk")),
        P(),
        P(),
    )
    return jax.shard_map(
        body, mesh=mesh, in_specs=placed, out_specs=P(("groups", "blk"), None), check_vma=False
    )
```

time: 50 us -> 47.5 us (0.950)
  Pallas kernels: 17.7 us -> 12.8 us
  waiting for transfers between devices: 15.5 us -> 17.6 us
  other arithmetic: 2.09 us -> 0.95 us
  local copies, waits for them, and re-layouts: 3.12 us -> 4.25 us
    pallas_call x2, Pallas kernels: 11.7 us -> 8.05 us  [the longest x1 7.78 us: run_points(): pl.pallas_call(functools.partial(points_kernel, devices), in_specs=[pl.Bl...]
    ppermute x9, waiting for transfers between devices: 15.5 us -> 17.6 us  [swap(): return lax.ppermute(array, 'blk', [(i, i ^ flip) for i in range(devices)])]
    unnamed x12 -> x20, local copies, waits for them, and re-layouts: 2.48 us -> 4.22 us
    pallas_call x1, Pallas kernels: 5.97 us -> 4.77 us  [run_attention(): pl.pallas_call(attention_kernel, in_specs=[pl.BlockSpec(memory_space=pltp...]
    convert_element_type x2, other arithmetic: 1.17 us -> 0.17 us  [add_up(): return total.astype(jnp.bfloat16)]
    reshape x1, local copies, waits for them, and re-layouts: 0.59 us -> 0.01 us  [body(): return run_attention(first, proj_weight, final_gain.reshape(1, D), pieces)]
  transfers between devices with their start and end apart: 9 -> 9, of which waited for: 9 -> 8; matrix products, arithmetic and copies ran while one was open for 3% -> 0% of each run, Pallas kernels for 0% -> 0%
where the time goes in v2:
time: 47.5 us; the launch traced here: 47.2 us
  waiting for transfers between devices  17.6 us (37%)
  Pallas kernels  12.8 us (27%)
  starting transfers between devices  11.5 us (24%)
  local copies, waits for them, and re-layouts  4.25 us (9%)
  other arithmetic  0.95 us (2%)
    ppermute x9, waiting for transfers between devices, swap(): return lax.ppermute(array, 'blk', [(i, i ^ flip) for i in range(devices)])  17.6 us
    ppermute x9, starting transfers between devices, swap(): return lax.ppermute(array, 'blk', [(i, i ^ flip) for i in range(devices)])  11.5 us
    pallas_call x1, Pallas kernels, run_points(): pl.pallas_call(functools.partial(points_kernel, devices), in_specs=[pl.Bl...  7.78 us
    pallas_call x1, Pallas kernels, run_attention(): pl.pallas_call(attention_kernel, in_specs=[pl.BlockSpec(memory_space=pltp...  4.77 us
    unnamed x20, local copies, waits for them, and re-layouts  4.22 us
  transfers between devices with their start and end apart: 9, of which 8 were waited for; matrix products, arithmetic and copies ran while one was open for 0% of the time, Pallas kernels for 0%

profile of v2, /device:TPU:0, one launch (start us, length us, event | category | flops | bytes accessed | tf_op | source)
XLA Modules:
  0.0 47.2 jit_solution(5718875329132983461)
XLA Ops:
  0.0 0.0 copy-start.9
  0.0 0.0 copy-start
  0.0 7.8 %points.1 = (bf16[1600,128]{1,0:T(8,128)(2,1)S(1)}, bf16[1600,128]{1,0:T(8,128)(2,1)S(1)}) custom-call(s32[1]{0:T(128)} %bitcast.1.me_ref, bf16[512,768]{1,0:T(8,128)(2,1)} %x_hbm.1, bf16[768,2560]{1,0:T(8,128)(2,1)} %hidden_hbm.1, bf16[2560,768]{1,0:T(8,128)(2,1)} %output_hbm.1, s32[1,512]{1,0:T(1,128)} %bitcast.5, s32[1,512]{1,0:T(1,128)} %bitcast.6, ...), custom_call_target="tpu_custom_call" | custom-call | tf_op jit(solution)/shard_map/points/pallas_call | solution.py:143
  7.8 0.5 %collective-permute-start = (bf16[1600,128]{1,0:T(8,128)(2,1)S(1)}, bf16[1600,128]{1,0:T(8,128)(2,1)S(1)}, u32[]{:S(2)}, u32[]{:S(2)}) collective-permute-start(bf16[1600,128]{1,0:T(8,128)(2,1)S(1)} %get-tuple-element.8), channel_id=1, source_target_pairs={{0,1},{1,0},{2,3},{3,2},{4,5},{5,4},{6,7},{7,6},{8,9},{9,8},{10,11... | collective-permute-start | bytes 1228808 | tf_op jit(solution)/shard_map/ppermute | solution.py:277
  8.3 1.4 %collective-permute-done = bf16[1600,128]{1,0:T(8,128)(2,1)S(1)} collective-permute-done((bf16[1600,128]{1,0:T(8,128)(2,1)S(1)}, bf16[1600,128]{1,0:T(8,128)(2,1)S(1)}, u32[]{:S(2)}, u32[]{:S(2)}) %collective-permute-start) | collective-permute-done | bytes 409632 | tf_op jit(solution)/shard_map/ppermute | solution.py:277
  9.7 0.1 add_convert_fusion
  9.8 4.0 %collective-permute-start.1 = (bf16[400,128]{1,0:T(8,128)(2,1)S(1)}, bf16[400,128]{1,0:T(8,128)(2,1)S(1)}, u32[]{:S(2)}, u32[]{:S(2)}) collective-permute-start(bf16[400,128]{1,0:T(8,128)(2,1)S(1)} %get-tuple-element.9), channel_id=1, source_target_pairs={{0,6},{1,7},{2,4},{3,5},{4,2},{5,3},{6,0},{7,1},{8,14},{9,15},{10,... | collective-permute-start | bytes 307208 | tf_op jit(solution)/shard_map/ppermute | solution.py:277
  13.8 0.5 collective-permute-start.2
  14.2 0.2 collective-permute-start.3
  14.4 3.0 %collective-permute-done.1 = bf16[400,128]{1,0:T(8,128)(2,1)S(1)} collective-permute-done((bf16[400,128]{1,0:T(8,128)(2,1)S(1)}, bf16[400,128]{1,0:T(8,128)(2,1)S(1)}, u32[]{:S(2)}, u32[]{:S(2)}) %collective-permute-start.1) | collective-permute-done | bytes 102432 | tf_op jit(solution)/shard_map/ppermute | solution.py:277
  17.5 1.9 %collective-permute-done.2 = bf16[400,128]{1,0:T(8,128)(2,1)S(1)} collective-permute-done((bf16[400,128]{1,0:T(8,128)(2,1)S(1)}, bf16[400,128]{1,0:T(8,128)(2,1)S(1)}, u32[]{:S(2)}, u32[]{:S(2)}) %collective-permute-start.2) | collective-permute-done | bytes 102432 | tf_op jit(solution)/shard_map/ppermute | solution.py:277
  19.3 0.0 collective-permute-done.3
  19.3 0.1 add_convert_fusion.1.mine_ref
  19.4 2.7 %collective-permute-start.4 = (bf16[400,128]{1,0:T(8,128)(2,1)S(1)}, bf16[400,128]{1,0:T(8,128)(2,1)S(1)}, u32[]{:S(2)}, u32[]{:S(2)}) collective-permute-start(bf16[400,128]{1,0:T(8,128)(2,1)S(1)} %add_convert_fusion.1.mine_ref), channel_id=1, source_target_pairs={{0,8},{1,9},{2,10},{3,11},{4,12},{5,13},{6,14},{7,15},{8,0},{9,1},... | collective-permute-start | bytes 307208 | tf_op jit(solution)/shard_map/ppermute | solution.py:277
  22.1 4.6 %collective-permute-done.4.other_ref = bf16[400,128]{1,0:T(8,128)(2,1)S(1)} collective-permute-done((bf16[400,128]{1,0:T(8,128)(2,1)S(1)}, bf16[400,128]{1,0:T(8,128)(2,1)S(1)}, u32[]{:S(2)}, u32[]{:S(2)}) %collective-permute-start.4) | collective-permute-done | bytes 102432 | tf_op jit(solution)/shard_map/ppermute | solution.py:277
  26.7 0.3 nodes.1.refs_0_
  26.9 2.2 %collective-permute-start.5 = (bf16[64,768]{1,0:T(8,128)(2,1)S(1)}, bf16[64,768]{1,0:T(8,128)(2,1)S(1)}, u32[]{:S(2)}, u32[]{:S(2)}) collective-permute-start(bf16[64,768]{1,0:T(8,128)(2,1)S(1)} %nodes.1.refs_0_), channel_id=1, source_target_pairs={{0,2},{1,3},{2,0},{3,1},{4,6},{5,7},{6,4},{7,5},{8,10},{9,11},{10,... | collective-permute-start | bytes 294920 | tf_op jit(solution)/shard_map/ppermute | solution.py:277
  29.2 0.5 %collective-permute-start.6 = (bf16[64,768]{1,0:T(8,128)(2,1)S(1)}, bf16[64,768]{1,0:T(8,128)(2,1)S(1)}, u32[]{:S(2)}, u32[]{:S(2)}) collective-permute-start(bf16[64,768]{1,0:T(8,128)(2,1)S(1)} %nodes.1.refs_0_), channel_id=1, source_target_pairs={{0,4},{1,5},{2,6},{3,7},{4,0},{5,1},{6,2},{7,3},{8,12},{9,13},{10,... | collective-permute-start | bytes 294920 | tf_op jit(solution)/shard_map/ppermute | solution.py:277
  29.7 1.0 %collective-permute-start.7 = (bf16[64,768]{1,0:T(8,128)(2,1)S(1)}, bf16[64,768]{1,0:T(8,128)(2,1)S(1)}, u32[]{:S(2)}, u32[]{:S(2)}) collective-permute-start(bf16[64,768]{1,0:T(8,128)(2,1)S(1)} %nodes.1.refs_0_), channel_id=1, source_target_pairs={{0,6},{1,7},{2,4},{3,5},{4,2},{5,3},{6,0},{7,1},{8,14},{9,15},{10,... | collective-permute-start | bytes 294920 | tf_op jit(solution)/shard_map/ppermute | solution.py:277
  30.7 1.7 %collective-permute-done.5.refs_1_ = bf16[64,768]{1,0:T(8,128)(2,1)S(1)} collective-permute-done((bf16[64,768]{1,0:T(8,128)(2,1)S(1)}, bf16[64,768]{1,0:T(8,128)(2,1)S(1)}, u32[]{:S(2)}, u32[]{:S(2)}) %collective-permute-start.5) | collective-permute-done | bytes 98336 | tf_op jit(solution)/shard_map/ppermute | solution.py:277
  32.4 0.0 copy-start.3
  32.4 1.5 %collective-permute-done.6.refs_2_ = bf16[64,768]{1,0:T(8,128)(2,1)S(1)} collective-permute-done((bf16[64,768]{1,0:T(8,128)(2,1)S(1)}, bf16[64,768]{1,0:T(8,128)(2,1)S(1)}, u32[]{:S(2)}, u32[]{:S(2)}) %collective-permute-start.6) | collective-permute-done | bytes 98336 | tf_op jit(solution)/shard_map/ppermute | solution.py:277
  33.8 0.0 copy-start.5
  33.8 1.6 %collective-permute-done.7.refs_3_ = bf16[64,768]{1,0:T(8,128)(2,1)S(1)} collective-permute-done((bf16[64,768]{1,0:T(8,128)(2,1)S(1)}, bf16[64,768]{1,0:T(8,128)(2,1)S(1)}, u32[]{:S(2)}, u32[]{:S(2)}) %collective-permute-start.7) | collective-permute-done | bytes 98336 | tf_op jit(solution)/shard_map/ppermute | solution.py:277
  35.4 0.0 copy-start.7
  35.4 0.8 %pad_maximum_fusion = bf16[256,768]{1,0:T(8,128)(2,1)} fusion(bf16[64,768]{1,0:T(8,128)(2,1)S(1)} %collective-permute-done.7.refs_3_, bf16[64,768]{1,0:T(8,128)(2,1)S(1)} %collective-permute-done.6.refs_2_, bf16[64,768]{1,0:T(8,128)(2,1)S(1)} %collective-permute-done.5.refs_1_, bf16[64,768]{1,0:T(8,128)(2,1)S(1)} %nodes.1.refs_0_), kind=kLoop, calls=%fused_computation.1 | loop fusion | flops 1572864 | bytes 786432 | tf_op jit(solution)/shard_map/concatenate | solution.py:306
  36.2 0.0 copy-done.3
  36.2 0.0 copy-done.5
  36.2 0.0 copy-done.7
  36.2 0.0 copy-start.1
  36.2 0.6 %copy-done.1 = bf16[64,768]{1,0:T(8,128)(2,1)} copy-done((bf16[64,768]{1,0:T(8,128)(2,1)}, bf16[64,768]{1,0:T(8,128)(2,1)S(1)}, u32[]{:S(2)}) %copy-start.1) | copy-done | bytes 98328
  36.8 0.0 collective-permute-start.8
  36.8 0.0 copy-done.9
  36.9 2.0 %collective-permute-done.8.refs_4_ = bf16[256,768]{1,0:T(8,128)(2,1)} collective-permute-done((bf16[256,768]{1,0:T(8,128)(2,1)}, bf16[256,768]{1,0:T(8,128)(2,1)}, u32[]{:S(2)}, u32[]{:S(2)}) %collective-permute-start.8) | collective-permute-done | bytes 393248 | tf_op jit(solution)/shard_map/ppermute | solution.py:277
  38.9 0.0 copy-done
  38.9 0.0 copy-start.2
  38.9 0.9 %copy-done.2 = bf16[64,768]{1,0:T(8,128)(2,1)S(1)} copy-done((bf16[64,768]{1,0:T(8,128)(2,1)S(1)}, bf16[64,768]{1,0:T(8,128)(2,1)}, u32[]{:S(2)}) %copy-start.2) | copy-done | bytes 98328
  39.8 0.0 copy-start.4
  39.8 0.9 %copy-done.4 = bf16[64,768]{1,0:T(8,128)(2,1)S(1)} copy-done((bf16[64,768]{1,0:T(8,128)(2,1)S(1)}, bf16[64,768]{1,0:T(8,128)(2,1)}, u32[]{:S(2)}) %copy-start.4) | copy-done | bytes 98328
  40.7 0.0 copy-start.6
  40.7 0.9 %copy-done.6 = bf16[64,768]{1,0:T(8,128)(2,1)S(1)} copy-done((bf16[64,768]{1,0:T(8,128)(2,1)S(1)}, bf16[64,768]{1,0:T(8,128)(2,1)}, u32[]{:S(2)}) %copy-start.6) | copy-done | bytes 98328
  41.6 0.0 copy-start.8
  41.6 0.9 %copy-done.8 = bf16[64,768]{1,0:T(8,128)(2,1)S(1)} copy-done((bf16[64,768]{1,0:T(8,128)(2,1)S(1)}, bf16[64,768]{1,0:T(8,128)(2,1)}, u32[]{:S(2)}) %copy-start.8) | copy-done | bytes 98328
  42.5 4.8 %attention.1 = bf16[32,768]{1,0:T(8,128)(2,1)} custom-call(s32[1]{0:T(128)} %bitcast.first_ref, bf16[768,2304]{1,0:T(8,128)(2,1)S(1)} %copy-done, bf16[1,768]{1,0:T(2,128)(2,1)S(1)} %reshape.19.gain_ref, bf16[64,768]{1,0:T(8,128)(2,1)S(1)} %copy-done.2, bf16[64,768]{1,0:T(8,128)(2,1)S(1)} %copy-done.4, bf16[64,768]{1,0:T(8,128)(2,1)S(1)} %copy-done.6, ...), custom_call_target="tpu_custom_call" | custom-call | tf_op jit(solution)/shard_map/attention/pallas_call | solution.py:244
  (2 shorter events, 0.0 us)
Async XLA Ops:
  0.0 36.8 %copy-start.9 = (bf16[768]{0:T(1024)(128)(2,1)S(1)}, bf16[768]{0:T(1024)(128)(2,1)}, u32[]{:S(2)}) copy-start(bf16[768]{0:T(1024)(128)(2,1)} %param.15) | copy-start | bytes 4612
  0.0 38.9 %copy-start = (bf16[768,2304]{1,0:T(8,128)(2,1)S(1)}, bf16[768,2304]{1,0:T(8,128)(2,1)}, u32[]{:S(2)}) copy-start(bf16[768,2304]{1,0:T(8,128)(2,1)} %proj_ref.1) | copy-start | bytes 10616836
  7.8 1.9 %collective-permute-start = (bf16[1600,128]{1,0:T(8,128)(2,1)S(1)}, bf16[1600,128]{1,0:T(8,128)(2,1)S(1)}, u32[]{:S(2)}, u32[]{:S(2)}) collective-permute-start(bf16[1600,128]{1,0:T(8,128)(2,1)S(1)} %get-tuple-element.8), channel_id=1, source_target_pairs={{0,1},{1,0},{2,3},{3,2},{4,5},{5,4},{6,7},{7,6},{8,9},{9,8},{10,11... | collective-permute-start | bytes 1228808 | tf_op jit(solution)/shard_map/ppermute | solution.py:277
  9.8 7.6 %collective-permute-start.1 = (bf16[400,128]{1,0:T(8,128)(2,1)S(1)}, bf16[400,128]{1,0:T(8,128)(2,1)S(1)}, u32[]{:S(2)}, u32[]{:S(2)}) collective-permute-start(bf16[400,128]{1,0:T(8,128)(2,1)S(1)} %get-tuple-element.9), channel_id=1, source_target_pairs={{0,6},{1,7},{2,4},{3,5},{4,2},{5,3},{6,0},{7,1},{8,14},{9,15},{10,... | collective-permute-start | bytes 307208 | tf_op jit(solution)/shard_map/ppermute | solution.py:277
  13.8 5.5 %collective-permute-start.2 = (bf16[400,128]{1,0:T(8,128)(2,1)S(1)}, bf16[400,128]{1,0:T(8,128)(2,1)S(1)}, u32[]{:S(2)}, u32[]{:S(2)}) collective-permute-start(bf16[400,128]{1,0:T(8,128)(2,1)S(1)} %get-tuple-element.11), channel_id=1, source_target_pairs={{0,4},{1,5},{2,6},{3,7},{4,0},{5,1},{6,2},{7,3},{8,12},{9,13},{10,... | collective-permute-start | bytes 307208 | tf_op jit(solution)/shard_map/ppermute | solution.py:277
  14.2 5.1 %collective-permute-start.3 = (bf16[400,128]{1,0:T(8,128)(2,1)S(1)}, bf16[400,128]{1,0:T(8,128)(2,1)S(1)}, u32[]{:S(2)}, u32[]{:S(2)}) collective-permute-start(bf16[400,128]{1,0:T(8,128)(2,1)S(1)} %get-tuple-element.10), channel_id=1, source_target_pairs={{0,2},{1,3},{2,0},{3,1},{4,6},{5,7},{6,4},{7,5},{8,10},{9,11},{10,... | collective-permute-start | bytes 307208 | tf_op jit(solution)/shard_map/ppermute | solution.py:277
  19.4 7.3 %collective-permute-start.4 = (bf16[400,128]{1,0:T(8,128)(2,1)S(1)}, bf16[400,128]{1,0:T(8,128)(2,1)S(1)}, u32[]{:S(2)}, u32[]{:S(2)}) collective-permute-start(bf16[400,128]{1,0:T(8,128)(2,1)S(1)} %add_convert_fusion.1.mine_ref), channel_id=1, source_target_pairs={{0,8},{1,9},{2,10},{3,11},{4,12},{5,13},{6,14},{7,15},{8,0},{9,1},... | collective-permute-start | bytes 307208 | tf_op jit(solution)/shard_map/ppermute | solution.py:277
  26.9 5.4 %collective-permute-start.5 = (bf16[64,768]{1,0:T(8,128)(2,1)S(1)}, bf16[64,768]{1,0:T(8,128)(2,1)S(1)}, u32[]{:S(2)}, u32[]{:S(2)}) collective-permute-start(bf16[64,768]{1,0:T(8,128)(2,1)S(1)} %nodes.1.refs_0_), channel_id=1, source_target_pairs={{0,2},{1,3},{2,0},{3,1},{4,6},{5,7},{6,4},{7,5},{8,10},{9,11},{10,... | collective-permute-start | bytes 294920 | tf_op jit(solution)/shard_map/ppermute | solution.py:277
  29.2 4.7 %collective-permute-start.6 = (bf16[64,768]{1,0:T(8,128)(2,1)S(1)}, bf16[64,768]{1,0:T(8,128)(2,1)S(1)}, u32[]{:S(2)}, u32[]{:S(2)}) collective-permute-start(bf16[64,768]{1,0:T(8,128)(2,1)S(1)} %nodes.1.refs_0_), channel_id=1, source_target_pairs={{0,4},{1,5},{2,6},{3,7},{4,0},{5,1},{6,2},{7,3},{8,12},{9,13},{10,... | collective-permute-start | bytes 294920 | tf_op jit(solution)/shard_map/ppermute | solution.py:277
  29.7 5.7 %collective-permute-start.7 = (bf16[64,768]{1,0:T(8,128)(2,1)S(1)}, bf16[64,768]{1,0:T(8,128)(2,1)S(1)}, u32[]{:S(2)}, u32[]{:S(2)}) collective-permute-start(bf16[64,768]{1,0:T(8,128)(2,1)S(1)} %nodes.1.refs_0_), channel_id=1, source_target_pairs={{0,6},{1,7},{2,4},{3,5},{4,2},{5,3},{6,0},{7,1},{8,14},{9,15},{10,... | collective-permute-start | bytes 294920 | tf_op jit(solution)/shard_map/ppermute | solution.py:277
  32.4 3.8 %copy-start.3 = (bf16[64,768]{1,0:T(8,128)(2,1)}, bf16[64,768]{1,0:T(8,128)(2,1)S(1)}, u32[]{:S(2)}) copy-start(bf16[64,768]{1,0:T(8,128)(2,1)S(1)} %collective-permute-done.5.refs_1_) | copy-start | bytes 294916
  33.8 2.3 %copy-start.5 = (bf16[64,768]{1,0:T(8,128)(2,1)}, bf16[64,768]{1,0:T(8,128)(2,1)S(1)}, u32[]{:S(2)}) copy-start(bf16[64,768]{1,0:T(8,128)(2,1)S(1)} %collective-permute-done.6.refs_2_) | copy-start | bytes 294916
  35.4 0.8 %copy-start.7 = (bf16[64,768]{1,0:T(8,128)(2,1)}, bf16[64,768]{1,0:T(8,128)(2,1)S(1)}, u32[]{:S(2)}) copy-start(bf16[64,768]{1,0:T(8,128)(2,1)S(1)} %collective-permute-done.7.refs_3_) | copy-start | bytes 294916
  36.2 0.6 %copy-start.1 = (bf16[64,768]{1,0:T(8,128)(2,1)}, bf16[64,768]{1,0:T(8,128)(2,1)S(1)}, u32[]{:S(2)}) copy-start(bf16[64,768]{1,0:T(8,128)(2,1)S(1)} %nodes.1.refs_0_) | copy-start | bytes 294916
  36.8 2.1 %collective-permute-start.8 = (bf16[256,768]{1,0:T(8,128)(2,1)}, bf16[256,768]{1,0:T(8,128)(2,1)}, u32[]{:S(2)}, u32[]{:S(2)}) collective-permute-start(bf16[256,768]{1,0:T(8,128)(2,1)} %pad_maximum_fusion), channel_id=1, source_target_pairs={{0,1},{1,0},{2,3},{3,2},{4,5},{5,4},{6,7},{7,6},{8,9},{9,8},{10,11... | collective-permute-start | bytes 1179656 | tf_op jit(solution)/shard_map/ppermute | solution.py:277
  38.9 0.9 %copy-start.2 = (bf16[64,768]{1,0:T(8,128)(2,1)S(1)}, bf16[64,768]{1,0:T(8,128)(2,1)}, u32[]{:S(2)}) copy-start(bf16[64,768]{1,0:T(8,128)(2,1)} %copy-done.1) | copy-start | bytes 294916
  39.8 0.9 %copy-start.4 = (bf16[64,768]{1,0:T(8,128)(2,1)S(1)}, bf16[64,768]{1,0:T(8,128)(2,1)}, u32[]{:S(2)}) copy-start(bf16[64,768]{1,0:T(8,128)(2,1)} %copy-done.3) | copy-start | bytes 294916
  40.7 0.9 %copy-start.6 = (bf16[64,768]{1,0:T(8,128)(2,1)S(1)}, bf16[64,768]{1,0:T(8,128)(2,1)}, u32[]{:S(2)}) copy-start(bf16[64,768]{1,0:T(8,128)(2,1)} %copy-done.5) | copy-start | bytes 294916
  41.6 0.9 %copy-start.8 = (bf16[64,768]{1,0:T(8,128)(2,1)S(1)}, bf16[64,768]{1,0:T(8,128)(2,1)}, u32[]{:S(2)}) copy-start(bf16[64,768]{1,0:T(8,128)(2,1)} %copy-done.7) | copy-start | bytes 294916

commit v3 on v2

--- a/solution.py
+++ b/solution.py
@@ -193,26 +193,66 @@
         out_shape=pltpu.VMEM((GROUP_ROWS, D), jnp.bfloat16),
         compiler_params=pltpu.CompilerParams(vmem_limit_bytes=8 * MIB),
         name="nodes",
-    )(mine, other)
-
-
-def attention_kernel(first_ref, proj_ref, gain_ref, *refs):
-    *pieces, out_ref, nodes_ref = refs
-    first = pl.multiple_of(first_ref[0], S_DEV)
-    queries = jnp.dot(
-        pieces[0][pl.ds(first, S_DEV), :], proj_ref[:, :D], preferred_element_type=jnp.float32
-    ).astype(jnp.bfloat16)
+    )(*in_vmem(mine, other))
+
+
+def in_vmem(*arrays):
+    return [pltpu.with_memory_space_constraint(array, pltpu.VMEM) for array in arrays]
+
+
+def join_kernel(*refs):
+    *pieces, out_ref = refs
     start = 0
     for piece in pieces:
-        nodes_ref[start : start + piece.shape[0], :] = piece[...]
+        out_ref[start : start + piece.shape[0], :] = piece[...]
         start += piece.shape[0]
-    nodes = nodes_ref[...]
-    keys = jnp.dot(nodes, proj_ref[:, D : 2 * D], preferred_element_type=jnp.float32).astype(
-        jnp.bfloat16
-    )
-    values = jnp.dot(nodes, proj_ref[:, 2 * D :], preferred_element_type=jnp.float32).astype(
-        jnp.bfloat16
-    )
+
+
+def run_join(pieces):
+    rows = sum(piece.shape[0] for piece in pieces)
+    return pl.pallas_call(
+        join_kernel,
+        out_shape=pltpu.VMEM((rows, D), jnp.bfloat16),
+        compiler_params=pltpu.CompilerParams(vmem_limit_bytes=8 * MIB),
+        name="join",
+    )(*in_vmem(*pieces))
+
+
+def project(rows, proj_ref, start, size):
+    return jnp.dot(
+        rows, proj_ref[:, start : start + size], preferred_element_type=jnp.float32
+    ).astype(jnp.bfloat16)
+
+
+def project_kernel(first_ref, nodes_ref, proj_ref, query_ref, key_value_ref):
+    first = pl.multiple_of(first_ref[0], S_DEV)
+    query_ref[...] = project(nodes_ref[pl.ds(first, S_DEV), :], proj_ref, 0, D)
+    key_value_ref[...] = project(nodes_ref[...], proj_ref, D, 2 * D)
+
+
+def run_project(first, nodes, proj_weight):
+    rows = nodes.shape[0]
+    return pl.pallas_call(
+        project_kernel,
+        in_specs=[pl.BlockSpec(memory_space=pltpu.SMEM)]
+        + [pl.BlockSpec(memory_space=pltpu.VMEM)] * 2,
+        out_shape=[
+            pltpu.VMEM((S_DEV, D), jnp.bfloat16),
+            pltpu.VMEM((rows, 2 * D), jnp.bfloat16),
+        ],
+        compiler_params=pltpu.CompilerParams(vmem_limit_bytes=8 * MIB + 16 * rows * D),
+        cost_estimate=pl.CostEstimate(
+            flops=4 * rows * D * D, bytes_accessed=6 * D * D + 6 * rows * D, transcendentals=0
+        ),
+        name="project",
+    )(first, *in_vmem(nodes, proj_weight))
+
+
+def attention_kernel(query_ref, near_ref, nodes_ref, proj_ref, gain_ref, out_ref):
+    far = project(nodes_ref[...], proj_ref, D, 2 * D)
+    keys = jnp.concatenate([near_ref[:, :D], far[:, :D]], axis=0)
+    values = jnp.concatenate([near_ref[:, D:], far[:, D:]], axis=0)
+    queries = query_ref[...]
     lane = lax.broadcasted_iota(jnp.int32, (S_DEV, LANES), 1)
     low = lane < DH
     heads = []
@@ -238,18 +278,14 @@
     out_ref[...] = (attended * scale * gain_ref[...].astype(jnp.float32)).astype(jnp.bfloat16)
 
 
-def run_attention(first, proj_weight, gain, pieces):
-    vmem = pl.BlockSpec(memory_space=pltpu.VMEM)
-    nodes = sum(piece.shape[0] for piece in pieces)
+def run_attention(query, near, nodes, proj_weight, gain):
+    rows = nodes.shape[0]
     return pl.pallas_call(
         attention_kernel,
-        in_specs=[pl.BlockSpec(memory_space=pltpu.SMEM)] + [vmem] * (2 + len(pieces)),
-        out_specs=vmem,
         out_shape=jax.ShapeDtypeStruct((S_DEV, D), jnp.bfloat16),
-        scratch_shapes=[pltpu.VMEM((nodes, D), jnp.bfloat16)],
-        compiler_params=pltpu.CompilerParams(vmem_limit_bytes=16 * MIB + 6 * nodes * D),
+        compiler_params=pltpu.CompilerParams(vmem_limit_bytes=16 * MIB + 16 * rows * D),
         name="attention",
-    )(first, proj_weight, gain, *pieces)
+    )(*in_vmem(query, near, nodes, proj_weight), gain)
 
 
 def add_up(first, *rest):
@@ -299,13 +335,12 @@
         order = list(range(1, 1 << take))[::-1]
         table = add_up(parts[0], *[swap(parts[j], j << (width + 1)) for j in order])
     nodes = run_nodes(devices, rows, table, swap(table, devices // 2))
-    pieces = [nodes]
     for take, width in groups[::-1]:
-        nodes = jnp.concatenate(pieces, axis=0)
-        pieces = [nodes] + [swap(nodes, j << (width + 1)) for j in range(1, 1 << take)]
-    pieces.append(swap(jnp.concatenate(pieces, axis=0), 1))
+        nodes = run_join([nodes] + [swap(nodes, j << (width + 1)) for j in range(1, 1 << take)])
+    other = swap(nodes, 1)
     first = (me // (devices // 2) * S_DEV).reshape(1)
-    return run_attention(first, proj_weight, final_gain.reshape(1, D), pieces)
+    query, near = run_project(first, nodes, proj_weight)
+    return run_attention(query, near, other, proj_weight, final_gain.reshape(1, D))
 
 
 def solution(mesh):

time: 47.5 us -> 41.8 us (0.88)
  local copies, waits for them, and re-layouts: 4.25 us -> 0.03 us
  waiting for transfers between devices: 17.6 us -> 15.3 us
  Pallas kernels: 12.8 us -> 14.7 us
  other arithmetic: 0.95 us -> 0.17 us
    unnamed x20 -> x4, local copies, waits for them, and re-layouts: 4.22 us -> 0.01 us
    ppermute x9, waiting for transfers between devices: 17.6 us -> 15.3 us  [swap(): return lax.ppermute(array, 'blk', [(i, i ^ flip) for i in range(devices)])]
    pallas_call x1 -> x3, Pallas kernels: 4.77 us -> 6.7 us  [the longest x1 3.98 us: run_attention(): pl.pallas_call(attention_kernel, out_shape=jax.ShapeDtypeStruct((S_DEV, D...]
    concatenate x1 -> x0, other arithmetic: 0.78 us -> none  [body(): pieces.append(swap(jnp.concatenate(pieces, axis=0), 1))]
  transfers between devices with their start and end apart: 9 -> 9, of which waited for: 8 -> 9; matrix products, arithmetic and copies ran while one was open for 0% -> 0% of each run, Pallas kernels for 0% -> 5%
where the time goes in v3:
time: 41.8 us; the launch traced here: 41.6 us
  waiting for transfers between devices  15.3 us (37%)
  Pallas kernels  14.7 us (35%)
  starting transfers between devices  11.3 us (27%)
    ppermute x9, waiting for transfers between devices, swap(): return lax.ppermute(array, 'blk', [(i, i ^ flip) for i in range(devices)])  15.3 us
    ppermute x9, starting transfers between devices, swap(): return lax.ppermute(array, 'blk', [(i, i ^ flip) for i in range(devices)])  11.3 us
    pallas_call x1, Pallas kernels, run_points(): pl.pallas_call(functools.partial(points_kernel, devices), in_specs=[pl.Bl...  7.78 us
    pallas_call x1, Pallas kernels, run_attention(): pl.pallas_call(attention_kernel, out_shape=jax.ShapeDtypeStruct((S_DEV, D...  3.98 us
    pallas_call x1, Pallas kernels, run_project(): pl.pallas_call(project_kernel, in_specs=[pl.BlockSpec(memory_space=pltpu....  1.95 us
  transfers between devices with their start and end apart: 9, of which 9 were waited for; matrix products, arithmetic and copies ran while one was open for 0% of the time, Pallas kernels for 5%

profile of v3, /device:TPU:0, one launch (start us, length us, event | category | flops | bytes accessed | tf_op | source)
XLA Modules:
  0.0 41.6 jit_solution(3972295097078703366)
XLA Ops:
  0.0 0.0 copy-start.1
  0.0 0.0 copy-start
  0.0 7.8 %points.1 = (bf16[1600,128]{1,0:T(8,128)(2,1)S(1)}, bf16[1600,128]{1,0:T(8,128)(2,1)S(1)}) custom-call(s32[1]{0:T(128)} %bitcast.1.me_ref, bf16[512,768]{1,0:T(8,128)(2,1)} %x_hbm.1, bf16[768,2560]{1,0:T(8,128)(2,1)} %hidden_hbm.1, bf16[2560,768]{1,0:T(8,128)(2,1)} %output_hbm.1, s32[1,512]{1,0:T(1,128)} %bitcast.5, s32[1,512]{1,0:T(1,128)} %bitcast.6, ...), custom_call_target="tpu_custom_call" | custom-call | tf_op jit(solution)/shard_map/points/pallas_call | solution.py:143
  7.8 0.5 %collective-permute-start = (bf16[1600,128]{1,0:T(8,128)(2,1)S(1)}, bf16[1600,128]{1,0:T(8,128)(2,1)S(1)}, u32[]{:S(2)}, u32[]{:S(2)}) collective-permute-start(bf16[1600,128]{1,0:T(8,128)(2,1)S(1)} %get-tuple-element.10), channel_id=1, source_target_pairs={{0,1},{1,0},{2,3},{3,2},{4,5},{5,4},{6,7},{7,6},{8,9},{9,8},{10,11... | collective-permute-start | bytes 1228808 | tf_op jit(solution)/shard_map/ppermute | solution.py:313
  8.3 1.4 %collective-permute-done = bf16[1600,128]{1,0:T(8,128)(2,1)S(1)} collective-permute-done((bf16[1600,128]{1,0:T(8,128)(2,1)S(1)}, bf16[1600,128]{1,0:T(8,128)(2,1)S(1)}, u32[]{:S(2)}, u32[]{:S(2)}) %collective-permute-start) | collective-permute-done | bytes 409632 | tf_op jit(solution)/shard_map/ppermute | solution.py:313
  9.7 0.1 add_convert_fusion
  9.8 4.0 %collective-permute-start.1 = (bf16[400,128]{1,0:T(8,128)(2,1)S(1)}, bf16[400,128]{1,0:T(8,128)(2,1)S(1)}, u32[]{:S(2)}, u32[]{:S(2)}) collective-permute-start(bf16[400,128]{1,0:T(8,128)(2,1)S(1)} %get-tuple-element.13), channel_id=1, source_target_pairs={{0,6},{1,7},{2,4},{3,5},{4,2},{5,3},{6,0},{7,1},{8,14},{9,15},{10,... | collective-permute-start | bytes 307208 | tf_op jit(solution)/shard_map/ppermute | solution.py:313
  13.8 0.5 %collective-permute-start.3 = (bf16[400,128]{1,0:T(8,128)(2,1)S(1)}, bf16[400,128]{1,0:T(8,128)(2,1)S(1)}, u32[]{:S(2)}, u32[]{:S(2)}) collective-permute-start(bf16[400,128]{1,0:T(8,128)(2,1)S(1)} %get-tuple-element.14), channel_id=1, source_target_pairs={{0,2},{1,3},{2,0},{3,1},{4,6},{5,7},{6,4},{7,5},{8,10},{9,11},{10,... | collective-permute-start | bytes 307208 | tf_op jit(solution)/shard_map/ppermute | solution.py:313
  14.3 0.1 collective-permute-start.2
  14.4 2.6 %collective-permute-done.1 = bf16[400,128]{1,0:T(8,128)(2,1)S(1)} collective-permute-done((bf16[400,128]{1,0:T(8,128)(2,1)S(1)}, bf16[400,128]{1,0:T(8,128)(2,1)S(1)}, u32[]{:S(2)}, u32[]{:S(2)}) %collective-permute-start.1) | collective-permute-done | bytes 102432 | tf_op jit(solution)/shard_map/ppermute | solution.py:313
  17.1 2.1 %collective-permute-done.3 = bf16[400,128]{1,0:T(8,128)(2,1)S(1)} collective-permute-done((bf16[400,128]{1,0:T(8,128)(2,1)S(1)}, bf16[400,128]{1,0:T(8,128)(2,1)S(1)}, u32[]{:S(2)}, u32[]{:S(2)}) %collective-permute-start.3) | collective-permute-done | bytes 102432 | tf_op jit(solution)/shard_map/ppermute | solution.py:313
  19.2 0.2 collective-permute-done.2
  19.3 0.1 add_convert_fusion.1.mine_ref
  19.4 2.7 %collective-permute-start.4 = (bf16[400,128]{1,0:T(8,128)(2,1)S(1)}, bf16[400,128]{1,0:T(8,128)(2,1)S(1)}, u32[]{:S(2)}, u32[]{:S(2)}) collective-permute-start(bf16[400,128]{1,0:T(8,128)(2,1)S(1)} %add_convert_fusion.1.mine_ref), channel_id=1, source_target_pairs={{0,8},{1,9},{2,10},{3,11},{4,12},{5,13},{6,14},{7,15},{8,0},{9,1},... | collective-permute-start | bytes 307208 | tf_op jit(solution)/shard_map/ppermute | solution.py:313
  22.0 5.2 %collective-permute-done.4.other_ref = bf16[400,128]{1,0:T(8,128)(2,1)S(1)} collective-permute-done((bf16[400,128]{1,0:T(8,128)(2,1)S(1)}, bf16[400,128]{1,0:T(8,128)(2,1)S(1)}, u32[]{:S(2)}, u32[]{:S(2)}) %collective-permute-start.4) | collective-permute-done | bytes 102432 | tf_op jit(solution)/shard_map/ppermute | solution.py:313
  27.2 0.3 nodes.1.refs_0_
  27.5 0.7 %collective-permute-start.7 = (bf16[64,768]{1,0:T(8,128)(2,1)S(1)}, bf16[64,768]{1,0:T(8,128)(2,1)S(1)}, u32[]{:S(2)}, u32[]{:S(2)}) collective-permute-start(bf16[64,768]{1,0:T(8,128)(2,1)S(1)} %nodes.1.refs_0_), channel_id=1, source_target_pairs={{0,6},{1,7},{2,4},{3,5},{4,2},{5,3},{6,0},{7,1},{8,14},{9,15},{10,... | collective-permute-start | bytes 294920 | tf_op jit(solution)/shard_map/ppermute | solution.py:313
  28.2 1.8 %collective-permute-start.6 = (bf16[64,768]{1,0:T(8,128)(2,1)S(1)}, bf16[64,768]{1,0:T(8,128)(2,1)S(1)}, u32[]{:S(2)}, u32[]{:S(2)}) collective-permute-start(bf16[64,768]{1,0:T(8,128)(2,1)S(1)} %nodes.1.refs_0_), channel_id=1, source_target_pairs={{0,4},{1,5},{2,6},{3,7},{4,0},{5,1},{6,2},{7,3},{8,12},{9,13},{10,... | collective-permute-start | bytes 294920 | tf_op jit(solution)/shard_map/ppermute | solution.py:313
  30.0 1.0 %collective-permute-start.5 = (bf16[64,768]{1,0:T(8,128)(2,1)S(1)}, bf16[64,768]{1,0:T(8,128)(2,1)S(1)}, u32[]{:S(2)}, u32[]{:S(2)}) collective-permute-start(bf16[64,768]{1,0:T(8,128)(2,1)S(1)} %nodes.1.refs_0_), channel_id=1, source_target_pairs={{0,2},{1,3},{2,0},{3,1},{4,6},{5,7},{6,4},{7,5},{8,10},{9,11},{10,... | collective-permute-start | bytes 294920 | tf_op jit(solution)/shard_map/ppermute | solution.py:313
  31.1 2.5 %collective-permute-done.7.refs_3_ = bf16[64,768]{1,0:T(8,128)(2,1)S(1)} collective-permute-done((bf16[64,768]{1,0:T(8,128)(2,1)S(1)}, bf16[64,768]{1,0:T(8,128)(2,1)S(1)}, u32[]{:S(2)}, u32[]{:S(2)}) %collective-permute-start.7) | collective-permute-done | bytes 98336 | tf_op jit(solution)/shard_map/ppermute | solution.py:313
  33.5 0.9 %collective-permute-done.6.refs_2_ = bf16[64,768]{1,0:T(8,128)(2,1)S(1)} collective-permute-done((bf16[64,768]{1,0:T(8,128)(2,1)S(1)}, bf16[64,768]{1,0:T(8,128)(2,1)S(1)}, u32[]{:S(2)}, u32[]{:S(2)}) %collective-permute-start.6) | collective-permute-done | bytes 98336 | tf_op jit(solution)/shard_map/ppermute | solution.py:313
  34.4 0.4 collective-permute-done.5.refs_1_
  34.8 0.8 %join.1.nodes_ref = bf16[256,768]{1,0:T(8,128)(2,1)} custom-call(bf16[64,768]{1,0:T(8,128)(2,1)S(1)} %nodes.1.refs_0_, bf16[64,768]{1,0:T(8,128)(2,1)S(1)} %collective-permute-done.5.refs_1_, bf16[64,768]{1,0:T(8,128)(2,1)S(1)} %collective-permute-done.6.refs_2_, bf16[64,768]{1,0:T(8,128)(2,1)S(1)} %collective-permute-done.7.refs_3_), custom_call_target="tpu_custom_call" | custom-call | tf_op jit(solution)/shard_map/join/pallas_call | solution.py:213
  35.6 0.0 collective-permute-start.8
  35.6 0.0 copy-done.1
  35.6 0.0 copy-done
  35.6 2.0 %project.1 = (bf16[32,768]{1,0:T(8,128)(2,1)S(1)}, bf16[256,1536]{1,0:T(8,128)(2,1)S(1)}) custom-call(s32[1]{0:T(128)} %bitcast.first_ref, bf16[256,768]{1,0:T(8,128)(2,1)} %join.1.nodes_ref, bf16[768,2304]{1,0:T(8,128)(2,1)S(1)} %copy-done), custom_call_target="tpu_custom_call" | custom-call | flops 603979776 | bytes 4718592 | tf_op jit(solution)/shard_map/project/pallas_call | solution.py:235
  37.6 0.1 collective-permute-done.8.nodes_ref
  37.7 4.0 %attention.1 = bf16[32,768]{1,0:T(8,128)(2,1)} custom-call(bf16[32,768]{1,0:T(8,128)(2,1)S(1)} %get-tuple-element.11.query_ref, bf16[256,1536]{1,0:T(8,128)(2,1)S(1)} %get-tuple-element.12.near_ref, bf16[256,768]{1,0:T(8,128)(2,1)} %collective-permute-done.8.nodes_ref, bf16[768,2304]{1,0:T(8,128)(2,1)S(1)} %copy-done, bf16[1,768]{1,0:T(2,128)(2,1)S(1)} %reshape.23.gain_ref), custom_call_target="tpu_custom_call" | custom-call | tf_op jit(solution)/shard_map/attention/pallas_call | solution.py:283
  (2 shorter events, 0.0 us)
Async XLA Ops:
  0.0 35.6 %copy-start.1 = (bf16[768]{0:T(1024)(128)(2,1)S(1)}, bf16[768]{0:T(1024)(128)(2,1)}, u32[]{:S(2)}) copy-start(bf16[768]{0:T(1024)(128)(2,1)} %param.15) | copy-start | bytes 4612
  0.0 35.6 %copy-start = (bf16[768,2304]{1,0:T(8,128)(2,1)S(1)}, bf16[768,2304]{1,0:T(8,128)(2,1)}, u32[]{:S(2)}) copy-start(bf16[768,2304]{1,0:T(8,128)(2,1)} %proj_ref.3) | copy-start | bytes 10616836
  7.8 1.9 %collective-permute-start = (bf16[1600,128]{1,0:T(8,128)(2,1)S(1)}, bf16[1600,128]{1,0:T(8,128)(2,1)S(1)}, u32[]{:S(2)}, u32[]{:S(2)}) collective-permute-start(bf16[1600,128]{1,0:T(8,128)(2,1)S(1)} %get-tuple-element.10), channel_id=1, source_target_pairs={{0,1},{1,0},{2,3},{3,2},{4,5},{5,4},{6,7},{7,6},{8,9},{9,8},{10,11... | collective-permute-start | bytes 1228808 | tf_op jit(solution)/shard_map/ppermute | solution.py:313
  9.8 7.3 %collective-permute-start.1 = (bf16[400,128]{1,0:T(8,128)(2,1)S(1)}, bf16[400,128]{1,0:T(8,128)(2,1)S(1)}, u32[]{:S(2)}, u32[]{:S(2)}) collective-permute-start(bf16[400,128]{1,0:T(8,128)(2,1)S(1)} %get-tuple-element.13), channel_id=1, source_target_pairs={{0,6},{1,7},{2,4},{3,5},{4,2},{5,3},{6,0},{7,1},{8,14},{9,15},{10,... | collective-permute-start | bytes 307208 | tf_op jit(solution)/shard_map/ppermute | solution.py:313
  13.8 5.4 %collective-permute-start.3 = (bf16[400,128]{1,0:T(8,128)(2,1)S(1)}, bf16[400,128]{1,0:T(8,128)(2,1)S(1)}, u32[]{:S(2)}, u32[]{:S(2)}) collective-permute-start(bf16[400,128]{1,0:T(8,128)(2,1)S(1)} %get-tuple-element.14), channel_id=1, source_target_pairs={{0,2},{1,3},{2,0},{3,1},{4,6},{5,7},{6,4},{7,5},{8,10},{9,11},{10,... | collective-permute-start | bytes 307208 | tf_op jit(solution)/shard_map/ppermute | solution.py:313
  14.3 5.0 %collective-permute-start.2 = (bf16[400,128]{1,0:T(8,128)(2,1)S(1)}, bf16[400,128]{1,0:T(8,128)(2,1)S(1)}, u32[]{:S(2)}, u32[]{:S(2)}) collective-permute-start(bf16[400,128]{1,0:T(8,128)(2,1)S(1)} %get-tuple-element.15), channel_id=1, source_target_pairs={{0,4},{1,5},{2,6},{3,7},{4,0},{5,1},{6,2},{7,3},{8,12},{9,13},{10,... | collective-permute-start | bytes 307208 | tf_op jit(solution)/shard_map/ppermute | solution.py:313
  19.4 7.8 %collective-permute-start.4 = (bf16[400,128]{1,0:T(8,128)(2,1)S(1)}, bf16[400,128]{1,0:T(8,128)(2,1)S(1)}, u32[]{:S(2)}, u32[]{:S(2)}) collective-permute-start(bf16[400,128]{1,0:T(8,128)(2,1)S(1)} %add_convert_fusion.1.mine_ref), channel_id=1, source_target_pairs={{0,8},{1,9},{2,10},{3,11},{4,12},{5,13},{6,14},{7,15},{8,0},{9,1},... | collective-permute-start | bytes 307208 | tf_op jit(solution)/shard_map/ppermute | solution.py:313
  27.5 6.0 %collective-permute-start.7 = (bf16[64,768]{1,0:T(8,128)(2,1)S(1)}, bf16[64,768]{1,0:T(8,128)(2,1)S(1)}, u32[]{:S(2)}, u32[]{:S(2)}) collective-permute-start(bf16[64,768]{1,0:T(8,128)(2,1)S(1)} %nodes.1.refs_0_), channel_id=1, source_target_pairs={{0,6},{1,7},{2,4},{3,5},{4,2},{5,3},{6,0},{7,1},{8,14},{9,15},{10,... | collective-permute-start | bytes 294920 | tf_op jit(solution)/shard_map/ppermute | solution.py:313
  28.2 6.2 %collective-permute-start.6 = (bf16[64,768]{1,0:T(8,128)(2,1)S(1)}, bf16[64,768]{1,0:T(8,128)(2,1)S(1)}, u32[]{:S(2)}, u32[]{:S(2)}) collective-permute-start(bf16[64,768]{1,0:T(8,128)(2,1)S(1)} %nodes.1.refs_0_), channel_id=1, source_target_pairs={{0,4},{1,5},{2,6},{3,7},{4,0},{5,1},{6,2},{7,3},{8,12},{9,13},{10,... | collective-permute-start | bytes 294920 | tf_op jit(solution)/shard_map/ppermute | solution.py:313
  30.0 4.8 %collective-permute-start.5 = (bf16[64,768]{1,0:T(8,128)(2,1)S(1)}, bf16[64,768]{1,0:T(8,128)(2,1)S(1)}, u32[]{:S(2)}, u32[]{:S(2)}) collective-permute-start(bf16[64,768]{1,0:T(8,128)(2,1)S(1)} %nodes.1.refs_0_), channel_id=1, source_target_pairs={{0,2},{1,3},{2,0},{3,1},{4,6},{5,7},{6,4},{7,5},{8,10},{9,11},{10,... | collective-permute-start | bytes 294920 | tf_op jit(solution)/shard_map/ppermute | solution.py:313
  35.6 2.1 %collective-permute-start.8 = (bf16[256,768]{1,0:T(8,128)(2,1)}, bf16[256,768]{1,0:T(8,128)(2,1)}, u32[]{:S(2)}, u32[]{:S(2)}) collective-permute-start(bf16[256,768]{1,0:T(8,128)(2,1)} %join.1.nodes_ref), channel_id=1, source_target_pairs={{0,1},{1,0},{2,3},{3,2},{4,5},{5,4},{6,7},{7,6},{8,9},{9,8},{10,11... | collective-permute-start | bytes 1179656 | tf_op jit(solution)/shard_map/ppermute | solution.py:313

commit v4 on v2

--- a/solution.py
+++ b/solution.py
@@ -32,8 +32,9 @@
     return 0.5 * values * (1.0 + lax.erf(values * 0.7071067811865476))
 
 
-def hidden_cols(ff):
-    return 512 if ff % 512 == 0 else ff
+def hidden_parts(ff):
+    stops = [stop for stop in (256, 1024) if stop < ff] + [ff]
+    return [slice(start, stop) for start, stop in zip([0] + stops[:-1], stops)]
 
 
 def points_kernel(
@@ -42,16 +43,16 @@
 ):
     rows = x_ref.shape[0]
     ff = hidden_ref.shape[1]
-    cols = hidden_cols(ff)
+    parts = hidden_parts(ff)
 
     def hidden_copy(part):
-        at = pl.ds(pl.multiple_of(part * cols, cols), cols)
+        at = parts[part]
         return pltpu.make_async_copy(hidden_hbm.at[:, at], hidden_ref.at[:, at], sems.at[2 + part])
 
     x_copy = pltpu.make_async_copy(x_hbm, x_ref, sems.at[0])
     output_copy = pltpu.make_async_copy(output_hbm, output_ref, sems.at[1])
     index_copies = [
-        pltpu.make_async_copy(source, target, sems.at[2 + ff // cols + i])
+        pltpu.make_async_copy(source, target, sems.at[2 + len(parts) + i])
         for i, (source, target) in enumerate(
             ((owner_hbm, owner_ref), (node_hbm, node_ref), (weight_hbm, weight_ref))
         )
@@ -59,7 +60,7 @@
     for copy in index_copies:
         copy.start()
     x_copy.start()
-    for part in range(ff // cols):
+    for part in range(len(parts)):
         hidden_copy(part).start()
     output_copy.start()
 
@@ -106,15 +107,18 @@
     scale = lax.rsqrt(jnp.mean(x * x, axis=-1, keepdims=True) + 1e-06)
     normed_ref[...] = (x * scale).astype(jnp.bfloat16)
 
-    def one_part(part, carry):
-        at = pl.ds(pl.multiple_of(part * cols, cols), cols)
-        hidden_copy(part).wait()
-        middle_ref[:, at] = gelu(
-            jnp.dot(normed_ref[...], hidden_ref[:, at], preferred_element_type=jnp.float32)
-        ).astype(jnp.bfloat16)
-        return carry
-
-    lax.fori_loop(0, ff // cols, one_part, 0)
+    def one_part(part):
+        at = parts[part]
+
+        @pl.when(me >= 0)
+        def _():
+            hidden_copy(part).wait()
+            middle_ref[:, at] = gelu(
+                jnp.dot(normed_ref[...], hidden_ref[:, at], preferred_element_type=jnp.float32)
+            ).astype(jnp.bfloat16)
+
+    for part in range(len(parts)):
+        one_part(part)
     output_copy.wait()
     features = (
         x_ref[...].astype(jnp.float32)
@@ -155,14 +159,14 @@
             pltpu.VMEM((ff, D), jnp.bfloat16),
             pltpu.VMEM((nodes, rows), jnp.bfloat16),
             pltpu.VMEM((rows, ff), jnp.bfloat16),
-            pltpu.SemaphoreType.DMA((5 + ff // hidden_cols(ff),)),
+            pltpu.SemaphoreType.DMA((5 + len(hidden_parts(ff)),)),
         ],
         compiler_params=pltpu.CompilerParams(vmem_limit_bytes=28 * MIB + 8 * nodes * D),
         name="points",
     )(me, *in_hbm)
 
 
-def nodes_kernel(devices, rows, mine_ref, other_ref, out_ref):
+def nodes_kernel(devices, rows, me_ref, mine_ref, other_ref, out_ref, own_ref):
     def part(start, size):
         at = slice(start, start + size)
         return mine_ref[at, :].astype(jnp.float32) + other_ref[at, :].astype(jnp.float32)
@@ -185,37 +189,49 @@
     ) / (1.0 + totals)
     scale = lax.rsqrt(jnp.mean(pooled * pooled, axis=-1, keepdims=True) + 1e-06)
     out_ref[...] = (pooled * scale).astype(jnp.bfloat16)
-
-
-def run_nodes(devices, rows, mine, other):
+    first = me_ref[0] // (devices // 2) * S_DEV
+    own_ref[...] = out_ref[pl.ds(pl.multiple_of(first, S_DEV), S_DEV), :]
+
+
+def run_nodes(devices, rows, me, mine, other):
     return pl.pallas_call(
         functools.partial(nodes_kernel, devices, rows),
-        out_shape=pltpu.VMEM((GROUP_ROWS, D), jnp.bfloat16),
+        in_specs=[pl.BlockSpec(memory_space=pltpu.SMEM)]
+        + [pl.BlockSpec(memory_space=pltpu.VMEM)] * 2,
+        out_shape=[
+            pltpu.VMEM((GROUP_ROWS, D), jnp.bfloat16),
+            pltpu.VMEM((S_DEV, D), jnp.bfloat16),
+        ],
         compiler_params=pltpu.CompilerParams(vmem_limit_bytes=8 * MIB),
         name="nodes",
-    )(mine, other)
-
-
-def attention_kernel(first_ref, proj_ref, gain_ref, *refs):
-    *pieces, out_ref, nodes_ref = refs
-    first = pl.multiple_of(first_ref[0], S_DEV)
-    queries = jnp.dot(
-        pieces[0][pl.ds(first, S_DEV), :], proj_ref[:, :D], preferred_element_type=jnp.float32
+    )(me, *in_vmem(mine, other))
+
+
+def in_vmem(*arrays):
+    return [pltpu.with_memory_space_constraint(array, pltpu.VMEM) for array in arrays]
+
+
+def project(rows, proj_ref, start, size):
+    return jnp.dot(
+        rows, proj_ref[:, start : start + size], preferred_element_type=jnp.float32
     ).astype(jnp.bfloat16)
+
+
+def partial_kernel(own_ref, other_ref, proj_ref, *refs):
+    *pieces, mine_ref, theirs_ref, nodes_ref = refs
     start = 0
     for piece in pieces:
         nodes_ref[start : start + piece.shape[0], :] = piece[...]
         start += piece.shape[0]
-    nodes = nodes_ref[...]
-    keys = jnp.dot(nodes, proj_ref[:, D : 2 * D], preferred_element_type=jnp.float32).astype(
-        jnp.bfloat16
-    )
-    values = jnp.dot(nodes, proj_ref[:, 2 * D :], preferred_element_type=jnp.float32).astype(
-        jnp.bfloat16
-    )
-    lane = lax.broadcasted_iota(jnp.int32, (S_DEV, LANES), 1)
+    queries = project(
+        jnp.concatenate([own_ref[...], other_ref[...]], axis=0), proj_ref, 0, D
+    )
+    keys = project(nodes_ref[...], proj_ref, D, D)
+    values = project(nodes_ref[...], proj_ref, 2 * D, D)
+    rows = 2 * S_DEV
+    lane = lax.broadcasted_iota(jnp.int32, (rows, LANES), 1)
     low = lane < DH
-    heads = []
+    stats = jnp.zeros((rows, LANES), jnp.float32)
     for pair in range(COLS):
         at = slice(pair * LANES, (pair + 1) * LANES)
         both = queries[:, at]
@@ -226,30 +242,64 @@
         scores = lax.dot_general(
             stacked, keys[:, at], (((1,), (1,)), ((), ())), preferred_element_type=jnp.float32
         ) * (DH**-0.5)
-        exps = jnp.exp(scores - jnp.max(scores, axis=-1, keepdims=True))
+        highest = jnp.max(scores, axis=-1, keepdims=True)
+        exps = jnp.exp(scores - highest)
         total = jnp.sum(exps, axis=-1, keepdims=True)
-        summed = (
-            jnp.dot(exps.astype(jnp.bfloat16), values[:, at], preferred_element_type=jnp.float32)
-            / total
+        summed = jnp.dot(
+            exps.astype(jnp.bfloat16), values[:, at], preferred_element_type=jnp.float32
         )
-        heads.append(jnp.where(low, summed[:S_DEV], summed[S_DEV:]))
+        for half in (0, 1):
+            these = slice(half * rows, (half + 1) * rows)
+            stats = jnp.where(lane == 2 * pair + half, highest[these], stats)
+            stats = jnp.where(lane == DH + 2 * pair + half, total[these], stats)
+        piece = jnp.where(low, summed[:rows], summed[rows:])
+        mine_ref[:, at] = piece[:S_DEV]
+        theirs_ref[:, at] = piece[S_DEV:]
+    mine_ref[:, D:] = stats[:S_DEV]
+    theirs_ref[:, D:] = stats[S_DEV:]
+
+
+def run_partial(own, other, proj_weight, pieces):
+    rows = sum(piece.shape[0] for piece in pieces)
+    out = pltpu.VMEM((S_DEV, D + LANES), jnp.float32)
+    return pl.pallas_call(
+        partial_kernel,
+        out_shape=[out, out],
+        scratch_shapes=[pltpu.VMEM((rows, D), jnp.bfloat16)],
+        compiler_params=pltpu.CompilerParams(vmem_limit_bytes=12 * MIB + 24 * rows * D),
+        name="partial",
+    )(*in_vmem(own, other, proj_weight, *pieces))
+
+
+def merge_kernel(mine_ref, theirs_ref, gain_ref, out_ref):
+    mine, theirs = mine_ref[:, D:], theirs_ref[:, D:]
+    highest = jnp.maximum(mine, theirs)
+    mine_scale, theirs_scale = jnp.exp(mine - highest), jnp.exp(theirs - highest)
+    mine_total = pltpu.roll(mine, DH, 1)
+    theirs_total = pltpu.roll(theirs, DH, 1)
+    total = mine_total * mine_scale + theirs_total * theirs_scale
+    mine_scale, theirs_scale = mine_scale / total, theirs_scale / total
+    low = lax.broadcasted_iota(jnp.int32, (S_DEV, LANES), 1) < DH
+    heads = []
+    for pair in range(COLS):
+        at = slice(pair * LANES, (pair + 1) * LANES)
+        first, second = slice(2 * pair, 2 * pair + 1), slice(2 * pair + 1, 2 * pair + 2)
+        heads.append(
+            mine_ref[:, at] * jnp.where(low, mine_scale[:, first], mine_scale[:, second])
+            + theirs_ref[:, at] * jnp.where(low, theirs_scale[:, first], theirs_scale[:, second])
+        )
     attended = jnp.concatenate(heads, axis=1)
     scale = lax.rsqrt(jnp.mean(attended * attended, axis=-1, keepdims=True) + 1e-06)
     out_ref[...] = (attended * scale * gain_ref[...].astype(jnp.float32)).astype(jnp.bfloat16)
 
 
-def run_attention(first, proj_weight, gain, pieces):
-    vmem = pl.BlockSpec(memory_space=pltpu.VMEM)
-    nodes = sum(piece.shape[0] for piece in pieces)
+def run_merge(mine, theirs, gain):
     return pl.pallas_call(
-        attention_kernel,
-        in_specs=[pl.BlockSpec(memory_space=pltpu.SMEM)] + [vmem] * (2 + len(pieces)),
-        out_specs=vmem,
+        merge_kernel,
         out_shape=jax.ShapeDtypeStruct((S_DEV, D), jnp.bfloat16),
-        scratch_shapes=[pltpu.VMEM((nodes, D), jnp.bfloat16)],
-        compiler_params=pltpu.CompilerParams(vmem_limit_bytes=16 * MIB + 6 * nodes * D),
-        name="attention",
-    )(first, proj_weight, gain, *pieces)
+        compiler_params=pltpu.CompilerParams(vmem_limit_bytes=8 * MIB),
+        name="merge",
+    )(*in_vmem(mine, theirs), gain)
 
 
 def add_up(first, *rest):
@@ -271,14 +321,14 @@
 ):
     rows = points_in.shape[0]
     devices = lax.axis_size("blk")
-    me = lax.axis_index("blk").astype(jnp.int32)
+    me = lax.axis_index("blk").astype(jnp.int32).reshape(1)
 
     def swap(array, flip):
         return lax.ppermute(array, "blk", [(i, i ^ flip) for i in range(devices)])
 
     send, keep = run_points(
         devices,
-        me.reshape(1),
+        me,
         points_in,
         hidden_weight,
         output_weight,
@@ -298,14 +348,18 @@
         parts = [table[j * size : (j + 1) * size] for j in range(1 << take)]
         order = list(range(1, 1 << take))[::-1]
         table = add_up(parts[0], *[swap(parts[j], j << (width + 1)) for j in order])
-    nodes = run_nodes(devices, rows, table, swap(table, devices // 2))
+    nodes, own = run_nodes(devices, rows, me, table, swap(table, devices // 2))
     pieces = [nodes]
     for take, width in groups[::-1]:
-        nodes = jnp.concatenate(pieces, axis=0)
-        pieces = [nodes] + [swap(nodes, j << (width + 1)) for j in range(1, 1 << take)]
-    pieces.append(swap(jnp.concatenate(pieces, axis=0), 1))
-    first = (me // (devices // 2) * S_DEV).reshape(1)
-    return run_attention(first, proj_weight, final_gain.reshape(1, D), pieces)
+        pieces += [
+            swap(piece, j << (width + 1))
+            for j in range((1 << take) - 1, 0, -1)
+            for piece in pieces
+        ]
+    pieces[1], held = lax.optimization_barrier((pieces[1], own))
+    other = swap(held, 1)
+    mine, theirs = run_partial(own, other, proj_weight, pieces)
+    return run_merge(mine, swap(theirs, 1), final_gain.reshape(1, D))
 
 
 def solution(mesh):

time: 47.5 us -> 39.2 us (0.83)
  local copies, waits for them, and re-layouts: 4.25 us -> 0.04 us
  Pallas kernels: 12.8 us -> 10.4 us
  waiting for transfers between devices: 17.6 us -> 16.8 us
  other arithmetic: 0.95 us -> 0.17 us
    unnamed x20 -> x4, local copies, waits for them, and re-layouts: 4.22 us -> 0.01 us
    pallas_call x2 -> x3, Pallas kernels: 5.04 us -> 2.84 us  [the longest x1 1.56 us: run_partial(): pl.pallas_call(partial_kernel, out_shape=[out, out], scratch_shapes=[pltp...]
    ppermute x9 -> x10, waiting for transfers between devices: 17.6 us -> 16.8 us  [swap(): return lax.ppermute(array, 'blk', [(i, i ^ flip) for i in range(devices)])]
    concatenate x1 -> x0, other arithmetic: 0.78 us -> none  [body(): pieces.append(swap(jnp.concatenate(pieces, axis=0), 1))]
    ppermute x9 -> x10, starting transfers between devices: 11.5 us -> 11.5 us  [swap(): return lax.ppermute(array, 'blk', [(i, i ^ flip) for i in range(devices)])]
  transfers between devices with their start and end apart: 9 -> 10, of which waited for: 8 -> 8; matrix products, arithmetic and copies ran while one was open for 0% -> 0% of each run, Pallas kernels for 0% -> 0%
where the time goes in v4:
time: 39.2 us; the launch traced here: 39 us
  waiting for transfers between devices  16.8 us (43%)
  starting transfers between devices  11.5 us (29%)
  Pallas kernels  10.4 us (27%)
    ppermute x10, waiting for transfers between devices, swap(): return lax.ppermute(array, 'blk', [(i, i ^ flip) for i in range(devices)])  16.8 us
    ppermute x10, starting transfers between devices, swap(): return lax.ppermute(array, 'blk', [(i, i ^ flip) for i in range(devices)])  11.5 us
    pallas_call x1, Pallas kernels, run_points(): pl.pallas_call(functools.partial(points_kernel, devices), in_specs=[pl.Bl...  7.58 us
    pallas_call x1, Pallas kernels, run_partial(): pl.pallas_call(partial_kernel, out_shape=[out, out], scratch_shapes=[pltp...  1.56 us
    pallas_call x1, Pallas kernels, run_merge(): pl.pallas_call(merge_kernel, out_shape=jax.ShapeDtypeStruct((S_DEV, D), j...  1 us
  transfers between devices with their start and end apart: 10, of which 8 were waited for; matrix products, arithmetic and copies ran while one was open for 0% of the time, Pallas kernels for 0%

profile of v4, /device:TPU:0, one launch (start us, length us, event | category | flops | bytes accessed | tf_op | source)
XLA Modules:
  0.0 39.0 jit_solution(2143078868069326263)
XLA Ops:
  0.0 0.0 copy-start
  0.0 7.6 %points.1 = (bf16[1600,128]{1,0:T(8,128)(2,1)S(1)}, bf16[1600,128]{1,0:T(8,128)(2,1)S(1)}) custom-call(s32[1]{0:T(128)} %bitcast.me_ref, bf16[512,768]{1,0:T(8,128)(2,1)} %x_hbm.1, bf16[768,2560]{1,0:T(8,128)(2,1)} %hidden_hbm.1, bf16[2560,768]{1,0:T(8,128)(2,1)} %output_hbm.1, s32[1,512]{1,0:T(1,128)} %bitcast.4, s32[1,512]{1,0:T(1,128)} %bitcast.5, ...), custom_call_target="tpu_custom_call" | custom-call | tf_op jit(solution)/shard_map/points/pallas_call | solution.py:147
  7.6 0.0 copy-start.1
  7.6 0.5 %collective-permute-start = (bf16[1600,128]{1,0:T(8,128)(2,1)S(1)}, bf16[1600,128]{1,0:T(8,128)(2,1)S(1)}, u32[]{:S(2)}, u32[]{:S(2)}) collective-permute-start(bf16[1600,128]{1,0:T(8,128)(2,1)S(1)} %get-tuple-element.14), channel_id=1, source_target_pairs={{0,1},{1,0},{2,3},{3,2},{4,5},{5,4},{6,7},{7,6},{8,9},{9,8},{10,11... | collective-permute-start | bytes 1228808 | tf_op jit(solution)/shard_map/ppermute | solution.py:327
  8.1 1.4 %collective-permute-done = bf16[1600,128]{1,0:T(8,128)(2,1)S(1)} collective-permute-done((bf16[1600,128]{1,0:T(8,128)(2,1)S(1)}, bf16[1600,128]{1,0:T(8,128)(2,1)S(1)}, u32[]{:S(2)}, u32[]{:S(2)}) %collective-permute-start) | collective-permute-done | bytes 409632 | tf_op jit(solution)/shard_map/ppermute | solution.py:327
  9.5 0.1 add_convert_fusion
  9.6 4.0 %collective-permute-start.1 = (bf16[400,128]{1,0:T(8,128)(2,1)S(1)}, bf16[400,128]{1,0:T(8,128)(2,1)S(1)}, u32[]{:S(2)}, u32[]{:S(2)}) collective-permute-start(bf16[400,128]{1,0:T(8,128)(2,1)S(1)} %get-tuple-element.21), channel_id=1, source_target_pairs={{0,6},{1,7},{2,4},{3,5},{4,2},{5,3},{6,0},{7,1},{8,14},{9,15},{10,... | collective-permute-start | bytes 307208 | tf_op jit(solution)/shard_map/ppermute | solution.py:327
  13.6 0.4 %collective-permute-start.2 = (bf16[400,128]{1,0:T(8,128)(2,1)S(1)}, bf16[400,128]{1,0:T(8,128)(2,1)S(1)}, u32[]{:S(2)}, u32[]{:S(2)}) collective-permute-start(bf16[400,128]{1,0:T(8,128)(2,1)S(1)} %get-tuple-element.23), channel_id=1, source_target_pairs={{0,4},{1,5},{2,6},{3,7},{4,0},{5,1},{6,2},{7,3},{8,12},{9,13},{10,... | collective-permute-start | bytes 307208 | tf_op jit(solution)/shard_map/ppermute | solution.py:327
  14.1 0.2 collective-permute-start.3
  14.2 3.0 %collective-permute-done.1 = bf16[400,128]{1,0:T(8,128)(2,1)S(1)} collective-permute-done((bf16[400,128]{1,0:T(8,128)(2,1)S(1)}, bf16[400,128]{1,0:T(8,128)(2,1)S(1)}, u32[]{:S(2)}, u32[]{:S(2)}) %collective-permute-start.1) | collective-permute-done | bytes 102432 | tf_op jit(solution)/shard_map/ppermute | solution.py:327
  17.3 1.9 %collective-permute-done.2 = bf16[400,128]{1,0:T(8,128)(2,1)S(1)} collective-permute-done((bf16[400,128]{1,0:T(8,128)(2,1)S(1)}, bf16[400,128]{1,0:T(8,128)(2,1)S(1)}, u32[]{:S(2)}, u32[]{:S(2)}) %collective-permute-start.2) | collective-permute-done | bytes 102432 | tf_op jit(solution)/shard_map/ppermute | solution.py:327
  19.1 0.0 collective-permute-done.3
  19.1 0.1 add_convert_fusion.1.mine_ref
  19.2 2.7 %collective-permute-start.4 = (bf16[400,128]{1,0:T(8,128)(2,1)S(1)}, bf16[400,128]{1,0:T(8,128)(2,1)S(1)}, u32[]{:S(2)}, u32[]{:S(2)}) collective-permute-start(bf16[400,128]{1,0:T(8,128)(2,1)S(1)} %add_convert_fusion.1.mine_ref), channel_id=1, source_target_pairs={{0,8},{1,9},{2,10},{3,11},{4,12},{5,13},{6,14},{7,15},{8,0},{9,1},... | collective-permute-start | bytes 307208 | tf_op jit(solution)/shard_map/ppermute | solution.py:327
  21.9 4.6 %collective-permute-done.4.other_ref = bf16[400,128]{1,0:T(8,128)(2,1)S(1)} collective-permute-done((bf16[400,128]{1,0:T(8,128)(2,1)S(1)}, bf16[400,128]{1,0:T(8,128)(2,1)S(1)}, u32[]{:S(2)}, u32[]{:S(2)}) %collective-permute-start.4) | collective-permute-done | bytes 102432 | tf_op jit(solution)/shard_map/ppermute | solution.py:327
  26.5 0.3 nodes.1
  26.8 2.2 %collective-permute-start.5 = (bf16[64,768]{1,0:T(8,128)(2,1)S(1)}, bf16[64,768]{1,0:T(8,128)(2,1)S(1)}, u32[]{:S(2)}, u32[]{:S(2)}) collective-permute-start(bf16[64,768]{1,0:T(8,128)(2,1)S(1)} %get-tuple-element.16.refs_0_), channel_id=1, source_target_pairs={{0,6},{1,7},{2,4},{3,5},{4,2},{5,3},{6,0},{7,1},{8,14},{9,15},{10,... | collective-permute-start | bytes 294920 | tf_op jit(solution)/shard_map/ppermute | solution.py:327
  28.9 1.5 %collective-permute-start.7 = (bf16[64,768]{1,0:T(8,128)(2,1)S(1)}, bf16[64,768]{1,0:T(8,128)(2,1)S(1)}, u32[]{:S(2)}, u32[]{:S(2)}) collective-permute-start(bf16[64,768]{1,0:T(8,128)(2,1)S(1)} %get-tuple-element.16.refs_0_), channel_id=1, source_target_pairs={{0,4},{1,5},{2,6},{3,7},{4,0},{5,1},{6,2},{7,3},{8,12},{9,13},{10,... | collective-permute-start | bytes 294920 | tf_op jit(solution)/shard_map/ppermute | solution.py:327
  30.4 0.0 collective-permute-start.8
  30.4 2.6 %collective-permute-done.5.refs_1_ = bf16[64,768]{1,0:T(8,128)(2,1)S(1)} collective-permute-done((bf16[64,768]{1,0:T(8,128)(2,1)S(1)}, bf16[64,768]{1,0:T(8,128)(2,1)S(1)}, u32[]{:S(2)}, u32[]{:S(2)}) %collective-permute-start.5) | collective-permute-done | bytes 98336 | tf_op jit(solution)/shard_map/ppermute | solution.py:327
  33.1 0.0 collective-permute-start.6
  33.1 1.3 %collective-permute-done.7.refs_2_ = bf16[64,768]{1,0:T(8,128)(2,1)S(1)} collective-permute-done((bf16[64,768]{1,0:T(8,128)(2,1)S(1)}, bf16[64,768]{1,0:T(8,128)(2,1)S(1)}, u32[]{:S(2)}, u32[]{:S(2)}) %collective-permute-start.7) | collective-permute-done | bytes 98336 | tf_op jit(solution)/shard_map/ppermute | solution.py:327
  34.4 0.6 %collective-permute-done.8.refs_3_ = bf16[64,768]{1,0:T(8,128)(2,1)S(1)} collective-permute-done((bf16[64,768]{1,0:T(8,128)(2,1)S(1)}, bf16[64,768]{1,0:T(8,128)(2,1)S(1)}, u32[]{:S(2)}, u32[]{:S(2)}) %collective-permute-start.8) | collective-permute-done | bytes 98336 | tf_op jit(solution)/shard_map/ppermute | solution.py:327
  35.1 0.0 collective-permute-done.6.other_ref
  35.1 0.0 copy-done
  35.1 1.6 %partial.1 = (f32[32,896]{1,0:T(8,128)S(1)}, f32[32,896]{1,0:T(8,128)S(1)}) custom-call(bf16[32,768]{1,0:T(8,128)(2,1)S(1)} %get-tuple-element.17.own_ref, bf16[32,768]{1,0:T(8,128)(2,1)S(1)} %collective-permute-done.6.other_ref, bf16[768,2304]{1,0:T(8,128)(2,1)S(1)} %copy-done, bf16[64,768]{1,0:T(8,128)(2,1)S(1)} %get-tuple-element.16.refs_0_, ...), custom_call_target="tpu_custom_call" | custom-call | tf_op jit(solution)/shard_map/partial/pallas_call | solution.py:265
  36.6 0.1 collective-permute-start.9
  36.7 0.0 copy-done.1
  36.7 1.3 %collective-permute-done.9.theirs_ref = f32[32,896]{1,0:T(8,128)S(1)} collective-permute-done((f32[32,896]{1,0:T(8,128)S(1)}, f32[32,896]{1,0:T(8,128)S(1)}, u32[]{:S(2)}, u32[]{:S(2)}) %collective-permute-start.9) | collective-permute-done | bytes 114720 | tf_op jit(solution)/shard_map/ppermute | solution.py:327
  38.0 1.0 %merge.1 = bf16[32,768]{1,0:T(8,128)(2,1)} custom-call(f32[32,896]{1,0:T(8,128)S(1)} %get-tuple-element.19.mine_ref, f32[32,896]{1,0:T(8,128)S(1)} %collective-permute-done.9.theirs_ref, bf16[1,768]{1,0:T(2,128)(2,1)S(1)} %reshape.19.gain_ref), custom_call_target="tpu_custom_call" | custom-call | tf_op jit(solution)/shard_map/merge/pallas_call | solution.py:297
  (2 shorter events, 0.0 us)
Async XLA Ops:
  0.0 35.1 %copy-start = (bf16[768,2304]{1,0:T(8,128)(2,1)S(1)}, bf16[768,2304]{1,0:T(8,128)(2,1)}, u32[]{:S(2)}) copy-start(bf16[768,2304]{1,0:T(8,128)(2,1)} %proj_ref.1) | copy-start | bytes 10616836
  7.6 29.1 %copy-start.1 = (bf16[768]{0:T(1024)(128)(2,1)S(1)}, bf16[768]{0:T(1024)(128)(2,1)}, u32[]{:S(2)}) copy-start(bf16[768]{0:T(1024)(128)(2,1)} %param.15) | copy-start | bytes 4612
  7.6 1.9 %collective-permute-start = (bf16[1600,128]{1,0:T(8,128)(2,1)S(1)}, bf16[1600,128]{1,0:T(8,128)(2,1)S(1)}, u32[]{:S(2)}, u32[]{:S(2)}) collective-permute-start(bf16[1600,128]{1,0:T(8,128)(2,1)S(1)} %get-tuple-element.14), channel_id=1, source_target_pairs={{0,1},{1,0},{2,3},{3,2},{4,5},{5,4},{6,7},{7,6},{8,9},{9,8},{10,11... | collective-permute-start | bytes 1228808 | tf_op jit(solution)/shard_map/ppermute | solution.py:327
  9.6 7.6 %collective-permute-start.1 = (bf16[400,128]{1,0:T(8,128)(2,1)S(1)}, bf16[400,128]{1,0:T(8,128)(2,1)S(1)}, u32[]{:S(2)}, u32[]{:S(2)}) collective-permute-start(bf16[400,128]{1,0:T(8,128)(2,1)S(1)} %get-tuple-element.21), channel_id=1, source_target_pairs={{0,6},{1,7},{2,4},{3,5},{4,2},{5,3},{6,0},{7,1},{8,14},{9,15},{10,... | collective-permute-start | bytes 307208 | tf_op jit(solution)/shard_map/ppermute | solution.py:327
  13.6 5.5 %collective-permute-start.2 = (bf16[400,128]{1,0:T(8,128)(2,1)S(1)}, bf16[400,128]{1,0:T(8,128)(2,1)S(1)}, u32[]{:S(2)}, u32[]{:S(2)}) collective-permute-start(bf16[400,128]{1,0:T(8,128)(2,1)S(1)} %get-tuple-element.23), channel_id=1, source_target_pairs={{0,4},{1,5},{2,6},{3,7},{4,0},{5,1},{6,2},{7,3},{8,12},{9,13},{10,... | collective-permute-start | bytes 307208 | tf_op jit(solution)/shard_map/ppermute | solution.py:327
  14.1 5.1 %collective-permute-start.3 = (bf16[400,128]{1,0:T(8,128)(2,1)S(1)}, bf16[400,128]{1,0:T(8,128)(2,1)S(1)}, u32[]{:S(2)}, u32[]{:S(2)}) collective-permute-start(bf16[400,128]{1,0:T(8,128)(2,1)S(1)} %get-tuple-element.22), channel_id=1, source_target_pairs={{0,2},{1,3},{2,0},{3,1},{4,6},{5,7},{6,4},{7,5},{8,10},{9,11},{10,... | collective-permute-start | bytes 307208 | tf_op jit(solution)/shard_map/ppermute | solution.py:327
  19.2 7.3 %collective-permute-start.4 = (bf16[400,128]{1,0:T(8,128)(2,1)S(1)}, bf16[400,128]{1,0:T(8,128)(2,1)S(1)}, u32[]{:S(2)}, u32[]{:S(2)}) collective-permute-start(bf16[400,128]{1,0:T(8,128)(2,1)S(1)} %add_convert_fusion.1.mine_ref), channel_id=1, source_target_pairs={{0,8},{1,9},{2,10},{3,11},{4,12},{5,13},{6,14},{7,15},{8,0},{9,1},... | collective-permute-start | bytes 307208 | tf_op jit(solution)/shard_map/ppermute | solution.py:327
  26.8 6.3 %collective-permute-start.5 = (bf16[64,768]{1,0:T(8,128)(2,1)S(1)}, bf16[64,768]{1,0:T(8,128)(2,1)S(1)}, u32[]{:S(2)}, u32[]{:S(2)}) collective-permute-start(bf16[64,768]{1,0:T(8,128)(2,1)S(1)} %get-tuple-element.16.refs_0_), channel_id=1, source_target_pairs={{0,6},{1,7},{2,4},{3,5},{4,2},{5,3},{6,0},{7,1},{8,14},{9,15},{10,... | collective-permute-start | bytes 294920 | tf_op jit(solution)/shard_map/ppermute | solution.py:327
  28.9 5.5 %collective-permute-start.7 = (bf16[64,768]{1,0:T(8,128)(2,1)S(1)}, bf16[64,768]{1,0:T(8,128)(2,1)S(1)}, u32[]{:S(2)}, u32[]{:S(2)}) collective-permute-start(bf16[64,768]{1,0:T(8,128)(2,1)S(1)} %get-tuple-element.16.refs_0_), channel_id=1, source_target_pairs={{0,4},{1,5},{2,6},{3,7},{4,0},{5,1},{6,2},{7,3},{8,12},{9,13},{10,... | collective-permute-start | bytes 294920 | tf_op jit(solution)/shard_map/ppermute | solution.py:327
  30.4 4.6 %collective-permute-start.8 = (bf16[64,768]{1,0:T(8,128)(2,1)S(1)}, bf16[64,768]{1,0:T(8,128)(2,1)S(1)}, u32[]{:S(2)}, u32[]{:S(2)}) collective-permute-start(bf16[64,768]{1,0:T(8,128)(2,1)S(1)} %get-tuple-element.16.refs_0_), channel_id=1, source_target_pairs={{0,2},{1,3},{2,0},{3,1},{4,6},{5,7},{6,4},{7,5},{8,10},{9,11},{10,... | collective-permute-start | bytes 294920 | tf_op jit(solution)/shard_map/ppermute | solution.py:327
  33.1 2.0 %collective-permute-start.6 = (bf16[32,768]{1,0:T(8,128)(2,1)S(1)}, bf16[32,768]{1,0:T(8,128)(2,1)S(1)}, u32[]{:S(2)}, u32[]{:S(2)}) collective-permute-start(bf16[32,768]{1,0:T(8,128)(2,1)S(1)} %get-tuple-element.17.own_ref), channel_id=1, source_target_pairs={{0,1},{1,0},{2,3},{3,2},{4,5},{5,4},{6,7},{7,6},{8,9},{9,8},{10,11... | collective-permute-start | bytes 147464 | tf_op jit(solution)/shard_map/ppermute | solution.py:327
  36.6 1.4 %collective-permute-start.9 = (f32[32,896]{1,0:T(8,128)S(1)}, f32[32,896]{1,0:T(8,128)S(1)}, u32[]{:S(2)}, u32[]{:S(2)}) collective-permute-start(f32[32,896]{1,0:T(8,128)S(1)} %get-tuple-element.20), channel_id=1, source_target_pairs={{0,1},{1,0},{2,3},{3,2},{4,5},{5,4},{6,7},{7,6},{8,9},{9,8},{10,11... | collective-permute-start | bytes 344072 | tf_op jit(solution)/shard_map/ppermute | solution.py:327

commit v5 on v4

--- a/solution.py
+++ b/solution.py
@@ -33,7 +33,7 @@
 
 
 def hidden_parts(ff):
-    stops = [stop for stop in (256, 1024) if stop < ff] + [ff]
+    stops = [stop for stop in (768,) if stop < ff] + [ff]
     return [slice(start, stop) for start, stop in zip([0] + stops[:-1], stops)]
 
 
@@ -110,7 +110,7 @@
     def one_part(part):
         at = parts[part]
 
-        @pl.when(me >= 0)
+        @pl.when(me > -2 - part)
         def _():
             hidden_copy(part).wait()
             middle_ref[:, at] = gelu(
@@ -120,13 +120,16 @@
     for part in range(len(parts)):
         one_part(part)
     output_copy.wait()
-    features = (
-        x_ref[...].astype(jnp.float32)
-        + jnp.dot(middle_ref[...], output_ref[...], preferred_element_type=jnp.float32)
-    ).astype(jnp.bfloat16)
-    sums = jnp.dot(coeffs_ref[...], features, preferred_element_type=jnp.float32).astype(
-        jnp.bfloat16
-    )
+    sums = None
+    half_rows = rows // 2
+    for at in (slice(0, half_rows), slice(half_rows, rows)):
+        features = (
+            x_ref[at, :].astype(jnp.float32)
+            + jnp.dot(middle_ref[at, :], output_ref[...], preferred_element_type=jnp.float32)
+        ).astype(jnp.bfloat16)
+        term = jnp.dot(coeffs_ref[:, at], features, preferred_element_type=jnp.float32)
+        sums = term if sums is None else sums + term
+    sums = sums.astype(jnp.bfloat16)
     for out_ref, base, first in places:
         for col in range(COLS):
             out_ref[base + col * GROUP_ROWS : base + (col + 1) * GROUP_ROWS, :] = sums[
@@ -346,14 +349,14 @@
     for take, width in groups:
         size = (1 << width) * CHUNK
         parts = [table[j * size : (j + 1) * size] for j in range(1 << take)]
-        order = list(range(1, 1 << take))[::-1]
+        order = (2, 1, 3) if take == 2 else (1,)
         table = add_up(parts[0], *[swap(parts[j], j << (width + 1)) for j in order])
     nodes, own = run_nodes(devices, rows, me, table, swap(table, devices // 2))
     pieces = [nodes]
     for take, width in groups[::-1]:
         pieces += [
             swap(piece, j << (width + 1))
-            for j in range((1 << take) - 1, 0, -1)
+            for j in ((3, 1, 2) if take == 2 else (1,))
             for piece in pieces
         ]
     pieces[1], held = lax.optimization_barrier((pieces[1], own))

time: 39.2 us -> 37.3 us (0.952)
  waiting for transfers between devices: 16.8 us -> 15.5 us
  Pallas kernels: 10.4 us -> 9.86 us
    ppermute x10, waiting for transfers between devices: 16.8 us -> 15.5 us  [swap(): return lax.ppermute(array, 'blk', [(i, i ^ flip) for i in range(devices)])]
    pallas_call x1, Pallas kernels: 7.58 us -> 7.02 us  [run_points(): pl.pallas_call(functools.partial(points_kernel, devices), in_specs=[pl.Bl...]
  transfers between devices with their start and end apart: 10 -> 10, of which waited for: 8 -> 10; matrix products, arithmetic and copies ran while one was open for 0% -> 0% of each run, Pallas kernels for 0% -> 0%
where the time goes in v5:
time: 37.3 us; the launch traced here: 37.2 us
  waiting for transfers between devices  15.5 us (42%)
  starting transfers between devices  11.5 us (31%)
  Pallas kernels  9.86 us (26%)
    ppermute x10, waiting for transfers between devices, swap(): return lax.ppermute(array, 'blk', [(i, i ^ flip) for i in range(devices)])  15.5 us
    ppermute x10, starting transfers between devices, swap(): return lax.ppermute(array, 'blk', [(i, i ^ flip) for i in range(devices)])  11.5 us
    pallas_call x1, Pallas kernels, run_points(): pl.pallas_call(functools.partial(points_kernel, devices), in_specs=[pl.Bl...  7.02 us
    pallas_call x1, Pallas kernels, run_partial(): pl.pallas_call(partial_kernel, out_shape=[out, out], scratch_shapes=[pltp...  1.56 us
    pallas_call x1, Pallas kernels, run_merge(): pl.pallas_call(merge_kernel, out_shape=jax.ShapeDtypeStruct((S_DEV, D), j...  1 us
  transfers between devices with their start and end apart: 10, of which 10 were waited for; matrix products, arithmetic and copies ran while one was open for 0% of the time, Pallas kernels for 0%

profile of v5, /device:TPU:0, one launch (start us, length us, event | category | flops | bytes accessed | tf_op | source)
XLA Modules:
  0.0 37.2 jit_solution(2760526618606717647)
XLA Ops:
  0.0 0.0 copy-start
  0.0 7.0 %points.1 = (bf16[1600,128]{1,0:T(8,128)(2,1)S(1)}, bf16[1600,128]{1,0:T(8,128)(2,1)S(1)}) custom-call(s32[1]{0:T(128)} %bitcast.me_ref, bf16[512,768]{1,0:T(8,128)(2,1)} %x_hbm.1, bf16[768,2560]{1,0:T(8,128)(2,1)} %hidden_hbm.1, bf16[2560,768]{1,0:T(8,128)(2,1)} %output_hbm.1, s32[1,512]{1,0:T(1,128)} %bitcast.4, s32[1,512]{1,0:T(1,128)} %bitcast.5, ...), custom_call_target="tpu_custom_call" | custom-call | tf_op jit(solution)/shard_map/points/pallas_call | solution.py:150
  7.0 0.0 copy-start.1
  7.0 0.5 %collective-permute-start = (bf16[1600,128]{1,0:T(8,128)(2,1)S(1)}, bf16[1600,128]{1,0:T(8,128)(2,1)S(1)}, u32[]{:S(2)}, u32[]{:S(2)}) collective-permute-start(bf16[1600,128]{1,0:T(8,128)(2,1)S(1)} %get-tuple-element.14), channel_id=1, source_target_pairs={{0,1},{1,0},{2,3},{3,2},{4,5},{5,4},{6,7},{7,6},{8,9},{9,8},{10,11... | collective-permute-start | bytes 1228808 | tf_op jit(solution)/shard_map/ppermute | solution.py:330
  7.6 1.4 %collective-permute-done = bf16[1600,128]{1,0:T(8,128)(2,1)S(1)} collective-permute-done((bf16[1600,128]{1,0:T(8,128)(2,1)S(1)}, bf16[1600,128]{1,0:T(8,128)(2,1)S(1)}, u32[]{:S(2)}, u32[]{:S(2)}) %collective-permute-start) | collective-permute-done | bytes 409632 | tf_op jit(solution)/shard_map/ppermute | solution.py:330
  8.9 0.1 add_convert_fusion
  9.1 3.0 %collective-permute-start.1 = (bf16[400,128]{1,0:T(8,128)(2,1)S(1)}, bf16[400,128]{1,0:T(8,128)(2,1)S(1)}, u32[]{:S(2)}, u32[]{:S(2)}) collective-permute-start(bf16[400,128]{1,0:T(8,128)(2,1)S(1)} %get-tuple-element.21), channel_id=1, source_target_pairs={{0,4},{1,5},{2,6},{3,7},{4,0},{5,1},{6,2},{7,3},{8,12},{9,13},{10,... | collective-permute-start | bytes 307208 | tf_op jit(solution)/shard_map/ppermute | solution.py:330
  12.1 1.5 %collective-permute-start.2 = (bf16[400,128]{1,0:T(8,128)(2,1)S(1)}, bf16[400,128]{1,0:T(8,128)(2,1)S(1)}, u32[]{:S(2)}, u32[]{:S(2)}) collective-permute-start(bf16[400,128]{1,0:T(8,128)(2,1)S(1)} %get-tuple-element.23), channel_id=1, source_target_pairs={{0,2},{1,3},{2,0},{3,1},{4,6},{5,7},{6,4},{7,5},{8,10},{9,11},{10,... | collective-permute-start | bytes 307208 | tf_op jit(solution)/shard_map/ppermute | solution.py:330
  13.6 0.0 collective-permute-start.3
  13.6 1.7 %collective-permute-done.1 = bf16[400,128]{1,0:T(8,128)(2,1)S(1)} collective-permute-done((bf16[400,128]{1,0:T(8,128)(2,1)S(1)}, bf16[400,128]{1,0:T(8,128)(2,1)S(1)}, u32[]{:S(2)}, u32[]{:S(2)}) %collective-permute-start.1) | collective-permute-done | bytes 102432 | tf_op jit(solution)/shard_map/ppermute | solution.py:330
  15.3 2.6 %collective-permute-done.2 = bf16[400,128]{1,0:T(8,128)(2,1)S(1)} collective-permute-done((bf16[400,128]{1,0:T(8,128)(2,1)S(1)}, bf16[400,128]{1,0:T(8,128)(2,1)S(1)}, u32[]{:S(2)}, u32[]{:S(2)}) %collective-permute-start.2) | collective-permute-done | bytes 102432 | tf_op jit(solution)/shard_map/ppermute | solution.py:330
  18.0 1.2 %collective-permute-done.3 = bf16[400,128]{1,0:T(8,128)(2,1)S(1)} collective-permute-done((bf16[400,128]{1,0:T(8,128)(2,1)S(1)}, bf16[400,128]{1,0:T(8,128)(2,1)S(1)}, u32[]{:S(2)}, u32[]{:S(2)}) %collective-permute-start.3) | collective-permute-done | bytes 102432 | tf_op jit(solution)/shard_map/ppermute | solution.py:330
  19.2 0.1 add_convert_fusion.1.mine_ref
  19.2 2.7 %collective-permute-start.4 = (bf16[400,128]{1,0:T(8,128)(2,1)S(1)}, bf16[400,128]{1,0:T(8,128)(2,1)S(1)}, u32[]{:S(2)}, u32[]{:S(2)}) collective-permute-start(bf16[400,128]{1,0:T(8,128)(2,1)S(1)} %add_convert_fusion.1.mine_ref), channel_id=1, source_target_pairs={{0,8},{1,9},{2,10},{3,11},{4,12},{5,13},{6,14},{7,15},{8,0},{9,1},... | collective-permute-start | bytes 307208 | tf_op jit(solution)/shard_map/ppermute | solution.py:330
  21.9 4.1 %collective-permute-done.4.other_ref = bf16[400,128]{1,0:T(8,128)(2,1)S(1)} collective-permute-done((bf16[400,128]{1,0:T(8,128)(2,1)S(1)}, bf16[400,128]{1,0:T(8,128)(2,1)S(1)}, u32[]{:S(2)}, u32[]{:S(2)}) %collective-permute-start.4) | collective-permute-done | bytes 102432 | tf_op jit(solution)/shard_map/ppermute | solution.py:330
  26.0 0.3 nodes.1
  26.3 0.2 collective-permute-start.5
  26.5 1.7 %collective-permute-start.7 = (bf16[64,768]{1,0:T(8,128)(2,1)S(1)}, bf16[64,768]{1,0:T(8,128)(2,1)S(1)}, u32[]{:S(2)}, u32[]{:S(2)}) collective-permute-start(bf16[64,768]{1,0:T(8,128)(2,1)S(1)} %get-tuple-element.16.refs_0_), channel_id=1, source_target_pairs={{0,2},{1,3},{2,0},{3,1},{4,6},{5,7},{6,4},{7,5},{8,10},{9,11},{10,... | collective-permute-start | bytes 294920 | tf_op jit(solution)/shard_map/ppermute | solution.py:330
  28.2 1.7 %collective-permute-start.8 = (bf16[64,768]{1,0:T(8,128)(2,1)S(1)}, bf16[64,768]{1,0:T(8,128)(2,1)S(1)}, u32[]{:S(2)}, u32[]{:S(2)}) collective-permute-start(bf16[64,768]{1,0:T(8,128)(2,1)S(1)} %get-tuple-element.16.refs_0_), channel_id=1, source_target_pairs={{0,4},{1,5},{2,6},{3,7},{4,0},{5,1},{6,2},{7,3},{8,12},{9,13},{10,... | collective-permute-start | bytes 294920 | tf_op jit(solution)/shard_map/ppermute | solution.py:330
  29.8 2.1 %collective-permute-done.5.refs_1_ = bf16[64,768]{1,0:T(8,128)(2,1)S(1)} collective-permute-done((bf16[64,768]{1,0:T(8,128)(2,1)S(1)}, bf16[64,768]{1,0:T(8,128)(2,1)S(1)}, u32[]{:S(2)}, u32[]{:S(2)}) %collective-permute-start.5) | collective-permute-done | bytes 98336 | tf_op jit(solution)/shard_map/ppermute | solution.py:330
  32.0 0.0 collective-permute-start.6
  32.0 0.2 collective-permute-done.7.refs_2_
  32.2 0.6 %collective-permute-done.8.refs_3_ = bf16[64,768]{1,0:T(8,128)(2,1)S(1)} collective-permute-done((bf16[64,768]{1,0:T(8,128)(2,1)S(1)}, bf16[64,768]{1,0:T(8,128)(2,1)S(1)}, u32[]{:S(2)}, u32[]{:S(2)}) %collective-permute-start.8) | collective-permute-done | bytes 98336 | tf_op jit(solution)/shard_map/ppermute | solution.py:330
  32.8 0.4 %collective-permute-done.6.other_ref = bf16[32,768]{1,0:T(8,128)(2,1)S(1)} collective-permute-done((bf16[32,768]{1,0:T(8,128)(2,1)S(1)}, bf16[32,768]{1,0:T(8,128)(2,1)S(1)}, u32[]{:S(2)}, u32[]{:S(2)}) %collective-permute-start.6) | collective-permute-done | bytes 49184 | tf_op jit(solution)/shard_map/ppermute | solution.py:330
  33.2 0.0 copy-done
  33.2 1.6 %partial.1 = (f32[32,896]{1,0:T(8,128)S(1)}, f32[32,896]{1,0:T(8,128)S(1)}) custom-call(bf16[32,768]{1,0:T(8,128)(2,1)S(1)} %get-tuple-element.17.own_ref, bf16[32,768]{1,0:T(8,128)(2,1)S(1)} %collective-permute-done.6.other_ref, bf16[768,2304]{1,0:T(8,128)(2,1)S(1)} %copy-done, bf16[64,768]{1,0:T(8,128)(2,1)S(1)} %get-tuple-element.16.refs_0_, ...), custom_call_target="tpu_custom_call" | custom-call | tf_op jit(solution)/shard_map/partial/pallas_call | solution.py:268
  34.8 0.2 collective-permute-start.9
  35.0 0.0 copy-done.1
  35.0 1.2 %collective-permute-done.9.theirs_ref = f32[32,896]{1,0:T(8,128)S(1)} collective-permute-done((f32[32,896]{1,0:T(8,128)S(1)}, f32[32,896]{1,0:T(8,128)S(1)}, u32[]{:S(2)}, u32[]{:S(2)}) %collective-permute-start.9) | collective-permute-done | bytes 114720 | tf_op jit(solution)/shard_map/ppermute | solution.py:330
  36.2 1.0 %merge.1 = bf16[32,768]{1,0:T(8,128)(2,1)} custom-call(f32[32,896]{1,0:T(8,128)S(1)} %get-tuple-element.19.mine_ref, f32[32,896]{1,0:T(8,128)S(1)} %collective-permute-done.9.theirs_ref, bf16[1,768]{1,0:T(2,128)(2,1)S(1)} %reshape.19.gain_ref), custom_call_target="tpu_custom_call" | custom-call | tf_op jit(solution)/shard_map/merge/pallas_call | solution.py:300
  (2 shorter events, 0.0 us)
Async XLA Ops:
  0.0 33.2 %copy-start = (bf16[768,2304]{1,0:T(8,128)(2,1)S(1)}, bf16[768,2304]{1,0:T(8,128)(2,1)}, u32[]{:S(2)}) copy-start(bf16[768,2304]{1,0:T(8,128)(2,1)} %proj_ref.1) | copy-start | bytes 10616836
  7.0 28.0 %copy-start.1 = (bf16[768]{0:T(1024)(128)(2,1)S(1)}, bf16[768]{0:T(1024)(128)(2,1)}, u32[]{:S(2)}) copy-start(bf16[768]{0:T(1024)(128)(2,1)} %param.15) | copy-start | bytes 4612
  7.0 1.9 %collective-permute-start = (bf16[1600,128]{1,0:T(8,128)(2,1)S(1)}, bf16[1600,128]{1,0:T(8,128)(2,1)S(1)}, u32[]{:S(2)}, u32[]{:S(2)}) collective-permute-start(bf16[1600,128]{1,0:T(8,128)(2,1)S(1)} %get-tuple-element.14), channel_id=1, source_target_pairs={{0,1},{1,0},{2,3},{3,2},{4,5},{5,4},{6,7},{7,6},{8,9},{9,8},{10,11... | collective-permute-start | bytes 1228808 | tf_op jit(solution)/shard_map/ppermute | solution.py:330
  9.1 6.3 %collective-permute-start.1 = (bf16[400,128]{1,0:T(8,128)(2,1)S(1)}, bf16[400,128]{1,0:T(8,128)(2,1)S(1)}, u32[]{:S(2)}, u32[]{:S(2)}) collective-permute-start(bf16[400,128]{1,0:T(8,128)(2,1)S(1)} %get-tuple-element.21), channel_id=1, source_target_pairs={{0,4},{1,5},{2,6},{3,7},{4,0},{5,1},{6,2},{7,3},{8,12},{9,13},{10,... | collective-permute-start | bytes 307208 | tf_op jit(solution)/shard_map/ppermute | solution.py:330
  12.1 5.9 %collective-permute-start.2 = (bf16[400,128]{1,0:T(8,128)(2,1)S(1)}, bf16[400,128]{1,0:T(8,128)(2,1)S(1)}, u32[]{:S(2)}, u32[]{:S(2)}) collective-permute-start(bf16[400,128]{1,0:T(8,128)(2,1)S(1)} %get-tuple-element.23), channel_id=1, source_target_pairs={{0,2},{1,3},{2,0},{3,1},{4,6},{5,7},{6,4},{7,5},{8,10},{9,11},{10,... | collective-permute-start | bytes 307208 | tf_op jit(solution)/shard_map/ppermute | solution.py:330
  13.6 5.6 %collective-permute-start.3 = (bf16[400,128]{1,0:T(8,128)(2,1)S(1)}, bf16[400,128]{1,0:T(8,128)(2,1)S(1)}, u32[]{:S(2)}, u32[]{:S(2)}) collective-permute-start(bf16[400,128]{1,0:T(8,128)(2,1)S(1)} %get-tuple-element.22), channel_id=1, source_target_pairs={{0,6},{1,7},{2,4},{3,5},{4,2},{5,3},{6,0},{7,1},{8,14},{9,15},{10,... | collective-permute-start | bytes 307208 | tf_op jit(solution)/shard_map/ppermute | solution.py:330
  19.2 6.8 %collective-permute-start.4 = (bf16[400,128]{1,0:T(8,128)(2,1)S(1)}, bf16[400,128]{1,0:T(8,128)(2,1)S(1)}, u32[]{:S(2)}, u32[]{:S(2)}) collective-permute-start(bf16[400,128]{1,0:T(8,128)(2,1)S(1)} %add_convert_fusion.1.mine_ref), channel_id=1, source_target_pairs={{0,8},{1,9},{2,10},{3,11},{4,12},{5,13},{6,14},{7,15},{8,0},{9,1},... | collective-permute-start | bytes 307208 | tf_op jit(solution)/shard_map/ppermute | solution.py:330
  26.3 5.7 %collective-permute-start.5 = (bf16[64,768]{1,0:T(8,128)(2,1)S(1)}, bf16[64,768]{1,0:T(8,128)(2,1)S(1)}, u32[]{:S(2)}, u32[]{:S(2)}) collective-permute-start(bf16[64,768]{1,0:T(8,128)(2,1)S(1)} %get-tuple-element.16.refs_0_), channel_id=1, source_target_pairs={{0,6},{1,7},{2,4},{3,5},{4,2},{5,3},{6,0},{7,1},{8,14},{9,15},{10,... | collective-permute-start | bytes 294920 | tf_op jit(solution)/shard_map/ppermute | solution.py:330
  26.5 5.7 %collective-permute-start.7 = (bf16[64,768]{1,0:T(8,128)(2,1)S(1)}, bf16[64,768]{1,0:T(8,128)(2,1)S(1)}, u32[]{:S(2)}, u32[]{:S(2)}) collective-permute-start(bf16[64,768]{1,0:T(8,128)(2,1)S(1)} %get-tuple-element.16.refs_0_), channel_id=1, source_target_pairs={{0,2},{1,3},{2,0},{3,1},{4,6},{5,7},{6,4},{7,5},{8,10},{9,11},{10,... | collective-permute-start | bytes 294920 | tf_op jit(solution)/shard_map/ppermute | solution.py:330
  28.2 4.6 %collective-permute-start.8 = (bf16[64,768]{1,0:T(8,128)(2,1)S(1)}, bf16[64,768]{1,0:T(8,128)(2,1)S(1)}, u32[]{:S(2)}, u32[]{:S(2)}) collective-permute-start(bf16[64,768]{1,0:T(8,128)(2,1)S(1)} %get-tuple-element.16.refs_0_), channel_id=1, source_target_pairs={{0,4},{1,5},{2,6},{3,7},{4,0},{5,1},{6,2},{7,3},{8,12},{9,13},{10,... | collective-permute-start | bytes 294920 | tf_op jit(solution)/shard_map/ppermute | solution.py:330
  32.0 1.2 %collective-permute-start.6 = (bf16[32,768]{1,0:T(8,128)(2,1)S(1)}, bf16[32,768]{1,0:T(8,128)(2,1)S(1)}, u32[]{:S(2)}, u32[]{:S(2)}) collective-permute-start(bf16[32,768]{1,0:T(8,128)(2,1)S(1)} %get-tuple-element.17.own_ref), channel_id=1, source_target_pairs={{0,1},{1,0},{2,3},{3,2},{4,5},{5,4},{6,7},{7,6},{8,9},{9,8},{10,11... | collective-permute-start | bytes 147464 | tf_op jit(solution)/shard_map/ppermute | solution.py:330
  34.8 1.4 %collective-permute-start.9 = (f32[32,896]{1,0:T(8,128)S(1)}, f32[32,896]{1,0:T(8,128)S(1)}, u32[]{:S(2)}, u32[]{:S(2)}) collective-permute-start(f32[32,896]{1,0:T(8,128)S(1)} %get-tuple-element.20), channel_id=1, source_target_pairs={{0,1},{1,0},{2,3},{3,2},{4,5},{5,4},{6,7},{7,6},{8,9},{9,8},{10,11... | collective-permute-start | bytes 344072 | tf_op jit(solution)/shard_map/ppermute | solution.py:330

commit v6 on v5

--- a/solution.py
+++ b/solution.py
@@ -169,7 +169,7 @@
     )(me, *in_hbm)
 
 
-def nodes_kernel(devices, rows, me_ref, mine_ref, other_ref, out_ref, own_ref):
+def nodes_kernel(devices, rows, mine_ref, other_ref, out_ref):
     def part(start, size):
         at = slice(start, start + size)
         return mine_ref[at, :].astype(jnp.float32) + other_ref[at, :].astype(jnp.float32)
@@ -192,22 +192,15 @@
     ) / (1.0 + totals)
     scale = lax.rsqrt(jnp.mean(pooled * pooled, axis=-1, keepdims=True) + 1e-06)
     out_ref[...] = (pooled * scale).astype(jnp.bfloat16)
-    first = me_ref[0] // (devices // 2) * S_DEV
-    own_ref[...] = out_ref[pl.ds(pl.multiple_of(first, S_DEV), S_DEV), :]
-
-
-def run_nodes(devices, rows, me, mine, other):
+
+
+def run_nodes(devices, rows, mine, other):
     return pl.pallas_call(
         functools.partial(nodes_kernel, devices, rows),
-        in_specs=[pl.BlockSpec(memory_space=pltpu.SMEM)]
-        + [pl.BlockSpec(memory_space=pltpu.VMEM)] * 2,
-        out_shape=[
-            pltpu.VMEM((GROUP_ROWS, D), jnp.bfloat16),
-            pltpu.VMEM((S_DEV, D), jnp.bfloat16),
-        ],
+        out_shape=pltpu.VMEM((GROUP_ROWS, D), jnp.bfloat16),
         compiler_params=pltpu.CompilerParams(vmem_limit_bytes=8 * MIB),
         name="nodes",
-    )(me, *in_vmem(mine, other))
+    )(*in_vmem(mine, other))
 
 
 def in_vmem(*arrays):
@@ -220,17 +213,40 @@
     ).astype(jnp.bfloat16)
 
 
-def partial_kernel(own_ref, other_ref, proj_ref, *refs):
+def own_kernel(devices, me_ref, nodes_ref, proj_ref, query_ref, key_value_ref):
+    first = pl.multiple_of(me_ref[0] // (devices // 2) * S_DEV, S_DEV)
+    query_ref[...] = project(nodes_ref[pl.ds(first, S_DEV), :], proj_ref, 0, D)
+    key_value_ref[...] = project(nodes_ref[...], proj_ref, D, 2 * D)
+
+
+def run_own(devices, me, nodes, proj_weight):
+    return pl.pallas_call(
+        functools.partial(own_kernel, devices),
+        in_specs=[pl.BlockSpec(memory_space=pltpu.SMEM)]
+        + [pl.BlockSpec(memory_space=pltpu.VMEM)] * 2,
+        out_shape=[
+            pltpu.VMEM((S_DEV, D), jnp.bfloat16),
+            pltpu.VMEM((GROUP_ROWS, 2 * D), jnp.bfloat16),
+        ],
+        compiler_params=pltpu.CompilerParams(vmem_limit_bytes=12 * MIB),
+        cost_estimate=pl.CostEstimate(
+            flops=2 * (S_DEV + 2 * GROUP_ROWS) * D * D, bytes_accessed=6 * D * D, transcendentals=0
+        ),
+        name="own",
+    )(me, *in_vmem(nodes, proj_weight))
+
+
+def partial_kernel(own_ref, other_ref, own_key_value_ref, proj_ref, *refs):
     *pieces, mine_ref, theirs_ref, nodes_ref = refs
     start = 0
     for piece in pieces:
         nodes_ref[start : start + piece.shape[0], :] = piece[...]
         start += piece.shape[0]
-    queries = project(
-        jnp.concatenate([own_ref[...], other_ref[...]], axis=0), proj_ref, 0, D
-    )
-    keys = project(nodes_ref[...], proj_ref, D, D)
-    values = project(nodes_ref[...], proj_ref, 2 * D, D)
+    queries = jnp.concatenate([own_ref[...], other_ref[...]], axis=0)
+    key_value = jnp.concatenate(
+        [own_key_value_ref[...], project(nodes_ref[...], proj_ref, D, 2 * D)], axis=0
+    )
+    keys, values = key_value[:, :D], key_value[:, D:]
     rows = 2 * S_DEV
     lane = lax.broadcasted_iota(jnp.int32, (rows, LANES), 1)
     low = lane < DH
@@ -262,7 +278,7 @@
     theirs_ref[:, D:] = stats[S_DEV:]
 
 
-def run_partial(own, other, proj_weight, pieces):
+def run_partial(own, other, own_key_value, proj_weight, pieces):
     rows = sum(piece.shape[0] for piece in pieces)
     out = pltpu.VMEM((S_DEV, D + LANES), jnp.float32)
     return pl.pallas_call(
@@ -271,7 +287,7 @@
         scratch_shapes=[pltpu.VMEM((rows, D), jnp.bfloat16)],
         compiler_params=pltpu.CompilerParams(vmem_limit_bytes=12 * MIB + 24 * rows * D),
         name="partial",
-    )(*in_vmem(own, other, proj_weight, *pieces))
+    )(*in_vmem(own, other, own_key_value, proj_weight, *pieces))
 
 
 def merge_kernel(mine_ref, theirs_ref, gain_ref, out_ref):
@@ -351,7 +367,7 @@
         parts = [table[j * size : (j + 1) * size] for j in range(1 << take)]
         order = (2, 1, 3) if take == 2 else (1,)
         table = add_up(parts[0], *[swap(parts[j], j << (width + 1)) for j in order])
-    nodes, own = run_nodes(devices, rows, me, table, swap(table, devices // 2))
+    nodes = run_nodes(devices, rows, table, swap(table, devices // 2))
     pieces = [nodes]
     for take, width in groups[::-1]:
         pieces += [
@@ -359,9 +375,8 @@
             for j in ((3, 1, 2) if take == 2 else (1,))
             for piece in pieces
         ]
-    pieces[1], held = lax.optimization_barrier((pieces[1], own))
-    other = swap(held, 1)
-    mine, theirs = run_partial(own, other, proj_weight, pieces)
+    own, own_key_value = run_own(devices, me, nodes, proj_weight)
+    mine, theirs = run_partial(own, swap(own, 1), own_key_value, proj_weight, pieces[1:])
     return run_merge(mine, swap(theirs, 1), final_gain.reshape(1, D))
 
 

time: 37.3 us -> 36.4 us (0.976)
  waiting for transfers between devices: 15.5 us -> 14.4 us
    ppermute x10, waiting for transfers between devices: 15.5 us -> 14.4 us  [swap(): return lax.ppermute(array, 'blk', [(i, i ^ flip) for i in range(devices)])]
    pallas_call x1 -> x2, Pallas kernels: 0.28 us -> 1 us  [the longest x1 0.73 us: run_own(): pl.pallas_call(functools.partial(own_kernel, devices), in_specs=[pl.Block...]
    pallas_call x1, Pallas kernels: 1.56 us -> 1.05 us  [run_partial(): pl.pallas_call(partial_kernel, out_shape=[out, out], scratch_shapes=[pltp...]
  transfers between devices with their start and end apart: 10 -> 10, of which waited for: 10 -> 10; matrix products, arithmetic and copies ran while one was open for 0% -> 0% of each run, Pallas kernels for 0% -> 2%
where the time goes in v6:
time: 36.4 us; the launch traced here: 36.2 us
  waiting for transfers between devices  14.4 us (40%)
  starting transfers between devices  11.4 us (31%)
  Pallas kernels  10.1 us (28%)
    ppermute x10, waiting for transfers between devices, swap(): return lax.ppermute(array, 'blk', [(i, i ^ flip) for i in range(devices)])  14.4 us
    ppermute x10, starting transfers between devices, swap(): return lax.ppermute(array, 'blk', [(i, i ^ flip) for i in range(devices)])  11.4 us
    pallas_call x1, Pallas kernels, run_points(): pl.pallas_call(functools.partial(points_kernel, devices), in_specs=[pl.Bl...  7.02 us
    pallas_call x1, Pallas kernels, run_partial(): pl.pallas_call(partial_kernel, out_shape=[out, out], scratch_shapes=[pltp...  1.05 us
    pallas_call x1, Pallas kernels, run_merge(): pl.pallas_call(merge_kernel, out_shape=jax.ShapeDtypeStruct((S_DEV, D), j...  1 us
    pallas_call x1, Pallas kernels, run_own(): pl.pallas_call(functools.partial(own_kernel, devices), in_specs=[pl.Block...  0.73 us
  transfers between devices with their start and end apart: 10, of which 10 were waited for; matrix products, arithmetic and copies ran while one was open for 0% of the time, Pallas kernels for 2%

profile of v6, /device:TPU:0, one launch (start us, length us, event | category | flops | bytes accessed | tf_op | source)
XLA Modules:
  0.0 36.2 jit_solution(17037942875580245763)
XLA Ops:
  0.0 0.0 copy-start
  0.0 7.0 %points.1 = (bf16[1600,128]{1,0:T(8,128)(2,1)S(1)}, bf16[1600,128]{1,0:T(8,128)(2,1)S(1)}) custom-call(s32[1]{0:T(128)} %bitcast.me_ref, bf16[512,768]{1,0:T(8,128)(2,1)} %x_hbm.1, bf16[768,2560]{1,0:T(8,128)(2,1)} %hidden_hbm.1, bf16[2560,768]{1,0:T(8,128)(2,1)} %output_hbm.1, s32[1,512]{1,0:T(1,128)} %bitcast.4, s32[1,512]{1,0:T(1,128)} %bitcast.5, ...), custom_call_target="tpu_custom_call" | custom-call | tf_op jit(solution)/shard_map/points/pallas_call | solution.py:150
  7.0 0.5 %collective-permute-start = (bf16[1600,128]{1,0:T(8,128)(2,1)S(1)}, bf16[1600,128]{1,0:T(8,128)(2,1)S(1)}, u32[]{:S(2)}, u32[]{:S(2)}) collective-permute-start(bf16[1600,128]{1,0:T(8,128)(2,1)S(1)} %get-tuple-element.12), channel_id=1, source_target_pairs={{0,1},{1,0},{2,3},{3,2},{4,5},{5,4},{6,7},{7,6},{8,9},{9,8},{10,11... | collective-permute-start | bytes 1228808 | tf_op jit(solution)/shard_map/ppermute | solution.py:346
  7.5 1.4 %collective-permute-done = bf16[1600,128]{1,0:T(8,128)(2,1)S(1)} collective-permute-done((bf16[1600,128]{1,0:T(8,128)(2,1)S(1)}, bf16[1600,128]{1,0:T(8,128)(2,1)S(1)}, u32[]{:S(2)}, u32[]{:S(2)}) %collective-permute-start) | collective-permute-done | bytes 409632 | tf_op jit(solution)/shard_map/ppermute | solution.py:346
  8.9 0.1 add_convert_fusion
  9.1 3.0 %collective-permute-start.1 = (bf16[400,128]{1,0:T(8,128)(2,1)S(1)}, bf16[400,128]{1,0:T(8,128)(2,1)S(1)}, u32[]{:S(2)}, u32[]{:S(2)}) collective-permute-start(bf16[400,128]{1,0:T(8,128)(2,1)S(1)} %get-tuple-element.17), channel_id=1, source_target_pairs={{0,4},{1,5},{2,6},{3,7},{4,0},{5,1},{6,2},{7,3},{8,12},{9,13},{10,... | collective-permute-start | bytes 307208 | tf_op jit(solution)/shard_map/ppermute | solution.py:346
  12.1 1.5 %collective-permute-start.2 = (bf16[400,128]{1,0:T(8,128)(2,1)S(1)}, bf16[400,128]{1,0:T(8,128)(2,1)S(1)}, u32[]{:S(2)}, u32[]{:S(2)}) collective-permute-start(bf16[400,128]{1,0:T(8,128)(2,1)S(1)} %get-tuple-element.19), channel_id=1, source_target_pairs={{0,2},{1,3},{2,0},{3,1},{4,6},{5,7},{6,4},{7,5},{8,10},{9,11},{10,... | collective-permute-start | bytes 307208 | tf_op jit(solution)/shard_map/ppermute | solution.py:346
  13.6 0.0 collective-permute-start.3
  13.6 1.7 %collective-permute-done.1 = bf16[400,128]{1,0:T(8,128)(2,1)S(1)} collective-permute-done((bf16[400,128]{1,0:T(8,128)(2,1)S(1)}, bf16[400,128]{1,0:T(8,128)(2,1)S(1)}, u32[]{:S(2)}, u32[]{:S(2)}) %collective-permute-start.1) | collective-permute-done | bytes 102432 | tf_op jit(solution)/shard_map/ppermute | solution.py:346
  15.3 2.6 %collective-permute-done.2 = bf16[400,128]{1,0:T(8,128)(2,1)S(1)} collective-permute-done((bf16[400,128]{1,0:T(8,128)(2,1)S(1)}, bf16[400,128]{1,0:T(8,128)(2,1)S(1)}, u32[]{:S(2)}, u32[]{:S(2)}) %collective-permute-start.2) | collective-permute-done | bytes 102432 | tf_op jit(solution)/shard_map/ppermute | solution.py:346
  18.0 1.2 %collective-permute-done.3 = bf16[400,128]{1,0:T(8,128)(2,1)S(1)} collective-permute-done((bf16[400,128]{1,0:T(8,128)(2,1)S(1)}, bf16[400,128]{1,0:T(8,128)(2,1)S(1)}, u32[]{:S(2)}, u32[]{:S(2)}) %collective-permute-start.3) | collective-permute-done | bytes 102432 | tf_op jit(solution)/shard_map/ppermute | solution.py:346
  19.2 0.1 add_convert_fusion.1.mine_ref
  19.2 2.7 %collective-permute-start.4 = (bf16[400,128]{1,0:T(8,128)(2,1)S(1)}, bf16[400,128]{1,0:T(8,128)(2,1)S(1)}, u32[]{:S(2)}, u32[]{:S(2)}) collective-permute-start(bf16[400,128]{1,0:T(8,128)(2,1)S(1)} %add_convert_fusion.1.mine_ref), channel_id=1, source_target_pairs={{0,8},{1,9},{2,10},{3,11},{4,12},{5,13},{6,14},{7,15},{8,0},{9,1},... | collective-permute-start | bytes 307208 | tf_op jit(solution)/shard_map/ppermute | solution.py:346
  21.9 4.1 %collective-permute-done.4.other_ref = bf16[400,128]{1,0:T(8,128)(2,1)S(1)} collective-permute-done((bf16[400,128]{1,0:T(8,128)(2,1)S(1)}, bf16[400,128]{1,0:T(8,128)(2,1)S(1)}, u32[]{:S(2)}, u32[]{:S(2)}) %collective-permute-start.4) | collective-permute-done | bytes 102432 | tf_op jit(solution)/shard_map/ppermute | solution.py:346
  26.0 0.3 nodes.1.nodes_ref
  26.3 0.0 copy-start.1
  26.3 0.2 collective-permute-start.6
  26.5 1.7 %collective-permute-start.7 = (bf16[64,768]{1,0:T(8,128)(2,1)S(1)}, bf16[64,768]{1,0:T(8,128)(2,1)S(1)}, u32[]{:S(2)}, u32[]{:S(2)}) collective-permute-start(bf16[64,768]{1,0:T(8,128)(2,1)S(1)} %nodes.1.nodes_ref), channel_id=1, source_target_pairs={{0,2},{1,3},{2,0},{3,1},{4,6},{5,7},{6,4},{7,5},{8,10},{9,11},{10,... | collective-permute-start | bytes 294920 | tf_op jit(solution)/shard_map/ppermute | solution.py:346
  28.2 1.7 %collective-permute-start.8 = (bf16[64,768]{1,0:T(8,128)(2,1)S(1)}, bf16[64,768]{1,0:T(8,128)(2,1)S(1)}, u32[]{:S(2)}, u32[]{:S(2)}) collective-permute-start(bf16[64,768]{1,0:T(8,128)(2,1)S(1)} %nodes.1.nodes_ref), channel_id=1, source_target_pairs={{0,4},{1,5},{2,6},{3,7},{4,0},{5,1},{6,2},{7,3},{8,12},{9,13},{10,... | collective-permute-start | bytes 294920 | tf_op jit(solution)/shard_map/ppermute | solution.py:346
  29.8 0.0 copy-done
  29.8 0.7 %own.1 = (bf16[32,768]{1,0:T(8,128)(2,1)S(1)}, bf16[64,1536]{1,0:T(8,128)(2,1)S(1)}) custom-call(s32[1]{0:T(128)} %bitcast.me_ref, bf16[64,768]{1,0:T(8,128)(2,1)S(1)} %nodes.1.nodes_ref, bf16[768,2304]{1,0:T(8,128)(2,1)S(1)} %copy-done), custom_call_target="tpu_custom_call" | custom-call | flops 188743680 | bytes 3538944 | tf_op jit(solution)/shard_map/own/pallas_call | solution.py:223
  30.6 0.1 collective-permute-start.5
  30.7 1.2 %collective-permute-done.5.other_ref = bf16[32,768]{1,0:T(8,128)(2,1)S(1)} collective-permute-done((bf16[32,768]{1,0:T(8,128)(2,1)S(1)}, bf16[32,768]{1,0:T(8,128)(2,1)S(1)}, u32[]{:S(2)}, u32[]{:S(2)}) %collective-permute-start.5) | collective-permute-done | bytes 49184 | tf_op jit(solution)/shard_map/ppermute | solution.py:346
  31.9 0.1 collective-permute-done.6.refs_0_
  32.0 0.2 collective-permute-done.7.refs_1_
  32.2 0.6 %collective-permute-done.8.refs_2_ = bf16[64,768]{1,0:T(8,128)(2,1)S(1)} collective-permute-done((bf16[64,768]{1,0:T(8,128)(2,1)S(1)}, bf16[64,768]{1,0:T(8,128)(2,1)S(1)}, u32[]{:S(2)}, u32[]{:S(2)}) %collective-permute-start.8) | collective-permute-done | bytes 98336 | tf_op jit(solution)/shard_map/ppermute | solution.py:346
  32.8 1.0 %partial.1 = (f32[32,896]{1,0:T(8,128)S(1)}, f32[32,896]{1,0:T(8,128)S(1)}) custom-call(bf16[32,768]{1,0:T(8,128)(2,1)S(1)} %get-tuple-element.13.own_ref, bf16[32,768]{1,0:T(8,128)(2,1)S(1)} %collective-permute-done.5.other_ref, bf16[64,1536]{1,0:T(8,128)(2,1)S(1)} %get-tuple-element.14.own_key_value_ref, bf16[768,2304]{1,0:T(8,128)(2,1)S(1)} %copy-done, ...), custom_call_target="tpu_custom_call" | custom-call | tf_op jit(solution)/shard_map/partial/pallas_call | solution.py:284
  33.8 0.1 collective-permute-start.9
  33.9 0.0 copy-done.1
  33.9 1.3 %collective-permute-done.9.theirs_ref = f32[32,896]{1,0:T(8,128)S(1)} collective-permute-done((f32[32,896]{1,0:T(8,128)S(1)}, f32[32,896]{1,0:T(8,128)S(1)}, u32[]{:S(2)}, u32[]{:S(2)}) %collective-permute-start.9) | collective-permute-done | bytes 114720 | tf_op jit(solution)/shard_map/ppermute | solution.py:346
  35.2 1.0 %merge.1 = bf16[32,768]{1,0:T(8,128)(2,1)} custom-call(f32[32,896]{1,0:T(8,128)S(1)} %get-tuple-element.15.mine_ref, f32[32,896]{1,0:T(8,128)S(1)} %collective-permute-done.9.theirs_ref, bf16[1,768]{1,0:T(2,128)(2,1)S(1)} %reshape.19.gain_ref), custom_call_target="tpu_custom_call" | custom-call | tf_op jit(solution)/shard_map/merge/pallas_call | solution.py:316
  (2 shorter events, 0.0 us)
Async XLA Ops:
  0.0 29.8 %copy-start = (bf16[768,2304]{1,0:T(8,128)(2,1)S(1)}, bf16[768,2304]{1,0:T(8,128)(2,1)}, u32[]{:S(2)}) copy-start(bf16[768,2304]{1,0:T(8,128)(2,1)} %proj_ref.3) | copy-start | bytes 10616836
  7.0 1.9 %collective-permute-start = (bf16[1600,128]{1,0:T(8,128)(2,1)S(1)}, bf16[1600,128]{1,0:T(8,128)(2,1)S(1)}, u32[]{:S(2)}, u32[]{:S(2)}) collective-permute-start(bf16[1600,128]{1,0:T(8,128)(2,1)S(1)} %get-tuple-element.12), channel_id=1, source_target_pairs={{0,1},{1,0},{2,3},{3,2},{4,5},{5,4},{6,7},{7,6},{8,9},{9,8},{10,11... | collective-permute-start | bytes 1228808 | tf_op jit(solution)/shard_map/ppermute | solution.py:346
  9.1 6.3 %collective-permute-start.1 = (bf16[400,128]{1,0:T(8,128)(2,1)S(1)}, bf16[400,128]{1,0:T(8,128)(2,1)S(1)}, u32[]{:S(2)}, u32[]{:S(2)}) collective-permute-start(bf16[400,128]{1,0:T(8,128)(2,1)S(1)} %get-tuple-element.17), channel_id=1, source_target_pairs={{0,4},{1,5},{2,6},{3,7},{4,0},{5,1},{6,2},{7,3},{8,12},{9,13},{10,... | collective-permute-start | bytes 307208 | tf_op jit(solution)/shard_map/ppermute | solution.py:346
  12.1 5.9 %collective-permute-start.2 = (bf16[400,128]{1,0:T(8,128)(2,1)S(1)}, bf16[400,128]{1,0:T(8,128)(2,1)S(1)}, u32[]{:S(2)}, u32[]{:S(2)}) collective-permute-start(bf16[400,128]{1,0:T(8,128)(2,1)S(1)} %get-tuple-element.19), channel_id=1, source_target_pairs={{0,2},{1,3},{2,0},{3,1},{4,6},{5,7},{6,4},{7,5},{8,10},{9,11},{10,... | collective-permute-start | bytes 307208 | tf_op jit(solution)/shard_map/ppermute | solution.py:346
  13.6 5.6 %collective-permute-start.3 = (bf16[400,128]{1,0:T(8,128)(2,1)S(1)}, bf16[400,128]{1,0:T(8,128)(2,1)S(1)}, u32[]{:S(2)}, u32[]{:S(2)}) collective-permute-start(bf16[400,128]{1,0:T(8,128)(2,1)S(1)} %get-tuple-element.18), channel_id=1, source_target_pairs={{0,6},{1,7},{2,4},{3,5},{4,2},{5,3},{6,0},{7,1},{8,14},{9,15},{10,... | collective-permute-start | bytes 307208 | tf_op jit(solution)/shard_map/ppermute | solution.py:346
  19.2 6.8 %collective-permute-start.4 = (bf16[400,128]{1,0:T(8,128)(2,1)S(1)}, bf16[400,128]{1,0:T(8,128)(2,1)S(1)}, u32[]{:S(2)}, u32[]{:S(2)}) collective-permute-start(bf16[400,128]{1,0:T(8,128)(2,1)S(1)} %add_convert_fusion.1.mine_ref), channel_id=1, source_target_pairs={{0,8},{1,9},{2,10},{3,11},{4,12},{5,13},{6,14},{7,15},{8,0},{9,1},... | collective-permute-start | bytes 307208 | tf_op jit(solution)/shard_map/ppermute | solution.py:346
  26.3 7.6 %copy-start.1 = (bf16[768]{0:T(1024)(128)(2,1)S(1)}, bf16[768]{0:T(1024)(128)(2,1)}, u32[]{:S(2)}) copy-start(bf16[768]{0:T(1024)(128)(2,1)} %param.15) | copy-start | bytes 4612
  26.3 5.7 %collective-permute-start.6 = (bf16[64,768]{1,0:T(8,128)(2,1)S(1)}, bf16[64,768]{1,0:T(8,128)(2,1)S(1)}, u32[]{:S(2)}, u32[]{:S(2)}) collective-permute-start(bf16[64,768]{1,0:T(8,128)(2,1)S(1)} %nodes.1.nodes_ref), channel_id=1, source_target_pairs={{0,6},{1,7},{2,4},{3,5},{4,2},{5,3},{6,0},{7,1},{8,14},{9,15},{10,... | collective-permute-start | bytes 294920 | tf_op jit(solution)/shard_map/ppermute | solution.py:346
  26.5 5.7 %collective-permute-start.7 = (bf16[64,768]{1,0:T(8,128)(2,1)S(1)}, bf16[64,768]{1,0:T(8,128)(2,1)S(1)}, u32[]{:S(2)}, u32[]{:S(2)}) collective-permute-start(bf16[64,768]{1,0:T(8,128)(2,1)S(1)} %nodes.1.nodes_ref), channel_id=1, source_target_pairs={{0,2},{1,3},{2,0},{3,1},{4,6},{5,7},{6,4},{7,5},{8,10},{9,11},{10,... | collective-permute-start | bytes 294920 | tf_op jit(solution)/shard_map/ppermute | solution.py:346
  28.2 4.6 %collective-permute-start.8 = (bf16[64,768]{1,0:T(8,128)(2,1)S(1)}, bf16[64,768]{1,0:T(8,128)(2,1)S(1)}, u32[]{:S(2)}, u32[]{:S(2)}) collective-permute-start(bf16[64,768]{1,0:T(8,128)(2,1)S(1)} %nodes.1.nodes_ref), channel_id=1, source_target_pairs={{0,4},{1,5},{2,6},{3,7},{4,0},{5,1},{6,2},{7,3},{8,12},{9,13},{10,... | collective-permute-start | bytes 294920 | tf_op jit(solution)/shard_map/ppermute | solution.py:346
  30.6 1.3 %collective-permute-start.5 = (bf16[32,768]{1,0:T(8,128)(2,1)S(1)}, bf16[32,768]{1,0:T(8,128)(2,1)S(1)}, u32[]{:S(2)}, u32[]{:S(2)}) collective-permute-start(bf16[32,768]{1,0:T(8,128)(2,1)S(1)} %get-tuple-element.13.own_ref), channel_id=1, source_target_pairs={{0,1},{1,0},{2,3},{3,2},{4,5},{5,4},{6,7},{7,6},{8,9},{9,8},{10,11... | collective-permute-start | bytes 147464 | tf_op jit(solution)/shard_map/ppermute | solution.py:346
  33.8 1.4 %collective-permute-start.9 = (f32[32,896]{1,0:T(8,128)S(1)}, f32[32,896]{1,0:T(8,128)S(1)}, u32[]{:S(2)}, u32[]{:S(2)}) collective-permute-start(f32[32,896]{1,0:T(8,128)S(1)} %get-tuple-element.16), channel_id=1, source_target_pairs={{0,1},{1,0},{2,3},{3,2},{4,5},{5,4},{6,7},{7,6},{8,9},{9,8},{10,11... | collective-permute-start | bytes 344072 | tf_op jit(solution)/shard_map/ppermute | solution.py:346

commit v7 on v6

--- a/solution.py
+++ b/solution.py
@@ -39,7 +39,7 @@
 
 def points_kernel(
     devices, me_ref, x_hbm, hidden_hbm, output_hbm, owner_hbm, node_hbm, weight_hbm,
-    send_ref, keep_ref, owner_ref, node_ref, weight_ref, x_ref, normed_ref, hidden_ref, output_ref, coeffs_ref, middle_ref, sems,
+    send_ref, features_ref, kept_ref, tiles_ref, owner_ref, node_ref, weight_ref, x_ref, normed_ref, hidden_ref, output_ref, coeffs_ref, middle_ref, sems,
 ):
     rows = x_ref.shape[0]
     ff = hidden_ref.shape[1]
@@ -66,11 +66,6 @@
 
     chunks = devices // 4
     half = chunks * GROUP_ROWS
-    places = [
-        (out_ref, chunk * CHUNK, core * half + chunk * GROUP_ROWS)
-        for core, out_ref in ((0, keep_ref), (1, send_ref))
-        for chunk in range(chunks)
-    ]
     me = me_ref[0]
 
     @pl.when(me >= 0)
@@ -84,23 +79,26 @@
         coeffs = jnp.where(
             row_of == lax.broadcasted_iota(jnp.int32, (2 * half, rows), 0), weight_ref[...], 0
         ).astype(jnp.float32)
-        coeffs_ref[...] = coeffs.astype(jnp.bfloat16)
+        kept_ref[...] = coeffs[:half].astype(jnp.bfloat16)
+        coeffs_ref[...] = coeffs[half:].astype(jnp.bfloat16)
         totals = jnp.sum(coeffs, axis=1, keepdims=True).astype(jnp.int32)
         shift = digit_bits(devices)
         digits = -(-total_bits(rows) // shift)
         lane = lax.broadcasted_iota(jnp.int32, (TOTAL_ROWS, LANES), 1)
         digit = lane % LANES_PER_GROUP
         held = jnp.where(digit < digits, digit * shift, 31)
-        for out_ref, base, first in places:
+        for chunk in range(2 * chunks):
             tile = jnp.zeros((TOTAL_ROWS, LANES), jnp.int32)
             for group in range(GROUP_ROWS // TOTAL_ROWS):
-                start = first + group * TOTAL_ROWS
+                start = chunk * GROUP_ROWS + group * TOTAL_ROWS
                 value = jnp.broadcast_to(totals[start : start + TOTAL_ROWS], (TOTAL_ROWS, LANES))
                 tile = jnp.where(lane // LANES_PER_GROUP == group, value, tile)
-            tile = (tile >> held) & ((1 << shift) - 1)
-            out_ref[base + COLS * GROUP_ROWS : base + CHUNK, :] = tile.astype(
-                jnp.float32
-            ).astype(jnp.bfloat16)
+            tile = ((tile >> held) & ((1 << shift) - 1)).astype(jnp.float32).astype(jnp.bfloat16)
+            if chunk < chunks:
+                tiles_ref[chunk * TOTAL_ROWS : (chunk + 1) * TOTAL_ROWS, :] = tile
+            else:
+                end = (chunk - chunks + 1) * CHUNK
+                send_ref[end - TOTAL_ROWS : end, :] = tile
 
     x_copy.wait()
     x = x_ref[...].astype(jnp.float32)
@@ -127,14 +125,42 @@
             x_ref[at, :].astype(jnp.float32)
             + jnp.dot(middle_ref[at, :], output_ref[...], preferred_element_type=jnp.float32)
         ).astype(jnp.bfloat16)
+        features_ref[at, :] = features
         term = jnp.dot(coeffs_ref[:, at], features, preferred_element_type=jnp.float32)
         sums = term if sums is None else sums + term
-    sums = sums.astype(jnp.bfloat16)
-    for out_ref, base, first in places:
+    store_table(send_ref, sums.astype(jnp.bfloat16))
+
+
+def store_table(out_ref, sums):
+    for first in range(0, sums.shape[0], GROUP_ROWS):
         for col in range(COLS):
-            out_ref[base + col * GROUP_ROWS : base + (col + 1) * GROUP_ROWS, :] = sums[
+            at = first // GROUP_ROWS * CHUNK + col * GROUP_ROWS
+            out_ref[at : at + GROUP_ROWS, :] = sums[
                 first : first + GROUP_ROWS, col * LANES : (col + 1) * LANES
             ]
+
+
+def keep_kernel(features_ref, kept_ref, tiles_ref, out_ref):
+    sums = jnp.dot(kept_ref[...], features_ref[...], preferred_element_type=jnp.float32)
+    store_table(out_ref, sums.astype(jnp.bfloat16))
+    for chunk in range(tiles_ref.shape[0] // TOTAL_ROWS):
+        end = (chunk + 1) * CHUNK
+        out_ref[end - TOTAL_ROWS : end, :] = tiles_ref[
+            chunk * TOTAL_ROWS : (chunk + 1) * TOTAL_ROWS, :
+        ]
+
+
+def run_keep(features, kept, tiles):
+    nodes, rows = kept.shape
+    return pl.pallas_call(
+        keep_kernel,
+        out_shape=pltpu.VMEM((nodes // GROUP_ROWS * CHUNK, LANES), jnp.bfloat16),
+        compiler_params=pltpu.CompilerParams(vmem_limit_bytes=8 * MIB + 16 * nodes * D),
+        cost_estimate=pl.CostEstimate(
+            flops=2 * nodes * rows * D, bytes_accessed=4 * nodes * D, transcendentals=0
+        ),
+        name="keep",
+    )(*in_vmem(features, kept, tiles))
 
 
 def run_points(devices, me, x, hidden_weight, output_weight, owner, node, weight):
@@ -150,8 +176,13 @@
     return pl.pallas_call(
         functools.partial(points_kernel, devices),
         in_specs=[pl.BlockSpec(memory_space=pltpu.SMEM)] + [hbm] * 6,
-        out_specs=[vmem, vmem],
-        out_shape=[out, out],
+        out_specs=[vmem] * 4,
+        out_shape=[
+            out,
+            pltpu.VMEM((rows, D), jnp.bfloat16),
+            pltpu.VMEM((nodes // 2, rows), jnp.bfloat16),
+            pltpu.VMEM((devices // 4 * TOTAL_ROWS, LANES), jnp.bfloat16),
+        ],
         scratch_shapes=[
             pltpu.VMEM((1, rows), jnp.int32),
             pltpu.VMEM((1, rows), jnp.int32),
@@ -160,7 +191,7 @@
             pltpu.VMEM((rows, D), jnp.bfloat16),
             pltpu.VMEM((D, ff), jnp.bfloat16),
             pltpu.VMEM((ff, D), jnp.bfloat16),
-            pltpu.VMEM((nodes, rows), jnp.bfloat16),
+            pltpu.VMEM((nodes // 2, rows), jnp.bfloat16),
             pltpu.VMEM((rows, ff), jnp.bfloat16),
             pltpu.SemaphoreType.DMA((5 + len(hidden_parts(ff)),)),
         ],
@@ -345,7 +376,7 @@
     def swap(array, flip):
         return lax.ppermute(array, "blk", [(i, i ^ flip) for i in range(devices)])
 
-    send, keep = run_points(
+    send, *kept = run_points(
         devices,
         me,
         points_in,
@@ -355,7 +386,7 @@
         point_node.reshape(1, rows),
         point_weight.reshape(1, rows),
     )
-    table = add_up(keep, swap(send, 1))
+    table = add_up(run_keep(*kept), swap(send, 1))
     groups = []
     width = (devices // 4).bit_length() - 1
     while width > 0:

time: 36.4 us -> 36.1 us (level)
    ppermute x10, waiting for transfers between devices: 14.4 us -> 14.1 us  [swap(): return lax.ppermute(array, 'blk', [(i, i ^ flip) for i in range(devices)])]
    pallas_call x0 -> x1, Pallas kernels: none -> 0.37 us  [run_keep(): pl.pallas_call(keep_kernel, out_shape=pltpu.VMEM((nodes // GROUP_ROWS * C...]
  transfers between devices with their start and end apart: 10 -> 10, of which waited for: 10 -> 10; matrix products, arithmetic and copies ran while one was open for 0% -> 0% of each run, Pallas kernels for 2% -> 3%
where the time goes in v7:
time: 36.1 us; the launch traced here: 36 us
  waiting for transfers between devices  14.1 us (39%)
  starting transfers between devices  11.4 us (32%)
  Pallas kernels  10.2 us (28%)
    ppermute x10, waiting for transfers between devices, swap(): return lax.ppermute(array, 'blk', [(i, i ^ flip) for i in range(devices)])  14.1 us
    ppermute x10, starting transfers between devices, swap(): return lax.ppermute(array, 'blk', [(i, i ^ flip) for i in range(devices)])  11.4 us
    pallas_call x1, Pallas kernels, run_points(): pl.pallas_call(functools.partial(points_kernel, devices), in_specs=[pl.Bl...  6.76 us
    pallas_call x1, Pallas kernels, run_partial(): pl.pallas_call(partial_kernel, out_shape=[out, out], scratch_shapes=[pltp...  1.04 us
    pallas_call x1, Pallas kernels, run_merge(): pl.pallas_call(merge_kernel, out_shape=jax.ShapeDtypeStruct((S_DEV, D), j...  1 us
    pallas_call x1, Pallas kernels, run_own(): pl.pallas_call(functools.partial(own_kernel, devices), in_specs=[pl.Block...  0.73 us
  transfers between devices with their start and end apart: 10, of which 10 were waited for; matrix products, arithmetic and copies ran while one was open for 0% of the time, Pallas kernels for 3%

profile of v7, /device:TPU:0, one launch (start us, length us, event | category | flops | bytes accessed | tf_op | source)
XLA Modules:
  0.0 36.0 jit_solution(2517208485874219785)
XLA Ops:
  0.0 6.8 %points.1 = (bf16[1600,128]{1,0:T(8,128)(2,1)S(1)}, bf16[512,768]{1,0:T(8,128)(2,1)S(1)}, bf16[256,512]{1,0:T(8,128)(2,1)S(1)}, bf16[64,128]{1,0:T(8,128)(2,1)S(1)}) custom-call(s32[1]{0:T(128)} %bitcast.me_ref, bf16[512,768]{1,0:T(8,128)(2,1)} %x_hbm.1, bf16[768,2560]{1,0:T(8,128)(2,1)} %hidden_hbm.1, bf16[2560,768]{1,0:T(8,128)(2,1)} %output_hbm.1, ...), custom_call_target="tpu_custom_call" | custom-call | tf_op jit(solution)/shard_map/points/pallas_call | solution.py:176
  6.8 0.0 copy-start
  6.8 0.5 %collective-permute-start = (bf16[1600,128]{1,0:T(8,128)(2,1)S(1)}, bf16[1600,128]{1,0:T(8,128)(2,1)S(1)}, u32[]{:S(2)}, u32[]{:S(2)}) collective-permute-start(bf16[1600,128]{1,0:T(8,128)(2,1)S(1)} %get-tuple-element.16), channel_id=1, source_target_pairs={{0,1},{1,0},{2,3},{3,2},{4,5},{5,4},{6,7},{7,6},{8,9},{9,8},{10,11... | collective-permute-start | bytes 1228808 | tf_op jit(solution)/shard_map/ppermute | solution.py:377
  7.3 0.4 %keep.1 = bf16[1600,128]{1,0:T(8,128)(2,1)S(1)} custom-call(bf16[512,768]{1,0:T(8,128)(2,1)S(1)} %get-tuple-element.13.features_ref, bf16[256,512]{1,0:T(8,128)(2,1)S(1)} %get-tuple-element.14.kept_ref, bf16[64,128]{1,0:T(8,128)(2,1)S(1)} %get-tuple-element.15.tiles_ref), custom_call_target="tpu_custom_call" | custom-call | flops 201326592 | bytes 786432 | tf_op jit(solution)/shard_map/keep/pallas_call | solution.py:155
  7.7 1.0 %collective-permute-done = bf16[1600,128]{1,0:T(8,128)(2,1)S(1)} collective-permute-done((bf16[1600,128]{1,0:T(8,128)(2,1)S(1)}, bf16[1600,128]{1,0:T(8,128)(2,1)S(1)}, u32[]{:S(2)}, u32[]{:S(2)}) %collective-permute-start) | collective-permute-done | bytes 409632 | tf_op jit(solution)/shard_map/ppermute | solution.py:377
  8.7 0.1 add_convert_fusion
  8.8 3.0 %collective-permute-start.1 = (bf16[400,128]{1,0:T(8,128)(2,1)S(1)}, bf16[400,128]{1,0:T(8,128)(2,1)S(1)}, u32[]{:S(2)}, u32[]{:S(2)}) collective-permute-start(bf16[400,128]{1,0:T(8,128)(2,1)S(1)} %get-tuple-element.21), channel_id=1, source_target_pairs={{0,4},{1,5},{2,6},{3,7},{4,0},{5,1},{6,2},{7,3},{8,12},{9,13},{10,... | collective-permute-start | bytes 307208 | tf_op jit(solution)/shard_map/ppermute | solution.py:377
  11.8 1.5 %collective-permute-start.2 = (bf16[400,128]{1,0:T(8,128)(2,1)S(1)}, bf16[400,128]{1,0:T(8,128)(2,1)S(1)}, u32[]{:S(2)}, u32[]{:S(2)}) collective-permute-start(bf16[400,128]{1,0:T(8,128)(2,1)S(1)} %get-tuple-element.23), channel_id=1, source_target_pairs={{0,2},{1,3},{2,0},{3,1},{4,6},{5,7},{6,4},{7,5},{8,10},{9,11},{10,... | collective-permute-start | bytes 307208 | tf_op jit(solution)/shard_map/ppermute | solution.py:377
  13.3 0.0 collective-permute-start.3
  13.4 1.7 %collective-permute-done.1 = bf16[400,128]{1,0:T(8,128)(2,1)S(1)} collective-permute-done((bf16[400,128]{1,0:T(8,128)(2,1)S(1)}, bf16[400,128]{1,0:T(8,128)(2,1)S(1)}, u32[]{:S(2)}, u32[]{:S(2)}) %collective-permute-start.1) | collective-permute-done | bytes 102432 | tf_op jit(solution)/shard_map/ppermute | solution.py:377
  15.1 2.6 %collective-permute-done.2 = bf16[400,128]{1,0:T(8,128)(2,1)S(1)} collective-permute-done((bf16[400,128]{1,0:T(8,128)(2,1)S(1)}, bf16[400,128]{1,0:T(8,128)(2,1)S(1)}, u32[]{:S(2)}, u32[]{:S(2)}) %collective-permute-start.2) | collective-permute-done | bytes 102432 | tf_op jit(solution)/shard_map/ppermute | solution.py:377
  17.7 1.2 %collective-permute-done.3 = bf16[400,128]{1,0:T(8,128)(2,1)S(1)} collective-permute-done((bf16[400,128]{1,0:T(8,128)(2,1)S(1)}, bf16[400,128]{1,0:T(8,128)(2,1)S(1)}, u32[]{:S(2)}, u32[]{:S(2)}) %collective-permute-start.3) | collective-permute-done | bytes 102432 | tf_op jit(solution)/shard_map/ppermute | solution.py:377
  18.9 0.1 add_convert_fusion.1.mine_ref
  19.0 2.7 %collective-permute-start.4 = (bf16[400,128]{1,0:T(8,128)(2,1)S(1)}, bf16[400,128]{1,0:T(8,128)(2,1)S(1)}, u32[]{:S(2)}, u32[]{:S(2)}) collective-permute-start(bf16[400,128]{1,0:T(8,128)(2,1)S(1)} %add_convert_fusion.1.mine_ref), channel_id=1, source_target_pairs={{0,8},{1,9},{2,10},{3,11},{4,12},{5,13},{6,14},{7,15},{8,0},{9,1},... | collective-permute-start | bytes 307208 | tf_op jit(solution)/shard_map/ppermute | solution.py:377
  21.6 4.1 %collective-permute-done.4.other_ref = bf16[400,128]{1,0:T(8,128)(2,1)S(1)} collective-permute-done((bf16[400,128]{1,0:T(8,128)(2,1)S(1)}, bf16[400,128]{1,0:T(8,128)(2,1)S(1)}, u32[]{:S(2)}, u32[]{:S(2)}) %collective-permute-start.4) | collective-permute-done | bytes 102432 | tf_op jit(solution)/shard_map/ppermute | solution.py:377
  25.7 0.3 nodes.1.nodes_ref
  26.0 0.0 copy-start.1
  26.0 0.2 collective-permute-start.6
  26.2 1.7 %collective-permute-start.7 = (bf16[64,768]{1,0:T(8,128)(2,1)S(1)}, bf16[64,768]{1,0:T(8,128)(2,1)S(1)}, u32[]{:S(2)}, u32[]{:S(2)}) collective-permute-start(bf16[64,768]{1,0:T(8,128)(2,1)S(1)} %nodes.1.nodes_ref), channel_id=1, source_target_pairs={{0,2},{1,3},{2,0},{3,1},{4,6},{5,7},{6,4},{7,5},{8,10},{9,11},{10,... | collective-permute-start | bytes 294920 | tf_op jit(solution)/shard_map/ppermute | solution.py:377
  27.9 1.7 %collective-permute-start.8 = (bf16[64,768]{1,0:T(8,128)(2,1)S(1)}, bf16[64,768]{1,0:T(8,128)(2,1)S(1)}, u32[]{:S(2)}, u32[]{:S(2)}) collective-permute-start(bf16[64,768]{1,0:T(8,128)(2,1)S(1)} %nodes.1.nodes_ref), channel_id=1, source_target_pairs={{0,4},{1,5},{2,6},{3,7},{4,0},{5,1},{6,2},{7,3},{8,12},{9,13},{10,... | collective-permute-start | bytes 294920 | tf_op jit(solution)/shard_map/ppermute | solution.py:377
  29.6 0.0 copy-done
  29.6 0.7 %own.1 = (bf16[32,768]{1,0:T(8,128)(2,1)S(1)}, bf16[64,1536]{1,0:T(8,128)(2,1)S(1)}) custom-call(s32[1]{0:T(128)} %bitcast.me_ref, bf16[64,768]{1,0:T(8,128)(2,1)S(1)} %nodes.1.nodes_ref, bf16[768,2304]{1,0:T(8,128)(2,1)S(1)} %copy-done), custom_call_target="tpu_custom_call" | custom-call | flops 188743680 | bytes 3538944 | tf_op jit(solution)/shard_map/own/pallas_call | solution.py:254
  30.3 0.1 collective-permute-start.5
  30.4 1.2 %collective-permute-done.5.other_ref = bf16[32,768]{1,0:T(8,128)(2,1)S(1)} collective-permute-done((bf16[32,768]{1,0:T(8,128)(2,1)S(1)}, bf16[32,768]{1,0:T(8,128)(2,1)S(1)}, u32[]{:S(2)}, u32[]{:S(2)}) %collective-permute-start.5) | collective-permute-done | bytes 49184 | tf_op jit(solution)/shard_map/ppermute | solution.py:377
  31.6 0.1 collective-permute-done.6.refs_0_
  31.7 0.2 collective-permute-done.7.refs_1_
  31.9 0.6 %collective-permute-done.8.refs_2_ = bf16[64,768]{1,0:T(8,128)(2,1)S(1)} collective-permute-done((bf16[64,768]{1,0:T(8,128)(2,1)S(1)}, bf16[64,768]{1,0:T(8,128)(2,1)S(1)}, u32[]{:S(2)}, u32[]{:S(2)}) %collective-permute-start.8) | collective-permute-done | bytes 98336 | tf_op jit(solution)/shard_map/ppermute | solution.py:377
  32.5 1.0 %partial.1 = (f32[32,896]{1,0:T(8,128)S(1)}, f32[32,896]{1,0:T(8,128)S(1)}) custom-call(bf16[32,768]{1,0:T(8,128)(2,1)S(1)} %get-tuple-element.17.own_ref, bf16[32,768]{1,0:T(8,128)(2,1)S(1)} %collective-permute-done.5.other_ref, bf16[64,1536]{1,0:T(8,128)(2,1)S(1)} %get-tuple-element.18.own_key_value_ref, bf16[768,2304]{1,0:T(8,128)(2,1)S(1)} %copy-done, ...), custom_call_target="tpu_custom_call" | custom-call | tf_op jit(solution)/shard_map/partial/pallas_call | solution.py:315
  33.6 0.1 collective-permute-start.9
  33.7 0.0 copy-done.1
  33.7 1.3 %collective-permute-done.9.theirs_ref = f32[32,896]{1,0:T(8,128)S(1)} collective-permute-done((f32[32,896]{1,0:T(8,128)S(1)}, f32[32,896]{1,0:T(8,128)S(1)}, u32[]{:S(2)}, u32[]{:S(2)}) %collective-permute-start.9) | collective-permute-done | bytes 114720 | tf_op jit(solution)/shard_map/ppermute | solution.py:377
  35.0 1.0 %merge.1 = bf16[32,768]{1,0:T(8,128)(2,1)} custom-call(f32[32,896]{1,0:T(8,128)S(1)} %get-tuple-element.19.mine_ref, f32[32,896]{1,0:T(8,128)S(1)} %collective-permute-done.9.theirs_ref, bf16[1,768]{1,0:T(2,128)(2,1)S(1)} %reshape.19.gain_ref), custom_call_target="tpu_custom_call" | custom-call | tf_op jit(solution)/shard_map/merge/pallas_call | solution.py:347
  (2 shorter events, 0.0 us)
Async XLA Ops:
  6.8 22.8 %copy-start = (bf16[768,2304]{1,0:T(8,128)(2,1)S(1)}, bf16[768,2304]{1,0:T(8,128)(2,1)}, u32[]{:S(2)}) copy-start(bf16[768,2304]{1,0:T(8,128)(2,1)} %proj_ref.3) | copy-start | bytes 10616836
  6.8 1.9 %collective-permute-start = (bf16[1600,128]{1,0:T(8,128)(2,1)S(1)}, bf16[1600,128]{1,0:T(8,128)(2,1)S(1)}, u32[]{:S(2)}, u32[]{:S(2)}) collective-permute-start(bf16[1600,128]{1,0:T(8,128)(2,1)S(1)} %get-tuple-element.16), channel_id=1, source_target_pairs={{0,1},{1,0},{2,3},{3,2},{4,5},{5,4},{6,7},{7,6},{8,9},{9,8},{10,11... | collective-permute-start | bytes 1228808 | tf_op jit(solution)/shard_map/ppermute | solution.py:377
  8.8 6.2 %collective-permute-start.1 = (bf16[400,128]{1,0:T(8,128)(2,1)S(1)}, bf16[400,128]{1,0:T(8,128)(2,1)S(1)}, u32[]{:S(2)}, u32[]{:S(2)}) collective-permute-start(bf16[400,128]{1,0:T(8,128)(2,1)S(1)} %get-tuple-element.21), channel_id=1, source_target_pairs={{0,4},{1,5},{2,6},{3,7},{4,0},{5,1},{6,2},{7,3},{8,12},{9,13},{10,... | collective-permute-start | bytes 307208 | tf_op jit(solution)/shard_map/ppermute | solution.py:377
  11.8 5.9 %collective-permute-start.2 = (bf16[400,128]{1,0:T(8,128)(2,1)S(1)}, bf16[400,128]{1,0:T(8,128)(2,1)S(1)}, u32[]{:S(2)}, u32[]{:S(2)}) collective-permute-start(bf16[400,128]{1,0:T(8,128)(2,1)S(1)} %get-tuple-element.23), channel_id=1, source_target_pairs={{0,2},{1,3},{2,0},{3,1},{4,6},{5,7},{6,4},{7,5},{8,10},{9,11},{10,... | collective-permute-start | bytes 307208 | tf_op jit(solution)/shard_map/ppermute | solution.py:377
  13.3 5.6 %collective-permute-start.3 = (bf16[400,128]{1,0:T(8,128)(2,1)S(1)}, bf16[400,128]{1,0:T(8,128)(2,1)S(1)}, u32[]{:S(2)}, u32[]{:S(2)}) collective-permute-start(bf16[400,128]{1,0:T(8,128)(2,1)S(1)} %get-tuple-element.22), channel_id=1, source_target_pairs={{0,6},{1,7},{2,4},{3,5},{4,2},{5,3},{6,0},{7,1},{8,14},{9,15},{10,... | collective-permute-start | bytes 307208 | tf_op jit(solution)/shard_map/ppermute | solution.py:377
  19.0 6.8 %collective-permute-start.4 = (bf16[400,128]{1,0:T(8,128)(2,1)S(1)}, bf16[400,128]{1,0:T(8,128)(2,1)S(1)}, u32[]{:S(2)}, u32[]{:S(2)}) collective-permute-start(bf16[400,128]{1,0:T(8,128)(2,1)S(1)} %add_convert_fusion.1.mine_ref), channel_id=1, source_target_pairs={{0,8},{1,9},{2,10},{3,11},{4,12},{5,13},{6,14},{7,15},{8,0},{9,1},... | collective-permute-start | bytes 307208 | tf_op jit(solution)/shard_map/ppermute | solution.py:377
  26.0 7.6 %copy-start.1 = (bf16[768]{0:T(1024)(128)(2,1)S(1)}, bf16[768]{0:T(1024)(128)(2,1)}, u32[]{:S(2)}) copy-start(bf16[768]{0:T(1024)(128)(2,1)} %param.15) | copy-start | bytes 4612
  26.0 5.7 %collective-permute-start.6 = (bf16[64,768]{1,0:T(8,128)(2,1)S(1)}, bf16[64,768]{1,0:T(8,128)(2,1)S(1)}, u32[]{:S(2)}, u32[]{:S(2)}) collective-permute-start(bf16[64,768]{1,0:T(8,128)(2,1)S(1)} %nodes.1.nodes_ref), channel_id=1, source_target_pairs={{0,6},{1,7},{2,4},{3,5},{4,2},{5,3},{6,0},{7,1},{8,14},{9,15},{10,... | collective-permute-start | bytes 294920 | tf_op jit(solution)/shard_map/ppermute | solution.py:377
  26.2 5.7 %collective-permute-start.7 = (bf16[64,768]{1,0:T(8,128)(2,1)S(1)}, bf16[64,768]{1,0:T(8,128)(2,1)S(1)}, u32[]{:S(2)}, u32[]{:S(2)}) collective-permute-start(bf16[64,768]{1,0:T(8,128)(2,1)S(1)} %nodes.1.nodes_ref), channel_id=1, source_target_pairs={{0,2},{1,3},{2,0},{3,1},{4,6},{5,7},{6,4},{7,5},{8,10},{9,11},{10,... | collective-permute-start | bytes 294920 | tf_op jit(solution)/shard_map/ppermute | solution.py:377
  27.9 4.6 %collective-permute-start.8 = (bf16[64,768]{1,0:T(8,128)(2,1)S(1)}, bf16[64,768]{1,0:T(8,128)(2,1)S(1)}, u32[]{:S(2)}, u32[]{:S(2)}) collective-permute-start(bf16[64,768]{1,0:T(8,128)(2,1)S(1)} %nodes.1.nodes_ref), channel_id=1, source_target_pairs={{0,4},{1,5},{2,6},{3,7},{4,0},{5,1},{6,2},{7,3},{8,12},{9,13},{10,... | collective-permute-start | bytes 294920 | tf_op jit(solution)/shard_map/ppermute | solution.py:377
  30.3 1.3 %collective-permute-start.5 = (bf16[32,768]{1,0:T(8,128)(2,1)S(1)}, bf16[32,768]{1,0:T(8,128)(2,1)S(1)}, u32[]{:S(2)}, u32[]{:S(2)}) collective-permute-start(bf16[32,768]{1,0:T(8,128)(2,1)S(1)} %get-tuple-element.17.own_ref), channel_id=1, source_target_pairs={{0,1},{1,0},{2,3},{3,2},{4,5},{5,4},{6,7},{7,6},{8,9},{9,8},{10,11... | collective-permute-start | bytes 147464 | tf_op jit(solution)/shard_map/ppermute | solution.py:377
  33.6 1.4 %collective-permute-start.9 = (f32[32,896]{1,0:T(8,128)S(1)}, f32[32,896]{1,0:T(8,128)S(1)}, u32[]{:S(2)}, u32[]{:S(2)}) collective-permute-start(f32[32,896]{1,0:T(8,128)S(1)} %get-tuple-element.20), channel_id=1, source_target_pairs={{0,1},{1,0},{2,3},{3,2},{4,5},{5,4},{6,7},{7,6},{8,9},{9,8},{10,11... | collective-permute-start | bytes 344072 | tf_op jit(solution)/shard_map/ppermute | solution.py:377

commit v8 on v7

--- a/solution.py
+++ b/solution.py
@@ -39,7 +39,8 @@
 
 def points_kernel(
     devices, me_ref, x_hbm, hidden_hbm, output_hbm, owner_hbm, node_hbm, weight_hbm,
-    send_ref, features_ref, kept_ref, tiles_ref, owner_ref, node_ref, weight_ref, x_ref, normed_ref, hidden_ref, output_ref, coeffs_ref, middle_ref, sems,
+    own_ref, rest_ref, features_ref, kept_ref, tiles_ref, owner_ref, node_ref, weight_ref,
+    x_ref, normed_ref, hidden_ref, output_ref, coeffs_ref, middle_ref, sems,
 ):
     rows = x_ref.shape[0]
     ff = hidden_ref.shape[1]
@@ -97,8 +98,7 @@
             if chunk < chunks:
                 tiles_ref[chunk * TOTAL_ROWS : (chunk + 1) * TOTAL_ROWS, :] = tile
             else:
-                end = (chunk - chunks + 1) * CHUNK
-                send_ref[end - TOTAL_ROWS : end, :] = tile
+                store_totals(own_ref, rest_ref, chunk - chunks, tile)
 
     x_copy.wait()
     x = x_ref[...].astype(jnp.float32)
@@ -128,7 +128,17 @@
         features_ref[at, :] = features
         term = jnp.dot(coeffs_ref[:, at], features, preferred_element_type=jnp.float32)
         sums = term if sums is None else sums + term
-    store_table(send_ref, sums.astype(jnp.bfloat16))
+    sums = sums.astype(jnp.bfloat16)
+    own_rows = own_ref.shape[0] // CHUNK * GROUP_ROWS
+    store_table(own_ref, sums[:own_rows])
+    store_table(rest_ref, sums[own_rows:])
+
+
+def store_totals(own_ref, rest_ref, chunk, tile):
+    own_chunks = own_ref.shape[0] // CHUNK
+    out_ref, place = (own_ref, chunk) if chunk < own_chunks else (rest_ref, chunk - own_chunks)
+    end = (place + 1) * CHUNK
+    out_ref[end - TOTAL_ROWS : end, :] = tile
 
 
 def store_table(out_ref, sums):
@@ -140,21 +150,26 @@
             ]
 
 
-def keep_kernel(features_ref, kept_ref, tiles_ref, out_ref):
+def keep_kernel(features_ref, kept_ref, tiles_ref, own_ref, rest_ref):
     sums = jnp.dot(kept_ref[...], features_ref[...], preferred_element_type=jnp.float32)
-    store_table(out_ref, sums.astype(jnp.bfloat16))
+    sums = sums.astype(jnp.bfloat16)
+    own_rows = own_ref.shape[0] // CHUNK * GROUP_ROWS
+    store_table(own_ref, sums[:own_rows])
+    store_table(rest_ref, sums[own_rows:])
     for chunk in range(tiles_ref.shape[0] // TOTAL_ROWS):
-        end = (chunk + 1) * CHUNK
-        out_ref[end - TOTAL_ROWS : end, :] = tiles_ref[
-            chunk * TOTAL_ROWS : (chunk + 1) * TOTAL_ROWS, :
-        ]
-
-
-def run_keep(features, kept, tiles):
+        tile = tiles_ref[chunk * TOTAL_ROWS : (chunk + 1) * TOTAL_ROWS, :]
+        store_totals(own_ref, rest_ref, chunk, tile)
+
+
+def run_keep(own_chunks, features, kept, tiles):
     nodes, rows = kept.shape
+    rest_chunks = nodes // GROUP_ROWS - own_chunks
     return pl.pallas_call(
         keep_kernel,
-        out_shape=pltpu.VMEM((nodes // GROUP_ROWS * CHUNK, LANES), jnp.bfloat16),
+        out_shape=[
+            pltpu.VMEM((own_chunks * CHUNK, LANES), jnp.bfloat16),
+            pltpu.VMEM((rest_chunks * CHUNK, LANES), jnp.bfloat16),
+        ],
         compiler_params=pltpu.CompilerParams(vmem_limit_bytes=8 * MIB + 16 * nodes * D),
         cost_estimate=pl.CostEstimate(
             flops=2 * nodes * rows * D, bytes_accessed=4 * nodes * D, transcendentals=0
@@ -163,10 +178,10 @@
     )(*in_vmem(features, kept, tiles))
 
 
-def run_points(devices, me, x, hidden_weight, output_weight, owner, node, weight):
+def run_points(devices, own_chunks, me, x, hidden_weight, output_weight, owner, node, weight):
     rows, ff = x.shape[0], hidden_weight.shape[1]
     nodes = devices * S_DEV
-    out = pltpu.VMEM((devices // 4 * CHUNK, LANES), jnp.bfloat16)
+    rest_chunks = devices // 4 - own_chunks
     hbm = pl.BlockSpec(memory_space=pl.ANY)
     vmem = pl.BlockSpec(memory_space=pltpu.VMEM)
     in_hbm = [
@@ -176,9 +191,10 @@
     return pl.pallas_call(
         functools.partial(points_kernel, devices),
         in_specs=[pl.BlockSpec(memory_space=pltpu.SMEM)] + [hbm] * 6,
-        out_specs=[vmem] * 4,
+        out_specs=[vmem] * 5,
         out_shape=[
-            out,
+            pltpu.VMEM((own_chunks * CHUNK, LANES), jnp.bfloat16),
+            pltpu.VMEM((rest_chunks * CHUNK, LANES), jnp.bfloat16),
             pltpu.VMEM((rows, D), jnp.bfloat16),
             pltpu.VMEM((nodes // 2, rows), jnp.bfloat16),
             pltpu.VMEM((devices // 4 * TOTAL_ROWS, LANES), jnp.bfloat16),
@@ -376,8 +392,16 @@
     def swap(array, flip):
         return lax.ppermute(array, "blk", [(i, i ^ flip) for i in range(devices)])
 
-    send, *kept = run_points(
+    groups = []
+    width = (devices // 4).bit_length() - 1
+    while width > 0:
+        take = min(2, width)
+        width -= take
+        groups.append((take, width))
+    own_chunks = 1 << groups[0][1]
+    own_send, rest_send, *kept = run_points(
         devices,
+        own_chunks,
         me,
         points_in,
         hidden_weight,
@@ -386,18 +410,19 @@
         point_node.reshape(1, rows),
         point_weight.reshape(1, rows),
     )
-    table = add_up(run_keep(*kept), swap(send, 1))
-    groups = []
-    width = (devices // 4).bit_length() - 1
-    while width > 0:
-        take = min(2, width)
-        width -= take
-        groups.append((take, width))
+    rest_got = swap(rest_send, 1)
+    own_got = swap(own_send, 1)
+    own_kept, rest_kept = run_keep(own_chunks, *kept)
+    sent = add_up(rest_kept, rest_got)
+    terms = [own_kept, own_got]
     for take, width in groups:
         size = (1 << width) * CHUNK
-        parts = [table[j * size : (j + 1) * size] for j in range(1 << take)]
         order = (2, 1, 3) if take == 2 else (1,)
-        table = add_up(parts[0], *[swap(parts[j], j << (width + 1)) for j in order])
+        table = add_up(
+            *terms, *[swap(sent[(j - 1) * size : j * size], j << (width + 1)) for j in order]
+        )
+        size = table.shape[0] // 4 if width > 1 else table.shape[0] // 2
+        terms, sent = [table[:size]], table[size:]
     nodes = run_nodes(devices, rows, table, swap(table, devices // 2))
     pieces = [nodes]
     for take, width in groups[::-1]:

time: 36.1 us -> 36.1 us (level)
    ppermute x10 -> x11, waiting for transfers between devices: 14.1 us -> 13.8 us  [swap(): return lax.ppermute(array, 'blk', [(i, i ^ flip) for i in range(devices)])]
    ppermute x10 -> x11, starting transfers between devices: 11.4 us -> 11.5 us  [swap(): return lax.ppermute(array, 'blk', [(i, i ^ flip) for i in range(devices)])]
  transfers between devices with their start and end apart: 10 -> 11, of which waited for: 10 -> 10; matrix products, arithmetic and copies ran while one was open for 0% -> 0% of each run, Pallas kernels for 3% -> 3%
where the time goes in v8:
time: 36.1 us; the launch traced here: 35.9 us
  waiting for transfers between devices  13.8 us (38%)
  starting transfers between devices  11.5 us (32%)
  Pallas kernels  10.3 us (29%)
    ppermute x11, waiting for transfers between devices, swap(): return lax.ppermute(array, 'blk', [(i, i ^ flip) for i in range(devices)])  13.8 us
    ppermute x11, starting transfers between devices, swap(): return lax.ppermute(array, 'blk', [(i, i ^ flip) for i in range(devices)])  11.5 us
    pallas_call x1, Pallas kernels, run_points(): pl.pallas_call(functools.partial(points_kernel, devices), in_specs=[pl.Bl...  6.91 us
    pallas_call x1, Pallas kernels, run_partial(): pl.pallas_call(partial_kernel, out_shape=[out, out], scratch_shapes=[pltp...  1.05 us
    pallas_call x1, Pallas kernels, run_merge(): pl.pallas_call(merge_kernel, out_shape=jax.ShapeDtypeStruct((S_DEV, D), j...  1 us
    pallas_call x1, Pallas kernels, run_own(): pl.pallas_call(functools.partial(own_kernel, devices), in_specs=[pl.Block...  0.73 us
  transfers between devices with their start and end apart: 11, of which 10 were waited for; matrix products, arithmetic and copies ran while one was open for 0% of the time, Pallas kernels for 3%

profile of v8, /device:TPU:0, one launch (start us, length us, event | category | flops | bytes accessed | tf_op | source)
XLA Modules:
  0.0 35.9 jit_solution(6013548630239109014)
XLA Ops:
  0.0 0.0 copy-start
  0.0 6.9 %points.1 = (bf16[400,128]{1,0:T(8,128)(2,1)S(1)}, bf16[1200,128]{1,0:T(8,128)(2,1)S(1)}, bf16[512,768]{1,0:T(8,128)(2,1)S(1)}, bf16[256,512]{1,0:T(8,128)(2,1)S(1)}, bf16[64,128]{1,0:T(8,128)(2,1)S(1)}) custom-call(s32[1]{0:T(128)} %bitcast.me_ref, bf16[512,768]{1,0:T(8,128)(2,1)} %x_hbm.1, bf16[768,2560]{1,0:T(8,128)(2,1)} %hidden_hbm.1, ...), custom_call_target="tpu_custom_call" | custom-call | tf_op jit(solution)/shard_map/points/pallas_call | solution.py:191
  6.9 0.5 %collective-permute-start.1 = (bf16[1200,128]{1,0:T(8,128)(2,1)S(1)}, bf16[1200,128]{1,0:T(8,128)(2,1)S(1)}, u32[]{:S(2)}, u32[]{:S(2)}) collective-permute-start(bf16[1200,128]{1,0:T(8,128)(2,1)S(1)} %get-tuple-element.22), channel_id=1, source_target_pairs={{0,1},{1,0},{2,3},{3,2},{4,5},{5,4},{6,7},{7,6},{8,9},{9,8},{10,11... | collective-permute-start | bytes 921608 | tf_op jit(solution)/shard_map/ppermute | solution.py:393
  7.4 0.1 collective-permute-start
  7.5 0.4 %keep.1 = (bf16[400,128]{1,0:T(8,128)(2,1)S(1)}, bf16[1200,128]{1,0:T(8,128)(2,1)S(1)}) custom-call(bf16[512,768]{1,0:T(8,128)(2,1)S(1)} %get-tuple-element.16.features_ref, bf16[256,512]{1,0:T(8,128)(2,1)S(1)} %get-tuple-element.17.kept_ref, bf16[64,128]{1,0:T(8,128)(2,1)S(1)} %get-tuple-element.18.tiles_ref), custom_call_target="tpu_custom_call" | custom-call | flops 201326592 | bytes 786432 | tf_op jit(solution)/shard_map/keep/pallas_call | solution.py:167
  7.9 0.8 %collective-permute-done.1 = bf16[1200,128]{1,0:T(8,128)(2,1)S(1)} collective-permute-done((bf16[1200,128]{1,0:T(8,128)(2,1)S(1)}, bf16[1200,128]{1,0:T(8,128)(2,1)S(1)}, u32[]{:S(2)}, u32[]{:S(2)}) %collective-permute-start.1) | collective-permute-done | bytes 307232 | tf_op jit(solution)/shard_map/ppermute | solution.py:393
  8.7 0.1 add_convert_fusion
  8.8 3.0 %collective-permute-start.2 = (bf16[400,128]{1,0:T(8,128)(2,1)S(1)}, bf16[400,128]{1,0:T(8,128)(2,1)S(1)}, u32[]{:S(2)}, u32[]{:S(2)}) collective-permute-start(bf16[400,128]{1,0:T(8,128)(2,1)S(1)} %get-tuple-element.27), channel_id=1, source_target_pairs={{0,4},{1,5},{2,6},{3,7},{4,0},{5,1},{6,2},{7,3},{8,12},{9,13},{10,... | collective-permute-start | bytes 307208 | tf_op jit(solution)/shard_map/ppermute | solution.py:393
  11.8 1.5 %collective-permute-start.3 = (bf16[400,128]{1,0:T(8,128)(2,1)S(1)}, bf16[400,128]{1,0:T(8,128)(2,1)S(1)}, u32[]{:S(2)}, u32[]{:S(2)}) collective-permute-start(bf16[400,128]{1,0:T(8,128)(2,1)S(1)} %get-tuple-element.29), channel_id=1, source_target_pairs={{0,2},{1,3},{2,0},{3,1},{4,6},{5,7},{6,4},{7,5},{8,10},{9,11},{10,... | collective-permute-start | bytes 307208 | tf_op jit(solution)/shard_map/ppermute | solution.py:393
  13.3 0.0 collective-permute-start.4
  13.3 0.0 collective-permute-done
  13.3 1.7 %collective-permute-done.2 = bf16[400,128]{1,0:T(8,128)(2,1)S(1)} collective-permute-done((bf16[400,128]{1,0:T(8,128)(2,1)S(1)}, bf16[400,128]{1,0:T(8,128)(2,1)S(1)}, u32[]{:S(2)}, u32[]{:S(2)}) %collective-permute-start.2) | collective-permute-done | bytes 102432 | tf_op jit(solution)/shard_map/ppermute | solution.py:393
  15.0 2.6 %collective-permute-done.3 = bf16[400,128]{1,0:T(8,128)(2,1)S(1)} collective-permute-done((bf16[400,128]{1,0:T(8,128)(2,1)S(1)}, bf16[400,128]{1,0:T(8,128)(2,1)S(1)}, u32[]{:S(2)}, u32[]{:S(2)}) %collective-permute-start.3) | collective-permute-done | bytes 102432 | tf_op jit(solution)/shard_map/ppermute | solution.py:393
  17.7 1.2 %collective-permute-done.4 = bf16[400,128]{1,0:T(8,128)(2,1)S(1)} collective-permute-done((bf16[400,128]{1,0:T(8,128)(2,1)S(1)}, bf16[400,128]{1,0:T(8,128)(2,1)S(1)}, u32[]{:S(2)}, u32[]{:S(2)}) %collective-permute-start.4) | collective-permute-done | bytes 102432 | tf_op jit(solution)/shard_map/ppermute | solution.py:393
  18.9 0.1 add_convert_fusion.1.mine_ref
  18.9 2.7 %collective-permute-start.5 = (bf16[400,128]{1,0:T(8,128)(2,1)S(1)}, bf16[400,128]{1,0:T(8,128)(2,1)S(1)}, u32[]{:S(2)}, u32[]{:S(2)}) collective-permute-start(bf16[400,128]{1,0:T(8,128)(2,1)S(1)} %add_convert_fusion.1.mine_ref), channel_id=1, source_target_pairs={{0,8},{1,9},{2,10},{3,11},{4,12},{5,13},{6,14},{7,15},{8,0},{9,1},... | collective-permute-start | bytes 307208 | tf_op jit(solution)/shard_map/ppermute | solution.py:393
  21.6 4.1 %collective-permute-done.5.other_ref = bf16[400,128]{1,0:T(8,128)(2,1)S(1)} collective-permute-done((bf16[400,128]{1,0:T(8,128)(2,1)S(1)}, bf16[400,128]{1,0:T(8,128)(2,1)S(1)}, u32[]{:S(2)}, u32[]{:S(2)}) %collective-permute-start.5) | collective-permute-done | bytes 102432 | tf_op jit(solution)/shard_map/ppermute | solution.py:393
  25.7 0.3 nodes.1.nodes_ref
  26.0 0.0 copy-start.1
  26.0 0.2 collective-permute-start.7
  26.2 1.7 %collective-permute-start.8 = (bf16[64,768]{1,0:T(8,128)(2,1)S(1)}, bf16[64,768]{1,0:T(8,128)(2,1)S(1)}, u32[]{:S(2)}, u32[]{:S(2)}) collective-permute-start(bf16[64,768]{1,0:T(8,128)(2,1)S(1)} %nodes.1.nodes_ref), channel_id=1, source_target_pairs={{0,2},{1,3},{2,0},{3,1},{4,6},{5,7},{6,4},{7,5},{8,10},{9,11},{10,... | collective-permute-start | bytes 294920 | tf_op jit(solution)/shard_map/ppermute | solution.py:393
  27.9 1.7 %collective-permute-start.9 = (bf16[64,768]{1,0:T(8,128)(2,1)S(1)}, bf16[64,768]{1,0:T(8,128)(2,1)S(1)}, u32[]{:S(2)}, u32[]{:S(2)}) collective-permute-start(bf16[64,768]{1,0:T(8,128)(2,1)S(1)} %nodes.1.nodes_ref), channel_id=1, source_target_pairs={{0,4},{1,5},{2,6},{3,7},{4,0},{5,1},{6,2},{7,3},{8,12},{9,13},{10,... | collective-permute-start | bytes 294920 | tf_op jit(solution)/shard_map/ppermute | solution.py:393
  29.6 0.0 copy-done
  29.6 0.7 %own.1 = (bf16[32,768]{1,0:T(8,128)(2,1)S(1)}, bf16[64,1536]{1,0:T(8,128)(2,1)S(1)}) custom-call(s32[1]{0:T(128)} %bitcast.me_ref, bf16[64,768]{1,0:T(8,128)(2,1)S(1)} %nodes.1.nodes_ref, bf16[768,2304]{1,0:T(8,128)(2,1)S(1)} %copy-done), custom_call_target="tpu_custom_call" | custom-call | flops 188743680 | bytes 3538944 | tf_op jit(solution)/shard_map/own/pallas_call | solution.py:270
  30.3 0.1 collective-permute-start.6
  30.4 1.2 %collective-permute-done.6.other_ref = bf16[32,768]{1,0:T(8,128)(2,1)S(1)} collective-permute-done((bf16[32,768]{1,0:T(8,128)(2,1)S(1)}, bf16[32,768]{1,0:T(8,128)(2,1)S(1)}, u32[]{:S(2)}, u32[]{:S(2)}) %collective-permute-start.6) | collective-permute-done | bytes 49184 | tf_op jit(solution)/shard_map/ppermute | solution.py:393
  31.6 0.1 collective-permute-done.7.refs_0_
  31.7 0.2 collective-permute-done.8.refs_1_
  31.9 0.6 %collective-permute-done.9.refs_2_ = bf16[64,768]{1,0:T(8,128)(2,1)S(1)} collective-permute-done((bf16[64,768]{1,0:T(8,128)(2,1)S(1)}, bf16[64,768]{1,0:T(8,128)(2,1)S(1)}, u32[]{:S(2)}, u32[]{:S(2)}) %collective-permute-start.9) | collective-permute-done | bytes 98336 | tf_op jit(solution)/shard_map/ppermute | solution.py:393
  32.5 1.0 %partial.1 = (f32[32,896]{1,0:T(8,128)S(1)}, f32[32,896]{1,0:T(8,128)S(1)}) custom-call(bf16[32,768]{1,0:T(8,128)(2,1)S(1)} %get-tuple-element.23.own_ref, bf16[32,768]{1,0:T(8,128)(2,1)S(1)} %collective-permute-done.6.other_ref, bf16[64,1536]{1,0:T(8,128)(2,1)S(1)} %get-tuple-element.24.own_key_value_ref, bf16[768,2304]{1,0:T(8,128)(2,1)S(1)} %copy-done, ...), custom_call_target="tpu_custom_call" | custom-call | tf_op jit(solution)/shard_map/partial/pallas_call | solution.py:331
  33.6 0.1 collective-permute-start.10
  33.6 0.0 copy-done.1
  33.7 1.3 %collective-permute-done.10.theirs_ref = f32[32,896]{1,0:T(8,128)S(1)} collective-permute-done((f32[32,896]{1,0:T(8,128)S(1)}, f32[32,896]{1,0:T(8,128)S(1)}, u32[]{:S(2)}, u32[]{:S(2)}) %collective-permute-start.10) | collective-permute-done | bytes 114720 | tf_op jit(solution)/shard_map/ppermute | solution.py:393
  34.9 1.0 %merge.1 = bf16[32,768]{1,0:T(8,128)(2,1)} custom-call(f32[32,896]{1,0:T(8,128)S(1)} %get-tuple-element.25.mine_ref, f32[32,896]{1,0:T(8,128)S(1)} %collective-permute-done.10.theirs_ref, bf16[1,768]{1,0:T(2,128)(2,1)S(1)} %reshape.19.gain_ref), custom_call_target="tpu_custom_call" | custom-call | tf_op jit(solution)/shard_map/merge/pallas_call | solution.py:363
  (2 shorter events, 0.0 us)
Async XLA Ops:
  0.0 29.6 %copy-start = (bf16[768,2304]{1,0:T(8,128)(2,1)S(1)}, bf16[768,2304]{1,0:T(8,128)(2,1)}, u32[]{:S(2)}) copy-start(bf16[768,2304]{1,0:T(8,128)(2,1)} %proj_ref.3) | copy-start | bytes 10616836
  6.9 1.7 %collective-permute-start.1 = (bf16[1200,128]{1,0:T(8,128)(2,1)S(1)}, bf16[1200,128]{1,0:T(8,128)(2,1)S(1)}, u32[]{:S(2)}, u32[]{:S(2)}) collective-permute-start(bf16[1200,128]{1,0:T(8,128)(2,1)S(1)} %get-tuple-element.22), channel_id=1, source_target_pairs={{0,1},{1,0},{2,3},{3,2},{4,5},{5,4},{6,7},{7,6},{8,9},{9,8},{10,11... | collective-permute-start | bytes 921608 | tf_op jit(solution)/shard_map/ppermute | solution.py:393
  7.4 5.9 %collective-permute-start = (bf16[400,128]{1,0:T(8,128)(2,1)S(1)}, bf16[400,128]{1,0:T(8,128)(2,1)S(1)}, u32[]{:S(2)}, u32[]{:S(2)}) collective-permute-start(bf16[400,128]{1,0:T(8,128)(2,1)S(1)} %get-tuple-element.20), channel_id=1, source_target_pairs={{0,1},{1,0},{2,3},{3,2},{4,5},{5,4},{6,7},{7,6},{8,9},{9,8},{10,11... | collective-permute-start | bytes 307208 | tf_op jit(solution)/shard_map/ppermute | solution.py:393
  8.8 6.3 %collective-permute-start.2 = (bf16[400,128]{1,0:T(8,128)(2,1)S(1)}, bf16[400,128]{1,0:T(8,128)(2,1)S(1)}, u32[]{:S(2)}, u32[]{:S(2)}) collective-permute-start(bf16[400,128]{1,0:T(8,128)(2,1)S(1)} %get-tuple-element.27), channel_id=1, source_target_pairs={{0,4},{1,5},{2,6},{3,7},{4,0},{5,1},{6,2},{7,3},{8,12},{9,13},{10,... | collective-permute-start | bytes 307208 | tf_op jit(solution)/shard_map/ppermute | solution.py:393
  11.8 5.9 %collective-permute-start.3 = (bf16[400,128]{1,0:T(8,128)(2,1)S(1)}, bf16[400,128]{1,0:T(8,128)(2,1)S(1)}, u32[]{:S(2)}, u32[]{:S(2)}) collective-permute-start(bf16[400,128]{1,0:T(8,128)(2,1)S(1)} %get-tuple-element.29), channel_id=1, source_target_pairs={{0,2},{1,3},{2,0},{3,1},{4,6},{5,7},{6,4},{7,5},{8,10},{9,11},{10,... | collective-permute-start | bytes 307208 | tf_op jit(solution)/shard_map/ppermute | solution.py:393
  13.3 5.6 %collective-permute-start.4 = (bf16[400,128]{1,0:T(8,128)(2,1)S(1)}, bf16[400,128]{1,0:T(8,128)(2,1)S(1)}, u32[]{:S(2)}, u32[]{:S(2)}) collective-permute-start(bf16[400,128]{1,0:T(8,128)(2,1)S(1)} %get-tuple-element.28), channel_id=1, source_target_pairs={{0,6},{1,7},{2,4},{3,5},{4,2},{5,3},{6,0},{7,1},{8,14},{9,15},{10,... | collective-permute-start | bytes 307208 | tf_op jit(solution)/shard_map/ppermute | solution.py:393
  18.9 6.8 %collective-permute-start.5 = (bf16[400,128]{1,0:T(8,128)(2,1)S(1)}, bf16[400,128]{1,0:T(8,128)(2,1)S(1)}, u32[]{:S(2)}, u32[]{:S(2)}) collective-permute-start(bf16[400,128]{1,0:T(8,128)(2,1)S(1)} %add_convert_fusion.1.mine_ref), channel_id=1, source_target_pairs={{0,8},{1,9},{2,10},{3,11},{4,12},{5,13},{6,14},{7,15},{8,0},{9,1},... | collective-permute-start | bytes 307208 | tf_op jit(solution)/shard_map/ppermute | solution.py:393
  26.0 7.6 %copy-start.1 = (bf16[768]{0:T(1024)(128)(2,1)S(1)}, bf16[768]{0:T(1024)(128)(2,1)}, u32[]{:S(2)}) copy-start(bf16[768]{0:T(1024)(128)(2,1)} %param.15) | copy-start | bytes 4612
  26.0 5.7 %collective-permute-start.7 = (bf16[64,768]{1,0:T(8,128)(2,1)S(1)}, bf16[64,768]{1,0:T(8,128)(2,1)S(1)}, u32[]{:S(2)}, u32[]{:S(2)}) collective-permute-start(bf16[64,768]{1,0:T(8,128)(2,1)S(1)} %nodes.1.nodes_ref), channel_id=1, source_target_pairs={{0,6},{1,7},{2,4},{3,5},{4,2},{5,3},{6,0},{7,1},{8,14},{9,15},{10,... | collective-permute-start | bytes 294920 | tf_op jit(solution)/shard_map/ppermute | solution.py:393
  26.2 5.7 %collective-permute-start.8 = (bf16[64,768]{1,0:T(8,128)(2,1)S(1)}, bf16[64,768]{1,0:T(8,128)(2,1)S(1)}, u32[]{:S(2)}, u32[]{:S(2)}) collective-permute-start(bf16[64,768]{1,0:T(8,128)(2,1)S(1)} %nodes.1.nodes_ref), channel_id=1, source_target_pairs={{0,2},{1,3},{2,0},{3,1},{4,6},{5,7},{6,4},{7,5},{8,10},{9,11},{10,... | collective-permute-start | bytes 294920 | tf_op jit(solution)/shard_map/ppermute | solution.py:393
  27.9 4.6 %collective-permute-start.9 = (bf16[64,768]{1,0:T(8,128)(2,1)S(1)}, bf16[64,768]{1,0:T(8,128)(2,1)S(1)}, u32[]{:S(2)}, u32[]{:S(2)}) collective-permute-start(bf16[64,768]{1,0:T(8,128)(2,1)S(1)} %nodes.1.nodes_ref), channel_id=1, source_target_pairs={{0,4},{1,5},{2,6},{3,7},{4,0},{5,1},{6,2},{7,3},{8,12},{9,13},{10,... | collective-permute-start | bytes 294920 | tf_op jit(solution)/shard_map/ppermute | solution.py:393
  30.3 1.3 %collective-permute-start.6 = (bf16[32,768]{1,0:T(8,128)(2,1)S(1)}, bf16[32,768]{1,0:T(8,128)(2,1)S(1)}, u32[]{:S(2)}, u32[]{:S(2)}) collective-permute-start(bf16[32,768]{1,0:T(8,128)(2,1)S(1)} %get-tuple-element.23.own_ref), channel_id=1, source_target_pairs={{0,1},{1,0},{2,3},{3,2},{4,5},{5,4},{6,7},{7,6},{8,9},{9,8},{10,11... | collective-permute-start | bytes 147464 | tf_op jit(solution)/shard_map/ppermute | solution.py:393
  33.6 1.4 %collective-permute-start.10 = (f32[32,896]{1,0:T(8,128)S(1)}, f32[32,896]{1,0:T(8,128)S(1)}, u32[]{:S(2)}, u32[]{:S(2)}) collective-permute-start(f32[32,896]{1,0:T(8,128)S(1)} %get-tuple-element.26), channel_id=1, source_target_pairs={{0,1},{1,0},{2,3},{3,2},{4,5},{5,4},{6,7},{7,6},{8,9},{9,8},{10,11... | collective-permute-start | bytes 344072 | tf_op jit(solution)/shard_map/ppermute | solution.py:393

commit v9 on v7

--- a/solution.py
+++ b/solution.py
@@ -29,7 +29,8 @@
 
 
 def gelu(values):
-    return 0.5 * values * (1.0 + lax.erf(values * 0.7071067811865476))
+    half = 0.5 * values
+    return half + half * lax.erf(values * 0.7071067811865476)
 
 
 def hidden_parts(ff):

time: 36.1 us -> 36.1 us (level)
  no operation moved by 1% of the time
where the time goes in v9:
time: 36.1 us; the launch traced here: 36 us
  waiting for transfers between devices  14 us (39%)
  starting transfers between devices  11.4 us (32%)
  Pallas kernels  10.2 us (28%)
    ppermute x10, waiting for transfers between devices, swap(): return lax.ppermute(array, 'blk', [(i, i ^ flip) for i in range(devices)])  14 us
    ppermute x10, starting transfers between devices, swap(): return lax.ppermute(array, 'blk', [(i, i ^ flip) for i in range(devices)])  11.4 us
    pallas_call x1, Pallas kernels, run_points(): pl.pallas_call(functools.partial(points_kernel, devices), in_specs=[pl.Bl...  6.77 us
    pallas_call x1, Pallas kernels, run_partial(): pl.pallas_call(partial_kernel, out_shape=[out, out], scratch_shapes=[pltp...  1.04 us
    pallas_call x1, Pallas kernels, run_merge(): pl.pallas_call(merge_kernel, out_shape=jax.ShapeDtypeStruct((S_DEV, D), j...  1 us
    pallas_call x1, Pallas kernels, run_own(): pl.pallas_call(functools.partial(own_kernel, devices), in_specs=[pl.Block...  0.74 us
  transfers between devices with their start and end apart: 10, of which 10 were waited for; matrix products, arithmetic and copies ran while one was open for 0% of the time, Pallas kernels for 3%

profile of v9, /device:TPU:0, one launch (start us, length us, event | category | flops | bytes accessed | tf_op | source)
XLA Modules:
  0.0 36.0 jit_solution(3266520798437859734)
XLA Ops:
  0.0 6.8 %points.1 = (bf16[1600,128]{1,0:T(8,128)(2,1)S(1)}, bf16[512,768]{1,0:T(8,128)(2,1)S(1)}, bf16[256,512]{1,0:T(8,128)(2,1)S(1)}, bf16[64,128]{1,0:T(8,128)(2,1)S(1)}) custom-call(s32[1]{0:T(128)} %bitcast.me_ref, bf16[512,768]{1,0:T(8,128)(2,1)} %x_hbm.1, bf16[768,2560]{1,0:T(8,128)(2,1)} %hidden_hbm.1, bf16[2560,768]{1,0:T(8,128)(2,1)} %output_hbm.1, ...), custom_call_target="tpu_custom_call" | custom-call | tf_op jit(solution)/shard_map/points/pallas_call | solution.py:177
  6.8 0.0 copy-start
  6.8 0.5 %collective-permute-start = (bf16[1600,128]{1,0:T(8,128)(2,1)S(1)}, bf16[1600,128]{1,0:T(8,128)(2,1)S(1)}, u32[]{:S(2)}, u32[]{:S(2)}) collective-permute-start(bf16[1600,128]{1,0:T(8,128)(2,1)S(1)} %get-tuple-element.16), channel_id=1, source_target_pairs={{0,1},{1,0},{2,3},{3,2},{4,5},{5,4},{6,7},{7,6},{8,9},{9,8},{10,11... | collective-permute-start | bytes 1228808 | tf_op jit(solution)/shard_map/ppermute | solution.py:378
  7.3 0.4 %keep.1 = bf16[1600,128]{1,0:T(8,128)(2,1)S(1)} custom-call(bf16[512,768]{1,0:T(8,128)(2,1)S(1)} %get-tuple-element.13.features_ref, bf16[256,512]{1,0:T(8,128)(2,1)S(1)} %get-tuple-element.14.kept_ref, bf16[64,128]{1,0:T(8,128)(2,1)S(1)} %get-tuple-element.15.tiles_ref), custom_call_target="tpu_custom_call" | custom-call | flops 201326592 | bytes 786432 | tf_op jit(solution)/shard_map/keep/pallas_call | solution.py:156
  7.7 1.0 %collective-permute-done = bf16[1600,128]{1,0:T(8,128)(2,1)S(1)} collective-permute-done((bf16[1600,128]{1,0:T(8,128)(2,1)S(1)}, bf16[1600,128]{1,0:T(8,128)(2,1)S(1)}, u32[]{:S(2)}, u32[]{:S(2)}) %collective-permute-start) | collective-permute-done | bytes 409632 | tf_op jit(solution)/shard_map/ppermute | solution.py:378
  8.7 0.1 add_convert_fusion
  8.8 3.0 %collective-permute-start.1 = (bf16[400,128]{1,0:T(8,128)(2,1)S(1)}, bf16[400,128]{1,0:T(8,128)(2,1)S(1)}, u32[]{:S(2)}, u32[]{:S(2)}) collective-permute-start(bf16[400,128]{1,0:T(8,128)(2,1)S(1)} %get-tuple-element.21), channel_id=1, source_target_pairs={{0,4},{1,5},{2,6},{3,7},{4,0},{5,1},{6,2},{7,3},{8,12},{9,13},{10,... | collective-permute-start | bytes 307208 | tf_op jit(solution)/shard_map/ppermute | solution.py:378
  11.8 1.5 %collective-permute-start.2 = (bf16[400,128]{1,0:T(8,128)(2,1)S(1)}, bf16[400,128]{1,0:T(8,128)(2,1)S(1)}, u32[]{:S(2)}, u32[]{:S(2)}) collective-permute-start(bf16[400,128]{1,0:T(8,128)(2,1)S(1)} %get-tuple-element.23), channel_id=1, source_target_pairs={{0,2},{1,3},{2,0},{3,1},{4,6},{5,7},{6,4},{7,5},{8,10},{9,11},{10,... | collective-permute-start | bytes 307208 | tf_op jit(solution)/shard_map/ppermute | solution.py:378
  13.4 0.0 collective-permute-start.3
  13.4 1.7 %collective-permute-done.1 = bf16[400,128]{1,0:T(8,128)(2,1)S(1)} collective-permute-done((bf16[400,128]{1,0:T(8,128)(2,1)S(1)}, bf16[400,128]{1,0:T(8,128)(2,1)S(1)}, u32[]{:S(2)}, u32[]{:S(2)}) %collective-permute-start.1) | collective-permute-done | bytes 102432 | tf_op jit(solution)/shard_map/ppermute | solution.py:378
  15.1 2.6 %collective-permute-done.2 = bf16[400,128]{1,0:T(8,128)(2,1)S(1)} collective-permute-done((bf16[400,128]{1,0:T(8,128)(2,1)S(1)}, bf16[400,128]{1,0:T(8,128)(2,1)S(1)}, u32[]{:S(2)}, u32[]{:S(2)}) %collective-permute-start.2) | collective-permute-done | bytes 102432 | tf_op jit(solution)/shard_map/ppermute | solution.py:378
  17.7 1.2 %collective-permute-done.3 = bf16[400,128]{1,0:T(8,128)(2,1)S(1)} collective-permute-done((bf16[400,128]{1,0:T(8,128)(2,1)S(1)}, bf16[400,128]{1,0:T(8,128)(2,1)S(1)}, u32[]{:S(2)}, u32[]{:S(2)}) %collective-permute-start.3) | collective-permute-done | bytes 102432 | tf_op jit(solution)/shard_map/ppermute | solution.py:378
  18.9 0.1 add_convert_fusion.1.mine_ref
  19.0 2.7 %collective-permute-start.4 = (bf16[400,128]{1,0:T(8,128)(2,1)S(1)}, bf16[400,128]{1,0:T(8,128)(2,1)S(1)}, u32[]{:S(2)}, u32[]{:S(2)}) collective-permute-start(bf16[400,128]{1,0:T(8,128)(2,1)S(1)} %add_convert_fusion.1.mine_ref), channel_id=1, source_target_pairs={{0,8},{1,9},{2,10},{3,11},{4,12},{5,13},{6,14},{7,15},{8,0},{9,1},... | collective-permute-start | bytes 307208 | tf_op jit(solution)/shard_map/ppermute | solution.py:378
  21.6 4.1 %collective-permute-done.4.other_ref = bf16[400,128]{1,0:T(8,128)(2,1)S(1)} collective-permute-done((bf16[400,128]{1,0:T(8,128)(2,1)S(1)}, bf16[400,128]{1,0:T(8,128)(2,1)S(1)}, u32[]{:S(2)}, u32[]{:S(2)}) %collective-permute-start.4) | collective-permute-done | bytes 102432 | tf_op jit(solution)/shard_map/ppermute | solution.py:378
  25.8 0.3 nodes.1.nodes_ref
  26.0 0.0 copy-start.1
  26.0 0.2 collective-permute-start.6
  26.3 1.7 %collective-permute-start.7 = (bf16[64,768]{1,0:T(8,128)(2,1)S(1)}, bf16[64,768]{1,0:T(8,128)(2,1)S(1)}, u32[]{:S(2)}, u32[]{:S(2)}) collective-permute-start(bf16[64,768]{1,0:T(8,128)(2,1)S(1)} %nodes.1.nodes_ref), channel_id=1, source_target_pairs={{0,2},{1,3},{2,0},{3,1},{4,6},{5,7},{6,4},{7,5},{8,10},{9,11},{10,... | collective-permute-start | bytes 294920 | tf_op jit(solution)/shard_map/ppermute | solution.py:378
  27.9 1.7 %collective-permute-start.8 = (bf16[64,768]{1,0:T(8,128)(2,1)S(1)}, bf16[64,768]{1,0:T(8,128)(2,1)S(1)}, u32[]{:S(2)}, u32[]{:S(2)}) collective-permute-start(bf16[64,768]{1,0:T(8,128)(2,1)S(1)} %nodes.1.nodes_ref), channel_id=1, source_target_pairs={{0,4},{1,5},{2,6},{3,7},{4,0},{5,1},{6,2},{7,3},{8,12},{9,13},{10,... | collective-permute-start | bytes 294920 | tf_op jit(solution)/shard_map/ppermute | solution.py:378
  29.6 0.0 copy-done
  29.6 0.7 %own.1 = (bf16[32,768]{1,0:T(8,128)(2,1)S(1)}, bf16[64,1536]{1,0:T(8,128)(2,1)S(1)}) custom-call(s32[1]{0:T(128)} %bitcast.me_ref, bf16[64,768]{1,0:T(8,128)(2,1)S(1)} %nodes.1.nodes_ref, bf16[768,2304]{1,0:T(8,128)(2,1)S(1)} %copy-done), custom_call_target="tpu_custom_call" | custom-call | flops 188743680 | bytes 3538944 | tf_op jit(solution)/shard_map/own/pallas_call | solution.py:255
  30.3 0.1 collective-permute-start.5
  30.4 1.2 %collective-permute-done.5.other_ref = bf16[32,768]{1,0:T(8,128)(2,1)S(1)} collective-permute-done((bf16[32,768]{1,0:T(8,128)(2,1)S(1)}, bf16[32,768]{1,0:T(8,128)(2,1)S(1)}, u32[]{:S(2)}, u32[]{:S(2)}) %collective-permute-start.5) | collective-permute-done | bytes 49184 | tf_op jit(solution)/shard_map/ppermute | solution.py:378
  31.6 0.1 collective-permute-done.6.refs_0_
  31.7 0.2 collective-permute-done.7.refs_1_
  31.9 0.6 %collective-permute-done.8.refs_2_ = bf16[64,768]{1,0:T(8,128)(2,1)S(1)} collective-permute-done((bf16[64,768]{1,0:T(8,128)(2,1)S(1)}, bf16[64,768]{1,0:T(8,128)(2,1)S(1)}, u32[]{:S(2)}, u32[]{:S(2)}) %collective-permute-start.8) | collective-permute-done | bytes 98336 | tf_op jit(solution)/shard_map/ppermute | solution.py:378
  32.5 1.0 %partial.1 = (f32[32,896]{1,0:T(8,128)S(1)}, f32[32,896]{1,0:T(8,128)S(1)}) custom-call(bf16[32,768]{1,0:T(8,128)(2,1)S(1)} %get-tuple-element.17.own_ref, bf16[32,768]{1,0:T(8,128)(2,1)S(1)} %collective-permute-done.5.other_ref, bf16[64,1536]{1,0:T(8,128)(2,1)S(1)} %get-tuple-element.18.own_key_value_ref, bf16[768,2304]{1,0:T(8,128)(2,1)S(1)} %copy-done, ...), custom_call_target="tpu_custom_call" | custom-call | tf_op jit(solution)/shard_map/partial/pallas_call | solution.py:316
  33.6 0.1 collective-permute-start.9
  33.7 0.0 copy-done.1
  33.7 1.3 %collective-permute-done.9.theirs_ref = f32[32,896]{1,0:T(8,128)S(1)} collective-permute-done((f32[32,896]{1,0:T(8,128)S(1)}, f32[32,896]{1,0:T(8,128)S(1)}, u32[]{:S(2)}, u32[]{:S(2)}) %collective-permute-start.9) | collective-permute-done | bytes 114720 | tf_op jit(solution)/shard_map/ppermute | solution.py:378
  35.0 1.0 %merge.1 = bf16[32,768]{1,0:T(8,128)(2,1)} custom-call(f32[32,896]{1,0:T(8,128)S(1)} %get-tuple-element.19.mine_ref, f32[32,896]{1,0:T(8,128)S(1)} %collective-permute-done.9.theirs_ref, bf16[1,768]{1,0:T(2,128)(2,1)S(1)} %reshape.19.gain_ref), custom_call_target="tpu_custom_call" | custom-call | tf_op jit(solution)/shard_map/merge/pallas_call | solution.py:348
  (2 shorter events, 0.0 us)
Async XLA Ops:
  6.8 22.8 %copy-start = (bf16[768,2304]{1,0:T(8,128)(2,1)S(1)}, bf16[768,2304]{1,0:T(8,128)(2,1)}, u32[]{:S(2)}) copy-start(bf16[768,2304]{1,0:T(8,128)(2,1)} %proj_ref.3) | copy-start | bytes 10616836
  6.8 1.9 %collective-permute-start = (bf16[1600,128]{1,0:T(8,128)(2,1)S(1)}, bf16[1600,128]{1,0:T(8,128)(2,1)S(1)}, u32[]{:S(2)}, u32[]{:S(2)}) collective-permute-start(bf16[1600,128]{1,0:T(8,128)(2,1)S(1)} %get-tuple-element.16), channel_id=1, source_target_pairs={{0,1},{1,0},{2,3},{3,2},{4,5},{5,4},{6,7},{7,6},{8,9},{9,8},{10,11... | collective-permute-start | bytes 1228808 | tf_op jit(solution)/shard_map/ppermute | solution.py:378
  8.8 6.2 %collective-permute-start.1 = (bf16[400,128]{1,0:T(8,128)(2,1)S(1)}, bf16[400,128]{1,0:T(8,128)(2,1)S(1)}, u32[]{:S(2)}, u32[]{:S(2)}) collective-permute-start(bf16[400,128]{1,0:T(8,128)(2,1)S(1)} %get-tuple-element.21), channel_id=1, source_target_pairs={{0,4},{1,5},{2,6},{3,7},{4,0},{5,1},{6,2},{7,3},{8,12},{9,13},{10,... | collective-permute-start | bytes 307208 | tf_op jit(solution)/shard_map/ppermute | solution.py:378
  11.8 5.9 %collective-permute-start.2 = (bf16[400,128]{1,0:T(8,128)(2,1)S(1)}, bf16[400,128]{1,0:T(8,128)(2,1)S(1)}, u32[]{:S(2)}, u32[]{:S(2)}) collective-permute-start(bf16[400,128]{1,0:T(8,128)(2,1)S(1)} %get-tuple-element.23), channel_id=1, source_target_pairs={{0,2},{1,3},{2,0},{3,1},{4,6},{5,7},{6,4},{7,5},{8,10},{9,11},{10,... | collective-permute-start | bytes 307208 | tf_op jit(solution)/shard_map/ppermute | solution.py:378
  13.4 5.6 %collective-permute-start.3 = (bf16[400,128]{1,0:T(8,128)(2,1)S(1)}, bf16[400,128]{1,0:T(8,128)(2,1)S(1)}, u32[]{:S(2)}, u32[]{:S(2)}) collective-permute-start(bf16[400,128]{1,0:T(8,128)(2,1)S(1)} %get-tuple-element.22), channel_id=1, source_target_pairs={{0,6},{1,7},{2,4},{3,5},{4,2},{5,3},{6,0},{7,1},{8,14},{9,15},{10,... | collective-permute-start | bytes 307208 | tf_op jit(solution)/shard_map/ppermute | solution.py:378
  19.0 6.8 %collective-permute-start.4 = (bf16[400,128]{1,0:T(8,128)(2,1)S(1)}, bf16[400,128]{1,0:T(8,128)(2,1)S(1)}, u32[]{:S(2)}, u32[]{:S(2)}) collective-permute-start(bf16[400,128]{1,0:T(8,128)(2,1)S(1)} %add_convert_fusion.1.mine_ref), channel_id=1, source_target_pairs={{0,8},{1,9},{2,10},{3,11},{4,12},{5,13},{6,14},{7,15},{8,0},{9,1},... | collective-permute-start | bytes 307208 | tf_op jit(solution)/shard_map/ppermute | solution.py:378
  26.0 7.6 %copy-start.1 = (bf16[768]{0:T(1024)(128)(2,1)S(1)}, bf16[768]{0:T(1024)(128)(2,1)}, u32[]{:S(2)}) copy-start(bf16[768]{0:T(1024)(128)(2,1)} %param.15) | copy-start | bytes 4612
  26.0 5.7 %collective-permute-start.6 = (bf16[64,768]{1,0:T(8,128)(2,1)S(1)}, bf16[64,768]{1,0:T(8,128)(2,1)S(1)}, u32[]{:S(2)}, u32[]{:S(2)}) collective-permute-start(bf16[64,768]{1,0:T(8,128)(2,1)S(1)} %nodes.1.nodes_ref), channel_id=1, source_target_pairs={{0,6},{1,7},{2,4},{3,5},{4,2},{5,3},{6,0},{7,1},{8,14},{9,15},{10,... | collective-permute-start | bytes 294920 | tf_op jit(solution)/shard_map/ppermute | solution.py:378
  26.3 5.7 %collective-permute-start.7 = (bf16[64,768]{1,0:T(8,128)(2,1)S(1)}, bf16[64,768]{1,0:T(8,128)(2,1)S(1)}, u32[]{:S(2)}, u32[]{:S(2)}) collective-permute-start(bf16[64,768]{1,0:T(8,128)(2,1)S(1)} %nodes.1.nodes_ref), channel_id=1, source_target_pairs={{0,2},{1,3},{2,0},{3,1},{4,6},{5,7},{6,4},{7,5},{8,10},{9,11},{10,... | collective-permute-start | bytes 294920 | tf_op jit(solution)/shard_map/ppermute | solution.py:378
  27.9 4.6 %collective-permute-start.8 = (bf16[64,768]{1,0:T(8,128)(2,1)S(1)}, bf16[64,768]{1,0:T(8,128)(2,1)S(1)}, u32[]{:S(2)}, u32[]{:S(2)}) collective-permute-start(bf16[64,768]{1,0:T(8,128)(2,1)S(1)} %nodes.1.nodes_ref), channel_id=1, source_target_pairs={{0,4},{1,5},{2,6},{3,7},{4,0},{5,1},{6,2},{7,3},{8,12},{9,13},{10,... | collective-permute-start | bytes 294920 | tf_op jit(solution)/shard_map/ppermute | solution.py:378
  30.3 1.3 %collective-permute-start.5 = (bf16[32,768]{1,0:T(8,128)(2,1)S(1)}, bf16[32,768]{1,0:T(8,128)(2,1)S(1)}, u32[]{:S(2)}, u32[]{:S(2)}) collective-permute-start(bf16[32,768]{1,0:T(8,128)(2,1)S(1)} %get-tuple-element.17.own_ref), channel_id=1, source_target_pairs={{0,1},{1,0},{2,3},{3,2},{4,5},{5,4},{6,7},{7,6},{8,9},{9,8},{10,11... | collective-permute-start | bytes 147464 | tf_op jit(solution)/shard_map/ppermute | solution.py:378
  33.6 1.4 %collective-permute-start.9 = (f32[32,896]{1,0:T(8,128)S(1)}, f32[32,896]{1,0:T(8,128)S(1)}, u32[]{:S(2)}, u32[]{:S(2)}) collective-permute-start(f32[32,896]{1,0:T(8,128)S(1)} %get-tuple-element.20), channel_id=1, source_target_pairs={{0,1},{1,0},{2,3},{3,2},{4,5},{5,4},{6,7},{7,6},{8,9},{9,8},{10,11... | collective-permute-start | bytes 344072 | tf_op jit(solution)/shard_map/ppermute | solution.py:378

commit v10 on v7

--- a/solution.py
+++ b/solution.py
@@ -403,7 +403,7 @@
     for take, width in groups[::-1]:
         pieces += [
             swap(piece, j << (width + 1))
-            for j in ((3, 1, 2) if take == 2 else (1,))
+            for j in ((1, 3, 2) if take == 2 else (1,))
             for piece in pieces
         ]
     own, own_key_value = run_own(devices, me, nodes, proj_weight)

time: 36.1 us -> 36.8 us (1.019)
  waiting for transfers between devices: 14.1 us -> 14.7 us
    ppermute x10, waiting for transfers between devices: 14.1 us -> 14.7 us  [swap(): return lax.ppermute(array, 'blk', [(i, i ^ flip) for i in range(devices)])]
  transfers between devices with their start and end apart: 10 -> 10, of which waited for: 10 -> 9; matrix products, arithmetic and copies ran while one was open for 0% -> 0% of each run, Pallas kernels for 3% -> 3%
where the time goes in v10:
time: 36.8 us; the launch traced here: 36.6 us
  waiting for transfers between devices  14.7 us (40%)
  starting transfers between devices  11.4 us (31%)
  Pallas kernels  10.2 us (28%)
    ppermute x10, waiting for transfers between devices, swap(): return lax.ppermute(array, 'blk', [(i, i ^ flip) for i in range(devices)])  14.7 us
    ppermute x10, starting transfers between devices, swap(): return lax.ppermute(array, 'blk', [(i, i ^ flip) for i in range(devices)])  11.4 us
    pallas_call x1, Pallas kernels, run_points(): pl.pallas_call(functools.partial(points_kernel, devices), in_specs=[pl.Bl...  6.76 us
    pallas_call x1, Pallas kernels, run_partial(): pl.pallas_call(partial_kernel, out_shape=[out, out], scratch_shapes=[pltp...  1.04 us
    pallas_call x1, Pallas kernels, run_merge(): pl.pallas_call(merge_kernel, out_shape=jax.ShapeDtypeStruct((S_DEV, D), j...  1 us
  transfers between devices with their start and end apart: 10, of which 9 were waited for; matrix products, arithmetic and copies ran while one was open for 0% of the time, Pallas kernels for 3%

profile of v10, /device:TPU:0, one launch (start us, length us, event | category | flops | bytes accessed | tf_op | source)
XLA Modules:
  0.0 36.6 jit_solution(18217346565075067296)
XLA Ops:
  0.0 6.8 %points.1 = (bf16[1600,128]{1,0:T(8,128)(2,1)S(1)}, bf16[512,768]{1,0:T(8,128)(2,1)S(1)}, bf16[256,512]{1,0:T(8,128)(2,1)S(1)}, bf16[64,128]{1,0:T(8,128)(2,1)S(1)}) custom-call(s32[1]{0:T(128)} %bitcast.me_ref, bf16[512,768]{1,0:T(8,128)(2,1)} %x_hbm.1, bf16[768,2560]{1,0:T(8,128)(2,1)} %hidden_hbm.1, bf16[2560,768]{1,0:T(8,128)(2,1)} %output_hbm.1, ...), custom_call_target="tpu_custom_call" | custom-call | tf_op jit(solution)/shard_map/points/pallas_call | solution.py:176
  6.8 0.0 copy-start
  6.8 0.5 %collective-permute-start = (bf16[1600,128]{1,0:T(8,128)(2,1)S(1)}, bf16[1600,128]{1,0:T(8,128)(2,1)S(1)}, u32[]{:S(2)}, u32[]{:S(2)}) collective-permute-start(bf16[1600,128]{1,0:T(8,128)(2,1)S(1)} %get-tuple-element.16), channel_id=1, source_target_pairs={{0,1},{1,0},{2,3},{3,2},{4,5},{5,4},{6,7},{7,6},{8,9},{9,8},{10,11... | collective-permute-start | bytes 1228808 | tf_op jit(solution)/shard_map/ppermute | solution.py:377
  7.3 0.4 %keep.1 = bf16[1600,128]{1,0:T(8,128)(2,1)S(1)} custom-call(bf16[512,768]{1,0:T(8,128)(2,1)S(1)} %get-tuple-element.13.features_ref, bf16[256,512]{1,0:T(8,128)(2,1)S(1)} %get-tuple-element.14.kept_ref, bf16[64,128]{1,0:T(8,128)(2,1)S(1)} %get-tuple-element.15.tiles_ref), custom_call_target="tpu_custom_call" | custom-call | flops 201326592 | bytes 786432 | tf_op jit(solution)/shard_map/keep/pallas_call | solution.py:155
  7.7 1.0 %collective-permute-done = bf16[1600,128]{1,0:T(8,128)(2,1)S(1)} collective-permute-done((bf16[1600,128]{1,0:T(8,128)(2,1)S(1)}, bf16[1600,128]{1,0:T(8,128)(2,1)S(1)}, u32[]{:S(2)}, u32[]{:S(2)}) %collective-permute-start) | collective-permute-done | bytes 409632 | tf_op jit(solution)/shard_map/ppermute | solution.py:377
  8.7 0.1 add_convert_fusion
  8.8 3.0 %collective-permute-start.1 = (bf16[400,128]{1,0:T(8,128)(2,1)S(1)}, bf16[400,128]{1,0:T(8,128)(2,1)S(1)}, u32[]{:S(2)}, u32[]{:S(2)}) collective-permute-start(bf16[400,128]{1,0:T(8,128)(2,1)S(1)} %get-tuple-element.21), channel_id=1, source_target_pairs={{0,4},{1,5},{2,6},{3,7},{4,0},{5,1},{6,2},{7,3},{8,12},{9,13},{10,... | collective-permute-start | bytes 307208 | tf_op jit(solution)/shard_map/ppermute | solution.py:377
  11.8 1.5 %collective-permute-start.2 = (bf16[400,128]{1,0:T(8,128)(2,1)S(1)}, bf16[400,128]{1,0:T(8,128)(2,1)S(1)}, u32[]{:S(2)}, u32[]{:S(2)}) collective-permute-start(bf16[400,128]{1,0:T(8,128)(2,1)S(1)} %get-tuple-element.23), channel_id=1, source_target_pairs={{0,2},{1,3},{2,0},{3,1},{4,6},{5,7},{6,4},{7,5},{8,10},{9,11},{10,... | collective-permute-start | bytes 307208 | tf_op jit(solution)/shard_map/ppermute | solution.py:377
  13.3 0.0 collective-permute-start.3
  13.4 1.7 %collective-permute-done.1 = bf16[400,128]{1,0:T(8,128)(2,1)S(1)} collective-permute-done((bf16[400,128]{1,0:T(8,128)(2,1)S(1)}, bf16[400,128]{1,0:T(8,128)(2,1)S(1)}, u32[]{:S(2)}, u32[]{:S(2)}) %collective-permute-start.1) | collective-permute-done | bytes 102432 | tf_op jit(solution)/shard_map/ppermute | solution.py:377
  15.1 2.6 %collective-permute-done.2 = bf16[400,128]{1,0:T(8,128)(2,1)S(1)} collective-permute-done((bf16[400,128]{1,0:T(8,128)(2,1)S(1)}, bf16[400,128]{1,0:T(8,128)(2,1)S(1)}, u32[]{:S(2)}, u32[]{:S(2)}) %collective-permute-start.2) | collective-permute-done | bytes 102432 | tf_op jit(solution)/shard_map/ppermute | solution.py:377
  17.7 1.2 %collective-permute-done.3 = bf16[400,128]{1,0:T(8,128)(2,1)S(1)} collective-permute-done((bf16[400,128]{1,0:T(8,128)(2,1)S(1)}, bf16[400,128]{1,0:T(8,128)(2,1)S(1)}, u32[]{:S(2)}, u32[]{:S(2)}) %collective-permute-start.3) | collective-permute-done | bytes 102432 | tf_op jit(solution)/shard_map/ppermute | solution.py:377
  18.9 0.1 add_convert_fusion.1.mine_ref
  19.0 2.7 %collective-permute-start.4 = (bf16[400,128]{1,0:T(8,128)(2,1)S(1)}, bf16[400,128]{1,0:T(8,128)(2,1)S(1)}, u32[]{:S(2)}, u32[]{:S(2)}) collective-permute-start(bf16[400,128]{1,0:T(8,128)(2,1)S(1)} %add_convert_fusion.1.mine_ref), channel_id=1, source_target_pairs={{0,8},{1,9},{2,10},{3,11},{4,12},{5,13},{6,14},{7,15},{8,0},{9,1},... | collective-permute-start | bytes 307208 | tf_op jit(solution)/shard_map/ppermute | solution.py:377
  21.6 4.1 %collective-permute-done.4.other_ref = bf16[400,128]{1,0:T(8,128)(2,1)S(1)} collective-permute-done((bf16[400,128]{1,0:T(8,128)(2,1)S(1)}, bf16[400,128]{1,0:T(8,128)(2,1)S(1)}, u32[]{:S(2)}, u32[]{:S(2)}) %collective-permute-start.4) | collective-permute-done | bytes 102432 | tf_op jit(solution)/shard_map/ppermute | solution.py:377
  25.7 0.3 nodes.1.nodes_ref
  26.0 0.0 copy-start.1
  26.0 1.2 %collective-permute-start.6 = (bf16[64,768]{1,0:T(8,128)(2,1)S(1)}, bf16[64,768]{1,0:T(8,128)(2,1)S(1)}, u32[]{:S(2)}, u32[]{:S(2)}) collective-permute-start(bf16[64,768]{1,0:T(8,128)(2,1)S(1)} %nodes.1.nodes_ref), channel_id=1, source_target_pairs={{0,2},{1,3},{2,0},{3,1},{4,6},{5,7},{6,4},{7,5},{8,10},{9,11},{10,... | collective-permute-start | bytes 294920 | tf_op jit(solution)/shard_map/ppermute | solution.py:377
  27.2 0.7 %collective-permute-start.7 = (bf16[64,768]{1,0:T(8,128)(2,1)S(1)}, bf16[64,768]{1,0:T(8,128)(2,1)S(1)}, u32[]{:S(2)}, u32[]{:S(2)}) collective-permute-start(bf16[64,768]{1,0:T(8,128)(2,1)S(1)} %nodes.1.nodes_ref), channel_id=1, source_target_pairs={{0,6},{1,7},{2,4},{3,5},{4,2},{5,3},{6,0},{7,1},{8,14},{9,15},{10,... | collective-permute-start | bytes 294920 | tf_op jit(solution)/shard_map/ppermute | solution.py:377
  27.9 1.6 %collective-permute-start.8 = (bf16[64,768]{1,0:T(8,128)(2,1)S(1)}, bf16[64,768]{1,0:T(8,128)(2,1)S(1)}, u32[]{:S(2)}, u32[]{:S(2)}) collective-permute-start(bf16[64,768]{1,0:T(8,128)(2,1)S(1)} %nodes.1.nodes_ref), channel_id=1, source_target_pairs={{0,4},{1,5},{2,6},{3,7},{4,0},{5,1},{6,2},{7,3},{8,12},{9,13},{10,... | collective-permute-start | bytes 294920 | tf_op jit(solution)/shard_map/ppermute | solution.py:377
  29.5 0.0 copy-done
  29.5 0.7 %own.1 = (bf16[32,768]{1,0:T(8,128)(2,1)S(1)}, bf16[64,1536]{1,0:T(8,128)(2,1)S(1)}) custom-call(s32[1]{0:T(128)} %bitcast.me_ref, bf16[64,768]{1,0:T(8,128)(2,1)S(1)} %nodes.1.nodes_ref, bf16[768,2304]{1,0:T(8,128)(2,1)S(1)} %copy-done), custom_call_target="tpu_custom_call" | custom-call | flops 188743680 | bytes 3538944 | tf_op jit(solution)/shard_map/own/pallas_call | solution.py:254
  30.3 0.1 collective-permute-start.5
  30.4 1.2 %collective-permute-done.5.other_ref = bf16[32,768]{1,0:T(8,128)(2,1)S(1)} collective-permute-done((bf16[32,768]{1,0:T(8,128)(2,1)S(1)}, bf16[32,768]{1,0:T(8,128)(2,1)S(1)}, u32[]{:S(2)}, u32[]{:S(2)}) %collective-permute-start.5) | collective-permute-done | bytes 49184 | tf_op jit(solution)/shard_map/ppermute | solution.py:377
  31.6 0.0 collective-permute-done.6.refs_0_
  31.6 1.2 %collective-permute-done.7.refs_1_ = bf16[64,768]{1,0:T(8,128)(2,1)S(1)} collective-permute-done((bf16[64,768]{1,0:T(8,128)(2,1)S(1)}, bf16[64,768]{1,0:T(8,128)(2,1)S(1)}, u32[]{:S(2)}, u32[]{:S(2)}) %collective-permute-start.7) | collective-permute-done | bytes 98336 | tf_op jit(solution)/shard_map/ppermute | solution.py:377
  32.8 0.4 %collective-permute-done.8.refs_2_ = bf16[64,768]{1,0:T(8,128)(2,1)S(1)} collective-permute-done((bf16[64,768]{1,0:T(8,128)(2,1)S(1)}, bf16[64,768]{1,0:T(8,128)(2,1)S(1)}, u32[]{:S(2)}, u32[]{:S(2)}) %collective-permute-start.8) | collective-permute-done | bytes 98336 | tf_op jit(solution)/shard_map/ppermute | solution.py:377
  33.2 1.0 %partial.1 = (f32[32,896]{1,0:T(8,128)S(1)}, f32[32,896]{1,0:T(8,128)S(1)}) custom-call(bf16[32,768]{1,0:T(8,128)(2,1)S(1)} %get-tuple-element.17.own_ref, bf16[32,768]{1,0:T(8,128)(2,1)S(1)} %collective-permute-done.5.other_ref, bf16[64,1536]{1,0:T(8,128)(2,1)S(1)} %get-tuple-element.18.own_key_value_ref, bf16[768,2304]{1,0:T(8,128)(2,1)S(1)} %copy-done, ...), custom_call_target="tpu_custom_call" | custom-call | tf_op jit(solution)/shard_map/partial/pallas_call | solution.py:315
  34.2 0.1 collective-permute-start.9
  34.3 0.0 copy-done.1
  34.3 1.3 %collective-permute-done.9.theirs_ref = f32[32,896]{1,0:T(8,128)S(1)} collective-permute-done((f32[32,896]{1,0:T(8,128)S(1)}, f32[32,896]{1,0:T(8,128)S(1)}, u32[]{:S(2)}, u32[]{:S(2)}) %collective-permute-start.9) | collective-permute-done | bytes 114720 | tf_op jit(solution)/shard_map/ppermute | solution.py:377
  35.6 1.0 %merge.1 = bf16[32,768]{1,0:T(8,128)(2,1)} custom-call(f32[32,896]{1,0:T(8,128)S(1)} %get-tuple-element.19.mine_ref, f32[32,896]{1,0:T(8,128)S(1)} %collective-permute-done.9.theirs_ref, bf16[1,768]{1,0:T(2,128)(2,1)S(1)} %reshape.19.gain_ref), custom_call_target="tpu_custom_call" | custom-call | tf_op jit(solution)/shard_map/merge/pallas_call | solution.py:347
  (2 shorter events, 0.0 us)
Async XLA Ops:
  6.8 22.8 %copy-start = (bf16[768,2304]{1,0:T(8,128)(2,1)S(1)}, bf16[768,2304]{1,0:T(8,128)(2,1)}, u32[]{:S(2)}) copy-start(bf16[768,2304]{1,0:T(8,128)(2,1)} %proj_ref.3) | copy-start | bytes 10616836
  6.8 1.9 %collective-permute-start = (bf16[1600,128]{1,0:T(8,128)(2,1)S(1)}, bf16[1600,128]{1,0:T(8,128)(2,1)S(1)}, u32[]{:S(2)}, u32[]{:S(2)}) collective-permute-start(bf16[1600,128]{1,0:T(8,128)(2,1)S(1)} %get-tuple-element.16), channel_id=1, source_target_pairs={{0,1},{1,0},{2,3},{3,2},{4,5},{5,4},{6,7},{7,6},{8,9},{9,8},{10,11... | collective-permute-start | bytes 1228808 | tf_op jit(solution)/shard_map/ppermute | solution.py:377
  8.8 6.2 %collective-permute-start.1 = (bf16[400,128]{1,0:T(8,128)(2,1)S(1)}, bf16[400,128]{1,0:T(8,128)(2,1)S(1)}, u32[]{:S(2)}, u32[]{:S(2)}) collective-permute-start(bf16[400,128]{1,0:T(8,128)(2,1)S(1)} %get-tuple-element.21), channel_id=1, source_target_pairs={{0,4},{1,5},{2,6},{3,7},{4,0},{5,1},{6,2},{7,3},{8,12},{9,13},{10,... | collective-permute-start | bytes 307208 | tf_op jit(solution)/shard_map/ppermute | solution.py:377
  11.8 5.9 %collective-permute-start.2 = (bf16[400,128]{1,0:T(8,128)(2,1)S(1)}, bf16[400,128]{1,0:T(8,128)(2,1)S(1)}, u32[]{:S(2)}, u32[]{:S(2)}) collective-permute-start(bf16[400,128]{1,0:T(8,128)(2,1)S(1)} %get-tuple-element.23), channel_id=1, source_target_pairs={{0,2},{1,3},{2,0},{3,1},{4,6},{5,7},{6,4},{7,5},{8,10},{9,11},{10,... | collective-permute-start | bytes 307208 | tf_op jit(solution)/shard_map/ppermute | solution.py:377
  13.3 5.6 %collective-permute-start.3 = (bf16[400,128]{1,0:T(8,128)(2,1)S(1)}, bf16[400,128]{1,0:T(8,128)(2,1)S(1)}, u32[]{:S(2)}, u32[]{:S(2)}) collective-permute-start(bf16[400,128]{1,0:T(8,128)(2,1)S(1)} %get-tuple-element.22), channel_id=1, source_target_pairs={{0,6},{1,7},{2,4},{3,5},{4,2},{5,3},{6,0},{7,1},{8,14},{9,15},{10,... | collective-permute-start | bytes 307208 | tf_op jit(solution)/shard_map/ppermute | solution.py:377
  19.0 6.7 %collective-permute-start.4 = (bf16[400,128]{1,0:T(8,128)(2,1)S(1)}, bf16[400,128]{1,0:T(8,128)(2,1)S(1)}, u32[]{:S(2)}, u32[]{:S(2)}) collective-permute-start(bf16[400,128]{1,0:T(8,128)(2,1)S(1)} %add_convert_fusion.1.mine_ref), channel_id=1, source_target_pairs={{0,8},{1,9},{2,10},{3,11},{4,12},{5,13},{6,14},{7,15},{8,0},{9,1},... | collective-permute-start | bytes 307208 | tf_op jit(solution)/shard_map/ppermute | solution.py:377
  26.0 8.3 %copy-start.1 = (bf16[768]{0:T(1024)(128)(2,1)S(1)}, bf16[768]{0:T(1024)(128)(2,1)}, u32[]{:S(2)}) copy-start(bf16[768]{0:T(1024)(128)(2,1)} %param.15) | copy-start | bytes 4612
  26.0 5.6 %collective-permute-start.6 = (bf16[64,768]{1,0:T(8,128)(2,1)S(1)}, bf16[64,768]{1,0:T(8,128)(2,1)S(1)}, u32[]{:S(2)}, u32[]{:S(2)}) collective-permute-start(bf16[64,768]{1,0:T(8,128)(2,1)S(1)} %nodes.1.nodes_ref), channel_id=1, source_target_pairs={{0,2},{1,3},{2,0},{3,1},{4,6},{5,7},{6,4},{7,5},{8,10},{9,11},{10,... | collective-permute-start | bytes 294920 | tf_op jit(solution)/shard_map/ppermute | solution.py:377
  27.2 5.5 %collective-permute-start.7 = (bf16[64,768]{1,0:T(8,128)(2,1)S(1)}, bf16[64,768]{1,0:T(8,128)(2,1)S(1)}, u32[]{:S(2)}, u32[]{:S(2)}) collective-permute-start(bf16[64,768]{1,0:T(8,128)(2,1)S(1)} %nodes.1.nodes_ref), channel_id=1, source_target_pairs={{0,6},{1,7},{2,4},{3,5},{4,2},{5,3},{6,0},{7,1},{8,14},{9,15},{10,... | collective-permute-start | bytes 294920 | tf_op jit(solution)/shard_map/ppermute | solution.py:377
  27.9 5.3 %collective-permute-start.8 = (bf16[64,768]{1,0:T(8,128)(2,1)S(1)}, bf16[64,768]{1,0:T(8,128)(2,1)S(1)}, u32[]{:S(2)}, u32[]{:S(2)}) collective-permute-start(bf16[64,768]{1,0:T(8,128)(2,1)S(1)} %nodes.1.nodes_ref), channel_id=1, source_target_pairs={{0,4},{1,5},{2,6},{3,7},{4,0},{5,1},{6,2},{7,3},{8,12},{9,13},{10,... | collective-permute-start | bytes 294920 | tf_op jit(solution)/shard_map/ppermute | solution.py:377
  30.3 1.3 %collective-permute-start.5 = (bf16[32,768]{1,0:T(8,128)(2,1)S(1)}, bf16[32,768]{1,0:T(8,128)(2,1)S(1)}, u32[]{:S(2)}, u32[]{:S(2)}) collective-permute-start(bf16[32,768]{1,0:T(8,128)(2,1)S(1)} %get-tuple-element.17.own_ref), channel_id=1, source_target_pairs={{0,1},{1,0},{2,3},{3,2},{4,5},{5,4},{6,7},{7,6},{8,9},{9,8},{10,11... | collective-permute-start | bytes 147464 | tf_op jit(solution)/shard_map/ppermute | solution.py:377
  34.2 1.4 %collective-permute-start.9 = (f32[32,896]{1,0:T(8,128)S(1)}, f32[32,896]{1,0:T(8,128)S(1)}, u32[]{:S(2)}, u32[]{:S(2)}) collective-permute-start(f32[32,896]{1,0:T(8,128)S(1)} %get-tuple-element.20), channel_id=1, source_target_pairs={{0,1},{1,0},{2,3},{3,2},{4,5},{5,4},{6,7},{7,6},{8,9},{9,8},{10,11... | collective-permute-start | bytes 344072 | tf_op jit(solution)/shard_map/ppermute | solution.py:377
